TPU v7x, 32 devices: a whole 2x2x4 slice. The times are simulated.
32 devices in a mesh: dp: 8 (over z, y), tensor: 4 (over x, core).
Axes of the slice: x: 2, y: 2, z: 4, core: 2. Of those that a mesh axis runs over, the one named last changes fastest.
Arguments:
- tokens: bfloat16 [4096, 8192], P('dp', 'tensor'), may hold values from -55 to 55, as said below
- cotangent: bfloat16 [4096, 8192], P('dp', 'tensor'), may hold values from -1.1 to 1.1, as said below
- lowrank_down_factor: float32 [64, 8192], P(None, 'tensor'), may hold values from -0.22097087 to 0.22097087, as said below
- lowrank_up_factor: float32 [64, 8192], P(None, 'tensor'), may hold values from -0.22097087 to 0.22097087, as said below
- first_moment_estimate: float32 [2, 64, 8192], P(None, 'dp', 'tensor'), may hold values from -3 to 3
- second_moment_estimate: float32 [2, 64, 8192], P(None, 'dp', 'tensor'), may hold values from 0.02 to 0.5, as said below
Outputs:
- input_grad: bfloat16 [4096, 8192], P('dp', 'tensor')
- updated_down_factor: float32 [64, 8192], P('dp', 'tensor')
- updated_up_factor: float32 [64, 8192], P('dp', 'tensor')
- new_first: float32 [2, 64, 8192], P(None, 'dp', 'tensor')
- new_second: float32 [2, 64, 8192], P(None, 'dp', 'tensor')
Inputs may be any that keep to these rules, and one draw needn't show every extreme that they name: `tokens`: bounded activations. `cotangent`: bounded gradients. `lowrank_down_factor`: bounded factor entries. `lowrank_up_factor`: bounded factor entries. `second_moment_estimate`: positive moments.
All inputs are finite; a program needn't handle non-finite values.
Results may differ from a plain program's by a relative error of at most 0.0063.
Values sent between devices are 32-bit elements; how exact they have to be, the bound alone decides.
No kernel may reach another device: no remote copies, remote signals or barrier semaphores. Data moves between devices by JAX's collectives and lax.ppermute only.
A program may use at most 64 MiB of HBM per device.

v0:
```python
import jax
import jax.numpy as jnp
from jax import lax
from jax.sharding import PartitionSpec as P

SCALE = 2.0
NORM_EPS = 1e-06


def swapped(block, axis, apart):
    count = lax.axis_size(axis)
    route = []
    for low in range(count):
        high = low | 1 << apart
        if high != low and high < count:
            route += [(low, high), (high, low)]
    return lax.ppermute(block, axis, route)


def inner_stats(left_vec, right_vec):
    return jnp.stack(
        [
            jnp.sum(left_vec * left_vec, 1),
            jnp.sum(right_vec * right_vec, 1),
            jnp.sum(left_vec * right_vec, 1),
        ]
    )


def adasum_mix(left_vec, right_vec, totals):
    coef_left = 1.0 - totals[2] / (2.0 * (totals[0] + NORM_EPS))
    coef_right = 1.0 - totals[2] / (2.0 * (totals[1] + NORM_EPS))
    return coef_left[:, None] * left_vec + coef_right[:, None] * right_vec


def body(
    tokens,
    cotangent,
    lowrank_down_factor,
    lowrank_up_factor,
    first_moment_estimate,
    second_moment_estimate,
):
    adapter_input_width = lowrank_down_factor.astype(jnp.bfloat16)
    adapter_output_width = lowrank_up_factor.astype(jnp.bfloat16)
    adapter_rank_count = lowrank_down_factor.shape[0]
    column_count = lowrank_down_factor.shape[1]
    contract_last = (((1,), (1,)), ((), ()))
    partial_sums = jnp.concatenate(
        [
            lax.dot_general(
                tokens, adapter_input_width, contract_last, preferred_element_type=jnp.float32
            ),
            lax.dot_general(
                cotangent, adapter_output_width, contract_last, preferred_element_type=jnp.float32
            ),
        ],
        1,
    )
    summed = lax.psum(partial_sums, "tensor")
    scaled_sums = SCALE * summed
    scaled_hidden = scaled_sums[:, :adapter_rank_count].astype(jnp.bfloat16)
    scaled_upstream = scaled_sums[:, adapter_rank_count:].astype(jnp.bfloat16)
    input_grad = jnp.dot(
        scaled_upstream, adapter_input_width, preferred_element_type=jnp.float32
    ).astype(jnp.bfloat16)
    contract_first = (((0,), (0,)), ((), ()))
    grad_a = lax.dot_general(
        scaled_upstream, tokens, contract_first, preferred_element_type=jnp.float32
    )
    grad_b = lax.dot_general(
        scaled_hidden, cotangent, contract_first, preferred_element_type=jnp.float32
    )
    vector = jnp.stack([grad_a, grad_b]).reshape(2, adapter_rank_count * column_count)
    levels = lax.axis_size("dp").bit_length() - 1
    position = lax.axis_index("dp")
    for level_index in range(levels):
        partner_vec = swapped(vector, "dp", level_index)
        upper_side = position >> level_index & 1 == 1
        left_vec = jnp.where(upper_side, partner_vec, vector)
        right_vec = jnp.where(upper_side, vector, partner_vec)
        totals = lax.psum(inner_stats(left_vec, right_vec), "tensor")
        vector = adasum_mix(left_vec, right_vec, totals)
    combined = vector
    combined = combined.reshape(2, adapter_rank_count, column_count)
    owned_rows = first_moment_estimate.shape[1]
    row_start = position * owned_rows
    owned_grad = lax.dynamic_slice_in_dim(combined, row_start, owned_rows, 1)
    owned_down = lax.dynamic_slice_in_dim(lowrank_down_factor, row_start, owned_rows, 0)
    owned_up = lax.dynamic_slice_in_dim(lowrank_up_factor, row_start, owned_rows, 0)
    moment_one = 0.9 * first_moment_estimate + 0.1 * owned_grad
    moment_two = 0.95 * second_moment_estimate + 0.05 * owned_grad * owned_grad
    optimizer_update = 0.001 * moment_one / (jnp.sqrt(moment_two) + 1e-08)
    updated_down_factor = owned_down - optimizer_update[0]
    updated_up_factor = owned_up - optimizer_update[1]
    return (input_grad, updated_down_factor, updated_up_factor, moment_one, moment_two)


def solution(mesh):
    placed = (
        P("dp", "tensor"),
        P("dp", "tensor"),
        P(None, "tensor"),
        P(None, "tensor"),
        P(None, "dp", "tensor"),
        P(None, "dp", "tensor"),
    )
    return jax.shard_map(
        body,
        mesh=mesh,
        in_specs=placed,
        out_specs=(
            P("dp", "tensor"),
            P("dp", "tensor"),
            P("dp", "tensor"),
            P(None, "dp", "tensor"),
            P(None, "dp", "tensor"),
        ),
        check_vma=False,
    )
```

profile of v0, /device:TPU:0, one launch (start us, length us, event | category | flops | bytes accessed | tf_op | source)
XLA Modules:
  0.0 196.7 jit_solution(7578187759023210300)
XLA Ops:
  7.2 0.0 copy-start
  7.2 0.0 copy-start.3
  7.2 0.0 all-reduce.2.cloned.1.call-start
  7.2 2.6 %fusion = f32[512,64]{0,1:T(8,128)S(1)} fusion(bf16[512,2048]{1,0:T(8,128)(2,1)} %param.7, f32[64,2048]{1,0:T(8,128)} %param.9), kind=kOutput, calls=%fused_computation.25 | convolution fusion | flops 134348800 | bytes 2752512 | tf_op jit(solution)/shard_map/dot_general | solution.py:54
  9.8 0.0 copy-done
  9.8 0.0 copy-done.3
  9.8 0.8 fusion.4
  10.6 0.7 pad_maximum_fusion.1
  11.3 0.0 all-reduce.2.cloned.1.call-update
  11.3 34.8 %all-reduce.2.cloned.1.call-done = f32[512,128]{0,1:T(8,128)} async-done(((f32[512,128]{0,1:T(8,128)}), f32[512,128]{0,1:T(8,128)}) %all-reduce.2.cloned.1.call-update) | async-done | bytes 262160 | tf_op jit(solution)/shard_map/psum | solution.py:60
  46.2 0.0 copy-start.1
  46.2 1.1 multiply_convert_fusion
  47.3 0.5 convolution_bitcast_fusion.1
  47.8 0.1 copy-done.1
  47.8 0.5 convolution_bitcast_fusion
  48.3 0.5 copy.11
  48.9 0.5 copy.12
  49.4 1.9 pad_maximum_fusion
  51.3 1.5 collective-permute-start
  52.8 22.3 %collective-permute-done = f32[2,131072]{1,0:T(2,128)} collective-permute-done((f32[2,131072]{1,0:T(2,128)}, f32[2,131072]{1,0:T(2,128)}, u32[]{:S(2)}, u32[]{:S(2)}) %collective-permute-start) | collective-permute-done | bytes 1048608 | tf_op jit(solution)/shard_map/ppermute | solution.py:17
  75.2 4.4 %multiply_reduce_fusion.8 = (f32[2]{0:T(128)S(1)}, f32[2]{0:T(128)S(1)}, f32[2]{0:T(128)S(1)}, f32[2,131072]{1,0:T(2,128)}, f32[2,131072]{1,0:T(2,128)}) fusion(f32[2,131072]{1,0:T(2,128)} %collective-permute-done, f32[1,131072]{1,0:T(1,128)S(1)} %bitcast.48, f32[1,131072]{1,0:T(1,128)S(1)} %bitcast.46, pred[]{:T(512)S(6)} %eq.11), kind=kLoop, calls=%fused_computation.16 | loop fusion | flops 2359290 | bytes 4194329 | tf_op jit(solution)/shard_map/reduce_sum | solution.py:23
  79.5 5.7 %psum.29 = f32[3,2]{1,0:T(4,128)S(1)} all-reduce(f32[3,2]{1,0:T(4,128)S(1)} %pad_maximum_fusion.2), channel_id=1, replica_groups=mesh['dp'=8,'tensor'=4] {'tensor'}, use_global_device_ids=true, to_apply=%region_4.5 | all-reduce | flops 6 | bytes 48 | tf_op jit(solution)/shard_map/psum | solution.py:82
  85.2 2.1 %multiply_add_fusion.2 = f32[2,131072]{1,0:T(2,128)S(1)} fusion(f32[2,131072]{1,0:T(2,128)} %get-tuple-element.22, f32[2,131072]{1,0:T(2,128)} %get-tuple-element.21, f32[2]{0:T(128)S(1)} %get-tuple-element.30, f32[2]{0:T(128)S(1)} %get-tuple-element.29), kind=kLoop, calls=%fused_computation.13 | loop fusion | flops 786432 | bytes 3145744 | tf_op jit(solution)/shard_map/add | solution.py:33
  87.4 1.8 collective-permute-start.1
  89.2 23.3 %collective-permute-done.1 = f32[2,131072]{1,0:T(2,128)} collective-permute-done((f32[2,131072]{1,0:T(2,128)S(1)}, f32[2,131072]{1,0:T(2,128)}, u32[]{:S(2)}, u32[]{:S(2)}) %collective-permute-start.1) | collective-permute-done | bytes 1048608 | tf_op jit(solution)/shard_map/ppermute | solution.py:17
  112.5 4.2 %multiply_reduce_fusion.5 = (f32[2]{0:T(128)S(1)}, f32[2]{0:T(128)S(1)}, f32[2]{0:T(128)S(1)}, f32[2,131072]{1,0:T(2,128)}, f32[2,131072]{1,0:T(2,128)}) fusion(f32[2,131072]{1,0:T(2,128)} %collective-permute-done.1, f32[2,131072]{1,0:T(2,128)S(1)} %multiply_add_fusion.2, pred[]{:T(512)S(6)} %eq.10), kind=kLoop, calls=%fused_computation.12 | loop fusion | flops 2097146 | bytes 4194329 | tf_op jit(solution)/shard_map/reduce_sum | solution.py:23
  116.7 5.7 %psum.30 = f32[3,2]{1,0:T(4,128)S(1)} all-reduce(f32[3,2]{1,0:T(4,128)S(1)} %pad_maximum_fusion.3), channel_id=1, replica_groups=mesh['dp'=8,'tensor'=4] {'tensor'}, use_global_device_ids=true, to_apply=%region_8.9 | all-reduce | flops 6 | bytes 48 | tf_op jit(solution)/shard_map/psum | solution.py:82
  122.4 2.1 %multiply_add_fusion.1 = f32[2,131072]{1,0:T(2,128)S(1)} fusion(f32[2,131072]{1,0:T(2,128)} %get-tuple-element.20, f32[2,131072]{1,0:T(2,128)} %get-tuple-element.19, f32[2]{0:T(128)S(1)} %get-tuple-element.28, f32[2]{0:T(128)S(1)} %get-tuple-element.27), kind=kLoop, calls=%fused_computation.9 | loop fusion | flops 786432 | bytes 3145744 | tf_op jit(solution)/shard_map/add | solution.py:33
  124.5 2.7 %collective-permute-start.2 = (f32[2,131072]{1,0:T(2,128)S(1)}, f32[2,131072]{1,0:T(2,128)}, u32[]{:S(2)}, u32[]{:S(2)}) collective-permute-start(f32[2,131072]{1,0:T(2,128)S(1)} %multiply_add_fusion.1), channel_id=1, source_target_pairs={{0,16},{16,0},{4,20},{20,4},{8,24},{24,8},{12,28},{28,12},{1,17},{... | collective-permute-start | bytes 3145736 | tf_op jit(solution)/shard_map/ppermute | solution.py:17
  127.3 0.0 copy-start.4
  127.3 45.8 %collective-permute-done.2 = f32[2,131072]{1,0:T(2,128)} collective-permute-done((f32[2,131072]{1,0:T(2,128)S(1)}, f32[2,131072]{1,0:T(2,128)}, u32[]{:S(2)}, u32[]{:S(2)}) %collective-permute-start.2) | collective-permute-done | bytes 1048608 | tf_op jit(solution)/shard_map/ppermute | solution.py:17
  173.0 4.2 %multiply_reduce_fusion.2 = (f32[2]{0:T(128)S(1)}, f32[2]{0:T(128)S(1)}, f32[2]{0:T(128)S(1)}, f32[2,131072]{1,0:T(2,128)}, f32[2,131072]{1,0:T(2,128)}) fusion(f32[2,131072]{1,0:T(2,128)} %collective-permute-done.2, f32[2,131072]{1,0:T(2,128)S(1)} %multiply_add_fusion.1, pred[]{:T(512)S(6)} %eq.9), kind=kLoop, calls=%fused_computation.8 | loop fusion | flops 2097146 | bytes 4194329 | tf_op jit(solution)/shard_map/reduce_sum | solution.py:23
  177.2 0.0 copy-start.2
  177.3 0.0 copy-done.4
  177.3 2.0 %convolution_convert_fusion = bf16[512,2048]{1,0:T(8,128)(2,1)} fusion(f32[64,2048]{1,0:T(8,128)S(1)} %copy-done.4, bf16[512,128]{0,1:T(8,128)(2,1)S(1)} %multiply_convert_fusion), kind=kOutput, calls=%fused_computation | convolution fusion | flops 135397376 | bytes 2686976 | tf_op jit(solution)/shard_map/dot_general | solution.py:64
  179.3 5.6 %psum.31 = f32[3,2]{1,0:T(4,128)S(1)} all-reduce(f32[3,2]{1,0:T(4,128)S(1)} %pad_maximum_fusion.4), channel_id=1, replica_groups=mesh['dp'=8,'tensor'=4] {'tensor'}, use_global_device_ids=true, to_apply=%region_12.13 | all-reduce | flops 6 | bytes 48 | tf_op jit(solution)/shard_map/psum | solution.py:82
  185.0 0.0 copy-done.2
  185.0 0.0 copy-start.5
  185.0 0.0 copy-start.6
  185.0 1.9 multiply_add_fusion
  186.9 0.6 copy.15
  187.5 0.0 copy-done.5
  187.5 0.0 copy-done.6
  187.5 0.8 add_divide_fusion
  188.3 1.5 fusion.6
  (6 shorter events, 0.1 us)
Async XLA Ops:
  7.2 2.7 %copy-start = (bf16[512,2048]{1,0:T(8,128)(2,1)S(1)}, bf16[512,2048]{1,0:T(8,128)(2,1)}, u32[]{:S(2)}) copy-start(bf16[512,2048]{1,0:T(8,128)(2,1)} %param.6) | copy-start | bytes 6291460
  7.2 2.7 %copy-start.3 = (f32[64,2048]{1,0:T(8,128)S(1)}, f32[64,2048]{1,0:T(8,128)}, u32[]{:S(2)}) copy-start(f32[64,2048]{1,0:T(8,128)} %param.8) | copy-start | bytes 1572868
  7.2 39.0 %all-reduce.2.cloned.1.call-start = ((), (), s32[]{:S(2)}) async-start(), calls=%async_computation | async-start | bytes 524288 | tf_op jit(solution)/shard_map/psum | solution.py:60
  46.2 1.7 copy-start.1
  51.3 23.8 %collective-permute-start = (f32[2,131072]{1,0:T(2,128)}, f32[2,131072]{1,0:T(2,128)}, u32[]{:S(2)}, u32[]{:S(2)}) collective-permute-start(f32[2,131072]{1,0:T(2,128)} %pad_maximum_fusion), channel_id=1, source_target_pairs={{0,4},{4,0},{8,12},{12,8},{16,20},{20,16},{24,28},{28,24},{1,5},{5... | collective-permute-start | bytes 3145736 | tf_op jit(solution)/shard_map/ppermute | solution.py:17
  87.4 25.1 %collective-permute-start.1 = (f32[2,131072]{1,0:T(2,128)S(1)}, f32[2,131072]{1,0:T(2,128)}, u32[]{:S(2)}, u32[]{:S(2)}) collective-permute-start(f32[2,131072]{1,0:T(2,128)S(1)} %multiply_add_fusion.2), channel_id=1, source_target_pairs={{0,8},{8,0},{4,12},{12,4},{16,24},{24,16},{20,28},{28,20},{1,9},{9... | collective-permute-start | bytes 3145736 | tf_op jit(solution)/shard_map/ppermute | solution.py:17
  124.5 48.5 %collective-permute-start.2 = (f32[2,131072]{1,0:T(2,128)S(1)}, f32[2,131072]{1,0:T(2,128)}, u32[]{:S(2)}, u32[]{:S(2)}) collective-permute-start(f32[2,131072]{1,0:T(2,128)S(1)} %multiply_add_fusion.1), channel_id=1, source_target_pairs={{0,16},{16,0},{4,20},{20,4},{8,24},{24,8},{12,28},{28,12},{1,17},{... | collective-permute-start | bytes 3145736 | tf_op jit(solution)/shard_map/ppermute | solution.py:17
  127.3 50.0 %copy-start.4 = (f32[64,2048]{1,0:T(8,128)S(1)}, f32[64,2048]{1,0:T(8,128)}, u32[]{:S(2)}) copy-start(f32[64,2048]{1,0:T(8,128)} %param.8) | copy-start | bytes 1572868
  177.2 7.7 %copy-start.2 = (f32[2,131072]{1,0:T(2,128)S(1)}, f32[2,131072]{1,0:T(2,128)}, u32[]{:S(2)}) copy-start(f32[2,131072]{1,0:T(2,128)} %get-tuple-element.17) | copy-start | bytes 3145732
  185.0 2.5 %copy-start.5 = (f32[2,8,2048]{2,1,0:T(8,128)S(1)}, f32[2,8,2048]{2,1,0:T(8,128)}, u32[]{:S(2)}) copy-start(f32[2,8,2048]{2,1,0:T(8,128)} %param.10) | copy-start | bytes 393220
  185.0 2.5 %copy-start.6 = (f32[2,8,2048]{2,1,0:T(8,128)S(1)}, f32[2,8,2048]{2,1,0:T(8,128)}, u32[]{:S(2)}) copy-start(f32[2,8,2048]{2,1,0:T(8,128)} %param.11) | copy-start | bytes 393220
Sparse Core Ops, SparseCore 0:
  11.5 34.6 all-reduce.1
where the time goes:
time: 197 us
  waiting for transfers between devices  126 us (64%)
  other arithmetic  25.1 us (13%)
  blocking collectives  17 us (9%)
  between operations  14.2 us (7%)
  matrix products  6.35 us (3%)
  starting transfers between devices  6.06 us (3%)
    ppermute x3, waiting for transfers between devices, swapped(): return lax.ppermute(block, axis, route)  91.4 us
    psum x1, waiting for transfers between devices, body(): summed = lax.psum(partial_sums, 'tensor')  34.8 us
    psum x3, blocking collectives, body(): totals = lax.psum(inner_stats(left_vec, right_vec), 'tensor')  17 us
    reduce_sum x3, other arithmetic, inner_stats(): jnp.sum(left_vec * left_vec, 1)  12.8 us
    add x3, other arithmetic, adasum_mix(): return coef_left[:, None] * left_vec + coef_right[:, None] * right_vec  6.17 us
    ppermute x3, starting transfers between devices, swapped(): return lax.ppermute(block, axis, route)  6.02 us
  transfers between devices with their start and end apart: 4, of which 4 were waited for; matrix products, arithmetic and copies ran while one was open for 0% of the time, Pallas kernels for 0%

commit v1 on v0

v1 whole, which is shorter than its diff:
```python
import jax
import jax.numpy as jnp
from jax import lax
from jax.sharding import PartitionSpec as P

SCALE = 2.0
NORM_EPS = 1e-06


def butterfly_sum(block, axis):
    count = lax.axis_size(axis)
    apart = 1
    while apart < count:
        route = [(here, here ^ apart) for here in range(count)]
        block = block + lax.ppermute(block, axis, route)
        apart *= 2
    return block


def tree_weights(gram, levels):
    count = gram.shape[-1]
    index = jnp.arange(count)
    weights = jnp.ones(gram.shape[:-1], jnp.float32)
    for level in range(levels):
        group = index >> level
        same = (group[:, None] == group[None, :]).astype(jnp.float32)
        sibling = (group[:, None] == (group[None, :] ^ 1)).astype(jnp.float32)
        weighted = gram * weights[:, :, None] * weights[:, None, :]
        norm = jnp.sum(same * jnp.sum(same * weighted, -1)[:, None, :], -1)
        cross = jnp.sum(same * jnp.sum(sibling * weighted, -1)[:, None, :], -1)
        weights = weights * (1.0 - cross / (2.0 * (norm + NORM_EPS)))
    return weights


def body(
    tokens,
    cotangent,
    lowrank_down_factor,
    lowrank_up_factor,
    first_moment_estimate,
    second_moment_estimate,
):
    replicas = lax.axis_size("dp")
    everyone = replicas * lax.axis_size("tensor")
    levels = replicas.bit_length() - 1
    position = lax.axis_index("dp")
    rank, columns = lowrank_down_factor.shape
    owned_rows = first_moment_estimate.shape[1]
    adapter_in = lowrank_down_factor.astype(jnp.bfloat16)
    adapter_out = lowrank_up_factor.astype(jnp.bfloat16)
    contract_last = (((1,), (1,)), ((), ()))
    partial_sums = jnp.concatenate(
        [
            lax.dot_general(
                tokens, adapter_in, contract_last, preferred_element_type=jnp.float32
            ),
            lax.dot_general(
                cotangent, adapter_out, contract_last, preferred_element_type=jnp.float32
            ),
        ],
        1,
    )
    summed = SCALE * butterfly_sum(partial_sums, "tensor")
    hidden = summed[:, :rank].astype(jnp.bfloat16)
    upstream = summed[:, rank:].astype(jnp.bfloat16)
    input_grad = jnp.dot(upstream, adapter_in, preferred_element_type=jnp.float32)
    input_grad = input_grad.astype(jnp.bfloat16)
    contract_first = (((0,), (0,)), ((), ()))
    grad_a = lax.dot_general(
        upstream, tokens, contract_first, preferred_element_type=jnp.float32
    )
    grad_b = lax.dot_general(
        hidden, cotangent, contract_first, preferred_element_type=jnp.float32
    )
    outgoing = jnp.stack(
        [
            grad_a.reshape(replicas, owned_rows, columns),
            grad_b.reshape(replicas, owned_rows, columns),
        ],
        1,
    )
    pieces = lax.all_to_all(outgoing, "dp", 0, 0, tiled=True)
    gram = jnp.stack(
        [
            jnp.sum(pieces * pieces[other][None], (2, 3))
            for other in range(replicas)
        ],
        2,
    )
    gram = gram.transpose(1, 0, 2).reshape(1, -1)
    spread = jnp.broadcast_to(gram, (everyone, gram.shape[1]))
    gathered = lax.all_to_all(spread, ("dp", "tensor"), 0, 0, tiled=True)
    gram = jnp.sum(gathered, 0).reshape(2, replicas, replicas)
    weights = tree_weights(gram, levels)
    owned_grad = jnp.sum(pieces * weights.T[:, :, None, None], 0)
    row_start = position * owned_rows
    owned_down = lax.dynamic_slice_in_dim(lowrank_down_factor, row_start, owned_rows, 0)
    owned_up = lax.dynamic_slice_in_dim(lowrank_up_factor, row_start, owned_rows, 0)
    moment_one = 0.9 * first_moment_estimate + 0.1 * owned_grad
    moment_two = 0.95 * second_moment_estimate + 0.05 * owned_grad * owned_grad
    optimizer_update = 0.001 * moment_one / (jnp.sqrt(moment_two) + 1e-08)
    updated_down_factor = owned_down - optimizer_update[0]
    updated_up_factor = owned_up - optimizer_update[1]
    return (input_grad, updated_down_factor, updated_up_factor, moment_one, moment_two)


def solution(mesh):
    placed = (
        P("dp", "tensor"),
        P("dp", "tensor"),
        P(None, "tensor"),
        P(None, "tensor"),
        P(None, "dp", "tensor"),
        P(None, "dp", "tensor"),
    )
    return jax.shard_map(
        body,
        mesh=mesh,
        in_specs=placed,
        out_specs=(
            P("dp", "tensor"),
            P("dp", "tensor"),
            P("dp", "tensor"),
            P(None, "dp", "tensor"),
            P(None, "dp", "tensor"),
        ),
        check_vma=False,
    )
```

time: 197 us -> 82.7 us (0.42)
  waiting for transfers between devices: 126 us -> 35.2 us
  blocking collectives: 17 us -> 0 us
  between operations: 14.2 us -> 0.77 us
  other arithmetic: 25.1 us -> 11.8 us
  local copies, waits for them, and re-layouts: 1.79 us -> 14.8 us
  starting transfers between devices: 6.06 us -> 12.9 us
    ppermute x3 -> x2, waiting for transfers between devices: 91.4 us -> 7.77 us  [butterfly_sum(): block = block + lax.ppermute(block, axis, route)]
    psum x1 -> x0, waiting for transfers between devices: 34.8 us -> none  [body(): summed = lax.psum(partial_sums, 'tensor')]
    all_to_all x0 -> x2, waiting for transfers between devices: none -> 27.4 us  [the longest x1 23.4 us: body(): pieces = lax.all_to_all(outgoing, 'dp', 0, 0, tiled=True)]
    psum x3 -> x0, blocking collectives: 17 us -> none  [body(): totals = lax.psum(inner_stats(left_vec, right_vec), 'tensor')]
    all_to_all x0 -> x2, starting transfers between devices: none -> 9.47 us  [the longest x1 6.09 us: body(): pieces = lax.all_to_all(outgoing, 'dp', 0, 0, tiled=True)]
    reduce_sum x0 -> x8, local copies, waits for them, and re-layouts: none -> 7.37 us  [body(): jnp.sum(pieces * pieces[other][None], (2, 3))]
    reduce_sum x3 -> x9, other arithmetic: 12.8 us -> 6.25 us  [the longest x6 4.76 us: tree_weights(): norm = jnp.sum(same * jnp.sum(same * weighted, -1)[:, None, :], -1)]
    add x3 -> x1, other arithmetic: 6.17 us -> 0.04 us  [butterfly_sum(): block = block + lax.ppermute(block, axis, route)]
  transfers between devices with their start and end apart: 4 -> 4, of which waited for: 4 -> 4; matrix products, arithmetic and copies ran while one was open for 0% -> 6% of each run, Pallas kernels for 0% -> 0%
where the time goes in v1:
time: 82.7 us; the launch traced here: 82 us
  waiting for transfers between devices  35.2 us (43%)
  local copies, waits for them, and re-layouts  14.8 us (18%)
  starting transfers between devices  12.9 us (16%)
  other arithmetic  11.8 us (14%)
  matrix products  6.61 us (8%)
    all_to_all x1, waiting for transfers between devices, body(): pieces = lax.all_to_all(outgoing, 'dp', 0, 0, tiled=True)  23.4 us
    ppermute x2, waiting for transfers between devices, butterfly_sum(): block = block + lax.ppermute(block, axis, route)  7.77 us
    reduce_sum x8, local copies, waits for them, and re-layouts, body(): jnp.sum(pieces * pieces[other][None], (2, 3))  7.37 us
    all_to_all x1, starting transfers between devices, body(): pieces = lax.all_to_all(outgoing, 'dp', 0, 0, tiled=True)  6.09 us
    unnamed x17, local copies, waits for them, and re-layouts  5.68 us
    reduce_sum x6, other arithmetic, tree_weights(): norm = jnp.sum(same * jnp.sum(same * weighted, -1)[:, None, :], -1)  4.76 us
    all_to_all x1, waiting for transfers between devices, body(): gathered = lax.all_to_all(spread, ('dp', 'tensor'), 0, 0, tiled=True)  3.98 us
    ppermute x2, starting transfers between devices, butterfly_sum(): block = block + lax.ppermute(block, axis, route)  3.44 us
  transfers between devices with their start and end apart: 4, of which 4 were waited for; matrix products, arithmetic and copies ran while one was open for 6% of the time, Pallas kernels for 0%

profile of v1, /device:TPU:0, one launch (start us, length us, event | category | flops | bytes accessed | tf_op | source)
XLA Modules:
  0.0 82.0 jit_solution(13911915465024084218)
XLA Ops:
  0.7 1.6 %copy-done = bf16[512,2048]{1,0:T(8,128)(2,1)S(1)} copy-done((bf16[512,2048]{1,0:T(8,128)(2,1)S(1)}, bf16[512,2048]{1,0:T(8,128)(2,1)}, u32[]{:S(2)}) %copy-start) | copy-done | bytes 2097176
  2.2 1.8 %fusion.4 = f32[512,64]{0,1:T(8,128)S(1)} fusion(bf16[512,2048]{1,0:T(8,128)(2,1)S(1)} %copy-done, f32[64,2048]{1,0:T(8,128)} %param.8), kind=kOutput, calls=%fused_computation.30 | convolution fusion | flops 134348800 | bytes 2752512 | tf_op jit(solution)/shard_map/dot_general | solution.py:54
  4.0 0.8 fusion
  4.8 0.5 collective-permute-start
  5.3 1.2 %collective-permute-done = f32[512,128]{0,1:T(8,128)S(1)} collective-permute-done((f32[512,128]{0,1:T(8,128)S(1)}, f32[512,128]{0,1:T(8,128)S(1)}, u32[]{:S(2)}, u32[]{:S(2)}) %collective-permute-start) | collective-permute-done | bytes 262176 | tf_op jit(solution)/shard_map/ppermute | solution.py:15
  6.5 2.9 %collective-permute-start.1 = (f32[512,128]{0,1:T(8,128)S(1)}, f32[512,128]{0,1:T(8,128)S(1)}, u32[]{:S(2)}, u32[]{:S(2)}) collective-permute-start(f32[512,128]{0,1:T(8,128)S(1)} %fusion.12), channel_id=1, source_target_pairs={{0,2},{1,3},{2,0},{3,1},{4,6},{5,7},{6,4},{7,5},{8,10},{9,11},{10,... | collective-permute-start | bytes 786440 | tf_op jit(solution)/shard_map/ppermute | solution.py:15
  9.5 6.6 %collective-permute-done.1 = f32[512,128]{0,1:T(8,128)S(1)} collective-permute-done((f32[512,128]{0,1:T(8,128)S(1)}, f32[512,128]{0,1:T(8,128)S(1)}, u32[]{:S(2)}, u32[]{:S(2)}) %collective-permute-start.1) | collective-permute-done | bytes 262176 | tf_op jit(solution)/shard_map/ppermute | solution.py:15
  16.1 0.5 convolution_bitcast_fusion.1
  16.6 0.5 convolution_bitcast_fusion
  17.1 1.1 %pad_maximum_fusion = f32[8,2,8,2048]{3,2,1,0:T(8,128)} fusion(f32[8,1,8,2048]{3,2,1,0:T(8,128)S(1)} %convolution_bitcast_fusion, f32[8,1,8,2048]{3,2,1,0:T(8,128)S(1)} %convolution_bitcast_fusion.1), kind=kLoop, calls=%fused_computation.3 | loop fusion | flops 262144 | bytes 2097152 | tf_op jit(solution)/shard_map/stack | solution.py:75
  18.2 6.1 %all-to-all-start = ((f32[8,2,8,2048]{3,2,1,0:T(8,128)}), f32[8,2,8,2048]{3,2,1,0:T(8,128)S(1)}, u32[]{:S(2)}, u32[]{:S(2)}) async-start(f32[8,2,8,2048]{3,2,1,0:T(8,128)} %pad_maximum_fusion), calls=%async_computation | async-start | bytes 2097152 | tf_op jit(solution)/shard_map/all_to_all | solution.py:82
  24.3 0.7 compare_convert_fusion
  24.9 0.7 compare_convert_fusion.2
  25.6 0.7 compare_convert_fusion.4
  26.3 23.4 %all-to-all-done = f32[8,2,8,2048]{3,2,1,0:T(8,128)S(1)} async-done(((f32[8,2,8,2048]{3,2,1,0:T(8,128)}), f32[8,2,8,2048]{3,2,1,0:T(8,128)S(1)}, u32[]{:S(2)}, u32[]{:S(2)}) %all-to-all-start) | async-done | bytes 1048608 | tf_op jit(solution)/shard_map/all_to_all | solution.py:82
  49.7 0.1 slice_bitcast_fusion.7
  49.8 1.3 %multiply_reduce_fusion.1 = (f32[8,2]{1,0:T(8,128)}, f32[8,2]{1,0:T(8,128)}, f32[8,2]{1,0:T(8,128)}, f32[8,2]{1,0:T(8,128)}, f32[8,2]{1,0:T(8,128)S(1)}, /*index...) fusion(f32[8,2,8,2048]{3,2,1,0:T(8,128)S(1)} %all-to-all-done, f32[2,8,2048]{2,1,0:T(8,128)S(1)} %get-tuple-element.29, ...), kind=kLoop, calls=%fused_computation.5 | loop fusion | flops 4194176 | bytes 2097664 | tf_op jit(solution)/shard_map/reduce_sum | solution.py:85
  51.1 1.4 %copy.49 = f32[8,2]{0,1:T(2,128)} copy(f32[8,2]{1,0:T(8,128)} %get-tuple-element.5) | data formatting | bytes 128 | tf_op jit(solution)/shard_map/reduce_sum | solution.py:85
  52.5 1.4 %copy.48 = f32[8,2]{0,1:T(2,128)} copy(f32[8,2]{1,0:T(8,128)} %get-tuple-element.6) | data formatting | bytes 128 | tf_op jit(solution)/shard_map/reduce_sum | solution.py:85
  53.9 1.3 %copy.47 = f32[8,2]{0,1:T(2,128)} copy(f32[8,2]{1,0:T(8,128)} %get-tuple-element.7) | data formatting | bytes 128 | tf_op jit(solution)/shard_map/reduce_sum | solution.py:85
  55.2 1.3 %copy.46 = f32[8,2]{0,1:T(2,128)} copy(f32[8,2]{1,0:T(8,128)} %get-tuple-element.8) | data formatting | bytes 128 | tf_op jit(solution)/shard_map/reduce_sum | solution.py:85
  56.5 0.6 copy.45
  57.1 0.6 copy.44
  57.8 0.6 copy.43
  58.4 0.1 copy.42
  58.5 0.7 constant_dynamic-update-slice_fusion.6
  59.2 0.7 constant_dynamic-update-slice_fusion.5
  59.9 0.7 constant_dynamic-update-slice_fusion.4
  60.6 0.7 constant_dynamic-update-slice_fusion.3
  61.2 0.7 constant_dynamic-update-slice_fusion.2
  61.9 0.7 constant_dynamic-update-slice_fusion.1
  62.6 0.7 constant_dynamic-update-slice_fusion
  63.4 0.1 broadcast_in_dim.4
  63.4 0.6 broadcast_in_dim.5
  64.1 3.4 %all-to-all-start.1 = ((f32[32,1,128]{2,1,0:T(1,128)}), f32[32,1,128]{2,1,0:T(1,128)S(1)}, u32[]{:S(2)}, u32[]{:S(2)}) async-start(f32[32,1,128]{2,1,0:T(1,128)} %broadcast_in_dim.5), calls=%async_computation.1 | async-start | bytes 32768 | tf_op jit(solution)/shard_map/all_to_all | solution.py:92
  67.5 3.1 %convolution_convert_fusion = bf16[512,2048]{1,0:T(8,128)(2,1)} fusion(f32[64,2048]{1,0:T(8,128)} %param.8, bf16[512,128]{0,1:T(8,128)(2,1)S(1)} %multiply_convert_fusion), kind=kOutput, calls=%fused_computation | convolution fusion | flops 135397376 | bytes 2686976 | tf_op jit(solution)/shard_map/dot_general | solution.py:66
  70.6 4.0 %all-to-all-done.1 = f32[32,1,128]{2,1,0:T(1,128)S(1)} async-done(((f32[32,1,128]{2,1,0:T(1,128)}), f32[32,1,128]{2,1,0:T(1,128)S(1)}, u32[]{:S(2)}, u32[]{:S(2)}) %all-to-all-start.1) | async-done | bytes 16416 | tf_op jit(solution)/shard_map/all_to_all | solution.py:92
  74.6 0.1 reshape.275
  74.6 0.8 multiply_reduce_fusion.18
  75.4 0.8 multiply_reduce_fusion.17
  76.2 0.8 %multiply_reduce_fusion.14 = (f32[2,8]{1,0:T(2,128)S(1)}, f32[2,8]{1,0:T(2,128)S(1)}) fusion(f32[2,8,8]{2,1,0:T(8,128)S(1)} %reshape.275, f32[2,8]{1,0:T(2,128)S(1)} %fusion.11, f32[8,8]{1,0:T(8,128)} %get-tuple-element.41, f32[8,8]{1,0:T(8,128)} %get-tuple-element.40), kind=kLoop, calls=%fused_computation.53 | loop fusion | flops 736 | bytes 1216 | tf_op jit(solution)/shard_map/reduce_sum | solution.py:29
  77.0 0.8 multiply_reduce_fusion.13
  77.8 0.8 %multiply_reduce_fusion.10 = (f32[2,8]{1,0:T(2,128)S(1)}, f32[2,8]{1,0:T(2,128)S(1)}) fusion(f32[2,8,8]{2,1,0:T(8,128)S(1)} %reshape.275, f32[2,8]{1,0:T(2,128)S(1)} %subtract_multiply_fusion, f32[8,8]{1,0:T(8,128)} %get-tuple-element.39, f32[8,8]{1,0:T(8,128)} %get-tuple-element.38), kind=kLoop, calls=%fused_computation.48 | loop fusion | flops 736 | bytes 1216 | tf_op jit(solution)/shard_map/reduce_sum | solution.py:29
  78.7 0.8 multiply_reduce_fusion.9
  79.4 0.1 copy.52
  79.5 0.1 multiply_reduce_fusion
  79.7 0.8 add_divide_fusion
  80.5 1.5 %fusion.6 = (f32[8,2048]{1,0:T(8,128)}, f32[8,2048]{1,0:T(8,128)}) fusion(f32[2,8,2048]{2,1,0:T(8,128)S(1)} %get-tuple-element.25, f32[64,2048]{1,0:T(8,128)} %param.9, s32[]{:T(128)S(6)} %select_n.4, f32[64,2048]{1,0:T(8,128)} %param.8), kind=kLoop, calls=%fused_computation.33 | loop fusion | flops 32768 | bytes 393220 | tf_op jit(solution)/shard_map/sub | solution.py:103
  (21 shorter events, 0.3 us)
Async XLA Ops:
  0.6 1.6 %copy-start = (bf16[512,2048]{1,0:T(8,128)(2,1)S(1)}, bf16[512,2048]{1,0:T(8,128)(2,1)}, u32[]{:S(2)}) copy-start(bf16[512,2048]{1,0:T(8,128)(2,1)} %param.6) | copy-start | bytes 6291460
  0.6 3.4 %copy-start.2 = (f32[64,2048]{1,0:T(8,128)S(1)}, f32[64,2048]{1,0:T(8,128)}, u32[]{:S(2)}) copy-start(f32[64,2048]{1,0:T(8,128)} %param.9) | copy-start | bytes 1572868
  0.7 3.4 %copy-start.1 = (bf16[512,2048]{1,0:T(8,128)(2,1)S(1)}, bf16[512,2048]{1,0:T(8,128)(2,1)}, u32[]{:S(2)}) copy-start(bf16[512,2048]{1,0:T(8,128)(2,1)} %param.7) | copy-start | bytes 6291460
  4.8 1.7 %collective-permute-start = (f32[512,128]{0,1:T(8,128)S(1)}, f32[512,128]{0,1:T(8,128)S(1)}, u32[]{:S(2)}, u32[]{:S(2)}) collective-permute-start(f32[512,128]{0,1:T(8,128)S(1)} %pad_maximum_fusion.1), channel_id=1, source_target_pairs={{0,1},{1,0},{2,3},{3,2},{4,5},{5,4},{6,7},{7,6},{8,9},{9,8},{10,11... | collective-permute-start | bytes 786440 | tf_op jit(solution)/shard_map/ppermute | solution.py:15
  6.5 9.5 %collective-permute-start.1 = (f32[512,128]{0,1:T(8,128)S(1)}, f32[512,128]{0,1:T(8,128)S(1)}, u32[]{:S(2)}, u32[]{:S(2)}) collective-permute-start(f32[512,128]{0,1:T(8,128)S(1)} %fusion.12), channel_id=1, source_target_pairs={{0,2},{1,3},{2,0},{3,1},{4,6},{5,7},{6,4},{7,5},{8,10},{9,11},{10,... | collective-permute-start | bytes 786440 | tf_op jit(solution)/shard_map/ppermute | solution.py:15
  18.2 31.5 %all-to-all-start = ((f32[8,2,8,2048]{3,2,1,0:T(8,128)}), f32[8,2,8,2048]{3,2,1,0:T(8,128)S(1)}, u32[]{:S(2)}, u32[]{:S(2)}) async-start(f32[8,2,8,2048]{3,2,1,0:T(8,128)} %pad_maximum_fusion), calls=%async_computation | async-start | bytes 2097152 | tf_op jit(solution)/shard_map/all_to_all | solution.py:82
  51.1 28.6 %copy-start.3 = (f32[2,8,2048]{2,1,0:T(8,128)S(1)}, f32[2,8,2048]{2,1,0:T(8,128)}, u32[]{:S(2)}) copy-start(f32[2,8,2048]{2,1,0:T(8,128)} %param.10) | copy-start | bytes 393220
  51.1 28.6 %copy-start.4 = (f32[2,8,2048]{2,1,0:T(8,128)S(1)}, f32[2,8,2048]{2,1,0:T(8,128)}, u32[]{:S(2)}) copy-start(f32[2,8,2048]{2,1,0:T(8,128)} %param.11) | copy-start | bytes 393220
  64.1 10.5 %all-to-all-start.1 = ((f32[32,1,128]{2,1,0:T(1,128)}), f32[32,1,128]{2,1,0:T(1,128)S(1)}, u32[]{:S(2)}, u32[]{:S(2)}) async-start(f32[32,1,128]{2,1,0:T(1,128)} %broadcast_in_dim.5), calls=%async_computation.1 | async-start | bytes 32768 | tf_op jit(solution)/shard_map/all_to_all | solution.py:92

commit v2 on v1

v2 whole, which is shorter than its diff:
```python
import functools

import jax
import jax.numpy as jnp
from jax import lax
from jax.experimental import pallas as pl
from jax.experimental.pallas import tpu as pltpu
from jax.sharding import PartitionSpec as P

SCALE = 2.0
NORM_EPS = 1e-06
LANES = 128
VMEM_LIMIT = 32 * 1024 * 1024
IN_VMEM = pl.BlockSpec(memory_space=pltpu.VMEM)
IN_SMEM = pl.BlockSpec(memory_space=pltpu.SMEM)


def other_of(block, axis, apart):
    route = [(here, here ^ apart) for here in range(lax.axis_size(axis))]
    return lax.ppermute(block, axis, route)


def butterfly_sum(block, axis, apart):
    other = jnp.zeros_like(block)
    while apart < lax.axis_size(axis):
        block = block + other
        other = other_of(block, axis, apart)
        apart *= 2
    return block, other


def exact_dot(left, right, dims):
    return lax.dot_general(
        left,
        right,
        (dims, ((), ())),
        precision=lax.Precision.HIGHEST,
        preferred_element_type=jnp.float32,
    )


def rank_sums(mine_ref, other_ref):
    return (SCALE * (mine_ref[...] + other_ref[...])).astype(jnp.bfloat16)


def gradient(sums, rows_ref):
    return jnp.dot(sums, rows_ref[...], preferred_element_type=jnp.float32)


def rank_block(ref, me, k, owned):
    block = (me ^ k) % (ref.shape[0] // owned)
    return ref[pl.ds(pl.multiple_of(block * owned, owned), owned), :]


def far_kernel(me_ref, mine_ref, other_ref, rows_ref, sums_ref, *refs):
    *piece_refs, grad_ref = refs
    sums = rank_sums(mine_ref, other_ref)
    sums_ref[...] = sums
    grad_ref[...] = gradient(sums, rows_ref)
    owned = piece_refs[0].shape[0]
    for k, piece_ref in enumerate(piece_refs):
        piece_ref[...] = rank_block(grad_ref, me_ref[0], k, owned)


def near_kernel(me_ref, mine_ref, other_ref, tokens_ref, cotangent_ref, sums_ref, *refs):
    *piece_refs, grad_a_ref, grad_b_ref = refs
    sums = rank_sums(mine_ref, other_ref)
    half = sums.shape[0] // 2
    sums_ref[...] = sums[:half]
    grad_a_ref[...] = gradient(sums[:half], tokens_ref)
    grad_b_ref[...] = gradient(sums[half:], cotangent_ref)
    owned = piece_refs[0].shape[0] // 2
    for k, piece_ref in enumerate(piece_refs):
        piece_ref[:owned] = rank_block(grad_a_ref, me_ref[0], k, owned)
        piece_ref[owned:] = rank_block(grad_b_ref, me_ref[0], k, owned)


def pieces_of(factor, refs, replicas, owned):
    near = refs[: replicas // 2]
    far = refs[replicas // 2 : replicas]
    return [ref.at[factor * owned : (factor + 1) * owned] for ref in near] + list(far)


def inner_products(pieces, rows_ref, first):
    replicas = len(pieces)
    columns = pieces[0].shape[1]
    pairs = [(i, j) for i in range(replicas) for j in range(i, replicas)]
    sums = {}
    for start in range(0, columns, LANES):
        parts = [ref[:, start : start + LANES] for ref in pieces]
        for i, j in pairs:
            product = parts[i] * parts[j]
            sums[i, j] = sums[i, j] + product if start else product
    for i, j in pairs:
        row = jnp.sum(sums[i, j], axis=0, keepdims=True)
        at = first + i * replicas + j
        rows_ref[at : at + 1, :] = row
        if i != j:
            at = first + j * replicas + i
            rows_ref[at : at + 1, :] = row


def relabelled(gram, me, replicas):
    lanes = gram.shape[1]
    source = lax.broadcasted_iota(jnp.int32, (lanes, lanes), 0)
    target = lax.broadcasted_iota(jnp.int32, (lanes, lanes), 1)
    chosen = jnp.where(target == source ^ (me * replicas + me), 1.0, 0.0)
    return exact_dot(gram, chosen.astype(jnp.float32), ((1,), (0,)))


def first_gram_kernel(*refs):
    replicas = len(refs) - 1
    owned = refs[replicas - 1].shape[0]
    inner_products(pieces_of(0, refs, replicas, owned), refs[-1], 0)


def second_gram_kernel(me_ref, other_rows_ref, *refs):
    replicas = len(refs) - 2
    owned = refs[replicas - 1].shape[0]
    spread_ref, rows_ref = refs[-2:]
    size = replicas * replicas
    rows_ref[:size, :] = other_rows_ref[...]
    inner_products(pieces_of(1, refs, replicas, owned), rows_ref, size)
    ones = jnp.ones((8, LANES), jnp.float32)
    gram = exact_dot(ones, rows_ref[...], ((1,), (1,)))
    gram = relabelled(gram, me_ref[0], replicas)
    spread_ref[...] = jnp.broadcast_to(gram[:1, :][None], spread_ref.shape)


def tree_weights(gram, replicas):
    size = replicas * replicas
    lanes = gram.shape[1]
    source = lax.broadcasted_iota(jnp.int32, (lanes, lanes), 0)
    target = lax.broadcasted_iota(jnp.int32, (lanes, lanes), 1)
    same_factor = source // size == target // size
    source_i = source % size // replicas
    source_j = source % replicas
    target_i = target % size // replicas
    target_j = target % replicas

    def gather(values, wanted):
        chosen = jnp.where(same_factor & wanted, 1.0, 0.0).astype(jnp.float32)
        return exact_dot(values, chosen, ((1,), (0,)))

    weights = jnp.ones_like(gram)
    level = 0
    while 1 << level < replicas:
        left, right = source_i >> level, source_j >> level
        kept = []
        for target_at in (target_i >> level, target_j >> level):
            norm = gather(gram, (left == target_at) & (right == target_at))
            cross = gather(gram, (left == target_at) & (right == (target_at ^ 1)))
            kept.append(1.0 - cross / (2.0 * (norm + NORM_EPS)))
        gram = gram * kept[0] * kept[1]
        weights = weights * kept[0]
        level += 1
    return weights


def finish_kernel(me_ref, gathered_ref, *refs, replicas):
    half = replicas // 2
    near, far_a, far_b = refs[:half], refs[half : 2 * half], refs[2 * half : 3 * half]
    first_ref, second_ref, down_ref, up_ref = refs[3 * half : 3 * half + 4]
    new_down_ref, new_up_ref, new_first_ref, new_second_ref = refs[3 * half + 4 :]
    gram = jnp.sum(gathered_ref[...], axis=0)
    gram = jnp.broadcast_to(gram, (8, gram.shape[1]))
    weights = tree_weights(relabelled(gram, me_ref[0], replicas), replicas)
    factors = ((far_a, down_ref, new_down_ref), (far_b, up_ref, new_up_ref))
    for factor, (far, old_ref, new_ref) in enumerate(factors):
        owned = old_ref.shape[0]
        combined = jnp.zeros(old_ref.shape, jnp.float32)
        for i, piece_ref in enumerate(pieces_of(factor, near + far, replicas, owned)):
            lane = (factor * replicas + i) * replicas
            combined += weights[:1, lane : lane + 1] * piece_ref[...]
        moment_one = 0.9 * first_ref[factor] + 0.1 * combined
        moment_two = 0.95 * second_ref[factor] + 0.05 * combined * combined
        new_first_ref[factor] = moment_one
        new_second_ref[factor] = moment_two
        change = 0.001 * moment_one / (jnp.sqrt(moment_two) + 1e-08)
        new_ref[...] = old_ref[...] - change


def body(
    tokens,
    cotangent,
    lowrank_down_factor,
    lowrank_up_factor,
    first_moment_estimate,
    second_moment_estimate,
):
    replicas = lax.axis_size("dp")
    everyone = replicas * lax.axis_size("tensor")
    half = replicas // 2
    rows, columns = tokens.shape
    rank = lowrank_down_factor.shape[0]
    owned_rows = first_moment_estimate.shape[1]
    size = replicas * replicas
    me = lax.axis_index("dp")
    position = me.astype(jnp.int32).reshape(1)
    params = pltpu.CompilerParams(vmem_limit_bytes=VMEM_LIMIT)

    def shape(*dims, dtype=jnp.float32):
        return jax.ShapeDtypeStruct(dims, dtype)

    def chip_sum(block, factor):
        partial = lax.dot_general(
            factor,
            block,
            (((1,), (1,)), ((), ())),
            preferred_element_type=jnp.float32,
        )
        return partial + other_of(partial, "tensor", 1)

    def half_of(block, owner):
        start = owner // half * (half * owned_rows)
        return lax.dynamic_slice_in_dim(block, start, half * owned_rows, 0)

    def sent(block, apart):
        route = [(here, here ^ apart) for here in range(replicas)]
        return lax.ppermute(block, "dp", route)

    def far_exchange(sums, block, name):
        sums, *pieces = pl.pallas_call(
            far_kernel,
            in_specs=[IN_SMEM] + [IN_VMEM] * 3,
            out_shape=[shape(rank // 2, rows, dtype=jnp.bfloat16)]
            + [shape(owned_rows, columns)] * half,
            scratch_shapes=[pltpu.VMEM((rank // 2, columns), jnp.float32)],
            compiler_params=params,
            name=name,
        )(position, *sums, block)
        return sums, pieces

    adapter_in = lowrank_down_factor.astype(jnp.bfloat16)
    adapter_out = lowrank_up_factor.astype(jnp.bfloat16)
    upstream = chip_sum(cotangent, adapter_out)
    hidden = chip_sum(tokens, adapter_in)
    far_owner = (me + half) % replicas
    upstream_far = butterfly_sum(half_of(upstream, far_owner), "tensor", 2)
    hidden_far = butterfly_sum(half_of(hidden, far_owner), "tensor", 2)
    near = jnp.concatenate([half_of(upstream, me), half_of(hidden, me)])
    upstream_far, far_a = far_exchange(upstream_far, tokens, "far_a")
    _, far_b = far_exchange(hidden_far, cotangent, "far_b")
    near, far_b = lax.optimization_barrier((near, far_b))
    near = butterfly_sum(near, "tensor", 2)
    far_a = [sent(piece, half + k) for k, piece in enumerate(far_a)]
    far_b = [sent(piece, half + k) for k, piece in enumerate(far_b)]
    upstream_near, own, *near = pl.pallas_call(
        near_kernel,
        in_specs=[IN_SMEM] + [IN_VMEM] * 4,
        out_shape=[shape(rank // 2, rows, dtype=jnp.bfloat16)]
        + [shape(2 * owned_rows, columns)] * half,
        scratch_shapes=[pltpu.VMEM((rank // 2, columns), jnp.float32)] * 2,
        compiler_params=params,
        name="near",
    )(position, *near, tokens, cotangent)
    near = [own] + [sent(piece, k + 1) for k, piece in enumerate(near)]

    upstream = jnp.where(
        me < half,
        jnp.concatenate([upstream_near, upstream_far]),
        jnp.concatenate([upstream_far, upstream_near]),
    )
    input_grad = lax.dot_general(
        upstream,
        adapter_in,
        (((0,), (0,)), ((), ())),
        preferred_element_type=jnp.float32,
    )
    input_grad = input_grad.astype(jnp.bfloat16)
    owned_down = lax.dynamic_slice_in_dim(
        lowrank_down_factor, me * owned_rows, owned_rows, 0
    )
    owned_up = lax.dynamic_slice_in_dim(
        lowrank_up_factor, me * owned_rows, owned_rows, 0
    )
    near, input_grad, owned_down, owned_up = lax.optimization_barrier(
        (near, input_grad, owned_down, owned_up)
    )

    rows_a = pl.pallas_call(
        first_gram_kernel,
        out_shape=shape(size, LANES),
        compiler_params=params,
        name="gram_a",
    )(*near, *far_a)
    spread = pl.pallas_call(
        second_gram_kernel,
        in_specs=[IN_SMEM] + [IN_VMEM] * (1 + replicas),
        out_shape=shape(everyone, 1, 2 * size),
        scratch_shapes=[pltpu.VMEM((2 * size, LANES), jnp.float32)],
        compiler_params=params,
        name="gram_b",
    )(position, rows_a, *near, *far_b)
    gathered = lax.all_to_all(spread, ("dp", "tensor"), 0, 0, tiled=True)

    row_out = shape(owned_rows, columns)
    moment_out = shape(*first_moment_estimate.shape)
    updated_down_factor, updated_up_factor, moment_one, moment_two = pl.pallas_call(
        functools.partial(finish_kernel, replicas=replicas),
        in_specs=[IN_SMEM] + [IN_VMEM] * (3 * half + 5),
        out_shape=(row_out, row_out, moment_out, moment_out),
        compiler_params=params,
        name="finish",
    )(
        position,
        gathered,
        *near,
        *far_a,
        *far_b,
        first_moment_estimate,
        second_moment_estimate,
        owned_down,
        owned_up,
    )
    return (input_grad, updated_down_factor, updated_up_factor, moment_one, moment_two)


def solution(mesh):
    placed = (
        P("dp", "tensor"),
        P("dp", "tensor"),
        P(None, "tensor"),
        P(None, "tensor"),
        P(None, "dp", "tensor"),
        P(None, "dp", "tensor"),
    )
    return jax.shard_map(
        body,
        mesh=mesh,
        in_specs=placed,
        out_specs=(
            P("dp", "tensor"),
            P("dp", "tensor"),
            P("dp", "tensor"),
            P(None, "dp", "tensor"),
            P(None, "dp", "tensor"),
        ),
        check_vma=False,
    )
```

time: 82.7 us -> 57.3 us (0.69)
  waiting for transfers between devices: 35.2 us -> 6.14 us
  starting transfers between devices: 12.9 us -> 25.6 us
  local copies, waits for them, and re-layouts: 14.8 us -> 2.5 us
  other arithmetic: 11.8 us -> 0.05 us
  blocking collectives: 0 us -> 10.4 us
  Pallas kernels: 0 us -> 5.13 us
    all_to_all x2 -> x0, waiting for transfers between devices: 27.4 us -> none  [the longest x1 23.4 us: body(): pieces = lax.all_to_all(outgoing, 'dp', 0, 0, tiled=True)]
    ppermute x2 -> x16, starting transfers between devices: 3.44 us -> 25.6 us  [the longest x11 19.8 us: sent(): return lax.ppermute(block, 'dp', route)]
    all_to_all x0 -> x1, blocking collectives: none -> 10.4 us  [body(): gathered = lax.all_to_all(spread, ('dp', 'tensor'), 0, 0, tiled=True)]
    all_to_all x2 -> x0, starting transfers between devices: 9.47 us -> none  [the longest x1 6.09 us: body(): pieces = lax.all_to_all(outgoing, 'dp', 0, 0, tiled=True)]
    reduce_sum x8 -> x0, local copies, waits for them, and re-layouts: 7.37 us -> none  [body(): jnp.sum(pieces * pieces[other][None], (2, 3))]
    reduce_sum x9 -> x0, other arithmetic: 6.25 us -> none  [the longest x6 4.76 us: tree_weights(): norm = jnp.sum(same * jnp.sum(same * weighted, -1)[:, None, :], -1)]
    pallas_call x0 -> x6, Pallas kernels: none -> 5.13 us  [the longest x1 1.99 us: body(): pl.pallas_call(functools.partial(finish_kernel, replicas=replicas), in_sp...]
    unnamed x17 -> x12, local copies, waits for them, and re-layouts: 5.68 us -> 1.61 us
  transfers between devices with their start and end apart: 4 -> 16, of which waited for: 4 -> 5; matrix products, arithmetic and copies ran while one was open for 6% -> 8% of each run, Pallas kernels for 0% -> 4%
where the time goes in v2:
time: 57.3 us; the launch traced here: 57.1 us
  starting transfers between devices  25.6 us (45%)
  blocking collectives  10.4 us (18%)
  matrix products  6.55 us (11%)
  waiting for transfers between devices  6.14 us (11%)
  Pallas kernels  5.13 us (9%)
  local copies, waits for them, and re-layouts  2.5 us (4%)
  between operations  0.73 us (1%)
    ppermute x11, starting transfers between devices, sent(): return lax.ppermute(block, 'dp', route)  19.8 us
    all_to_all x1, blocking collectives, body(): gathered = lax.all_to_all(spread, ('dp', 'tensor'), 0, 0, tiled=True)  10.4 us
    ppermute x5, starting transfers between devices, other_of(): return lax.ppermute(block, axis, route)  5.77 us
    ppermute x5, waiting for transfers between devices, other_of(): return lax.ppermute(block, axis, route)  3.48 us
    dot_general x2, matrix products, chip_sum(): lax.dot_general(factor, block, (((1,), (1,)), ((), ())), preferred_elemen...  3.42 us
    dot_general x1, matrix products, body(): lax.dot_general(upstream, adapter_in, (((0,), (0,)), ((), ())), preferred...  3.13 us
    ppermute x11, waiting for transfers between devices, sent(): return lax.ppermute(block, 'dp', route)  2.66 us
    pallas_call x1, Pallas kernels, body(): pl.pallas_call(functools.partial(finish_kernel, replicas=replicas), in_sp...  1.99 us
  transfers between devices with their start and end apart: 16, of which 5 were waited for; matrix products, arithmetic and copies ran while one was open for 8% of the time, Pallas kernels for 4%

profile of v2, /device:TPU:0, one launch (start us, length us, event | category | flops | bytes accessed | tf_op | source)
XLA Modules:
  0.0 57.1 jit_solution(5379749427775346639)
XLA Ops:
  0.6 0.0 copy-start
  0.6 0.0 copy-start.5
  0.7 2.7 %fusion.3 = f32[64,512]{1,0:T(8,128)S(1)} fusion(bf16[512,2048]{1,0:T(8,128)(2,1)} %rows_ref.3, f32[64,2048]{1,0:T(8,128)} %param.8), kind=kOutput, calls=%fused_computation.5 | convolution fusion | flops 134348800 | bytes 2752512 | tf_op jit(solution)/shard_map/dot_general | solution.py:206
  3.3 0.5 collective-permute-start.1
  3.8 0.0 copy-done
  3.8 0.8 %fusion = f32[64,512]{1,0:T(8,128)S(1)} fusion(bf16[512,2048]{1,0:T(8,128)(2,1)S(1)} %copy-done, f32[64,2048]{1,0:T(8,128)S(1)} %copy-done.5), kind=kOutput, calls=%fused_computation.1 | convolution fusion | flops 134348800 | bytes 2752512 | tf_op jit(solution)/shard_map/dot_general | solution.py:206
  4.6 0.1 collective-permute-start
  4.7 0.1 collective-permute-done.1
  4.9 2.9 %collective-permute-start.2 = (f32[32,512]{1,0:T(8,128)S(1)}, f32[32,512]{1,0:T(8,128)S(1)}, u32[]{:S(2)}, u32[]{:S(2)}) collective-permute-start(f32[32,512]{1,0:T(8,128)S(1)} %get-tuple-element.67.mine_ref), channel_id=1, source_target_pairs={{0,2},{1,3},{2,0},{3,1},{4,6},{5,7},{6,4},{7,5},{8,10},{9,11},{10,... | collective-permute-start | bytes 196616 | tf_op jit(solution)/shard_map/ppermute | solution.py:20
  7.8 0.0 collective-permute-done
  7.8 0.9 %collective-permute-start.7 = (f32[32,512]{1,0:T(8,128)S(1)}, f32[32,512]{1,0:T(8,128)S(1)}, u32[]{:S(2)}, u32[]{:S(2)}) collective-permute-start(f32[32,512]{1,0:T(8,128)S(1)} %get-tuple-element.65.mine_ref), channel_id=1, source_target_pairs={{0,2},{1,3},{2,0},{3,1},{4,6},{5,7},{6,4},{7,5},{8,10},{9,11},{10,... | collective-permute-start | bytes 196616 | tf_op jit(solution)/shard_map/ppermute | solution.py:20
  8.8 3.4 %collective-permute-done.7.other_ref = f32[32,512]{1,0:T(8,128)S(1)} collective-permute-done((f32[32,512]{1,0:T(8,128)S(1)}, f32[32,512]{1,0:T(8,128)S(1)}, u32[]{:S(2)}, u32[]{:S(2)}) %collective-permute-start.7) | collective-permute-done | bytes 65568 | tf_op jit(solution)/shard_map/ppermute | solution.py:20
  12.2 1.6 %copy-done.1 = bf16[512,2048]{1,0:T(8,128)(2,1)S(1)} copy-done((bf16[512,2048]{1,0:T(8,128)(2,1)S(1)}, bf16[512,2048]{1,0:T(8,128)(2,1)}, u32[]{:S(2)}) %copy-start.1) | copy-done | bytes 2097176
  13.8 0.5 far_a.1
  14.2 2.7 %collective-permute-start.8 = (f32[8,2048]{1,0:T(8,128)S(1)}, f32[8,2048]{1,0:T(8,128)S(1)}, u32[]{:S(2)}, u32[]{:S(2)}) collective-permute-start(f32[8,2048]{1,0:T(8,128)S(1)} %get-tuple-element.51), channel_id=1, source_target_pairs={{0,16},{4,20},{8,24},{12,28},{16,0},{20,4},{24,8},{28,12},{1,17},{... | collective-permute-start | bytes 196616 | tf_op jit(solution)/shard_map/ppermute | solution.py:220
  16.9 0.0 collective-permute-done.2.other_ref
  16.9 0.9 %far_b.1 = (bf16[32,512]{1,0:T(8,128)(2,1)}, f32[8,2048]{1,0:T(8,128)S(1)}, f32[8,2048]{1,0:T(8,128)S(1)}, f32[8,2048]{1,0:T(8,128)S(1)}, f32[8,2048]{1,0:T(8,128)S(1)}) custom-call(s32[1]{0:T(128)} %bitcast.me_ref, f32[32,512]{1,0:T(8,128)S(1)} %get-tuple-element.67.mine_ref, f32[32,512]{1,0:T(8,128)S(1)} %collective-permute-done.2.other_ref, ...), custom_call_target="tpu_custom_call" | custom-call | tf_op jit(solution)/shard_map/far_b/pallas_call | solution.py:223
  17.9 1.3 %collective-permute-start.3 = (f32[64,512]{1,0:T(8,128)S(1)}, f32[64,512]{1,0:T(8,128)S(1)}, u32[]{:S(2)}, u32[]{:S(2)}) collective-permute-start(f32[64,512]{1,0:T(8,128)S(1)} %pad_maximum_fusion.mine_ref), channel_id=1, source_target_pairs={{0,2},{1,3},{2,0},{3,1},{4,6},{5,7},{6,4},{7,5},{8,10},{9,11},{10,... | collective-permute-start | bytes 393224 | tf_op jit(solution)/shard_map/ppermute | solution.py:20
  19.1 1.3 %collective-permute-start.9 = (f32[8,2048]{1,0:T(8,128)S(1)}, f32[8,2048]{1,0:T(8,128)S(1)}, u32[]{:S(2)}, u32[]{:S(2)}) collective-permute-start(f32[8,2048]{1,0:T(8,128)S(1)} %get-tuple-element.52), channel_id=1, source_target_pairs={{0,20},{4,16},{8,28},{12,24},{16,4},{20,0},{24,12},{28,8},{1,21},{... | collective-permute-start | bytes 196616 | tf_op jit(solution)/shard_map/ppermute | solution.py:220
  20.4 3.6 %collective-permute-start.10 = (f32[8,2048]{1,0:T(8,128)S(1)}, f32[8,2048]{1,0:T(8,128)S(1)}, u32[]{:S(2)}, u32[]{:S(2)}) collective-permute-start(f32[8,2048]{1,0:T(8,128)S(1)} %get-tuple-element.53), channel_id=1, source_target_pairs={{0,24},{4,28},{8,16},{12,20},{16,8},{20,12},{24,0},{28,4},{1,25},{... | collective-permute-start | bytes 196616 | tf_op jit(solution)/shard_map/ppermute | solution.py:220
  24.0 0.0 collective-permute-done.3.other_ref
  24.0 0.8 %near.1 = (bf16[32,512]{1,0:T(8,128)(2,1)S(1)}, f32[16,2048]{1,0:T(8,128)S(1)}, f32[16,2048]{1,0:T(8,128)S(1)}, f32[16,2048]{1,0:T(8,128)S(1)}, f32[16,2048]{1,0:T(8,128)S(1)}) custom-call(s32[1]{0:T(128)} %bitcast.me_ref, f32[64,512]{1,0:T(8,128)S(1)} %pad_maximum_fusion.mine_ref, f32[64,512]{1,0:T(8,128)S(1)} %collective-permute-done.3.other_ref, ...), custom_call_target="tpu_custom_call" | custom-call | tf_op jit(solution)/shard_map/near/pallas_call | solution.py:248
  24.9 0.6 %collective-permute-start.4 = (f32[16,2048]{1,0:T(8,128)S(1)}, f32[16,2048]{1,0:T(8,128)S(1)}, u32[]{:S(2)}, u32[]{:S(2)}) collective-permute-start(f32[16,2048]{1,0:T(8,128)S(1)} %get-tuple-element.41), channel_id=1, source_target_pairs={{0,4},{4,0},{8,12},{12,8},{16,20},{20,16},{24,28},{28,24},{1,5},{5... | collective-permute-start | bytes 393224 | tf_op jit(solution)/shard_map/ppermute | solution.py:220
  25.5 1.4 %collective-permute-start.5 = (f32[16,2048]{1,0:T(8,128)S(1)}, f32[16,2048]{1,0:T(8,128)S(1)}, u32[]{:S(2)}, u32[]{:S(2)}) collective-permute-start(f32[16,2048]{1,0:T(8,128)S(1)} %get-tuple-element.42), channel_id=1, source_target_pairs={{0,8},{4,12},{8,0},{12,4},{16,24},{20,28},{24,16},{28,20},{1,9},{5... | collective-permute-start | bytes 393224 | tf_op jit(solution)/shard_map/ppermute | solution.py:220
  26.8 0.0 collective-permute-done.8.refs_4_
  26.8 1.6 %collective-permute-start.6 = (f32[16,2048]{1,0:T(8,128)S(1)}, f32[16,2048]{1,0:T(8,128)S(1)}, u32[]{:S(2)}, u32[]{:S(2)}) collective-permute-start(f32[16,2048]{1,0:T(8,128)S(1)} %get-tuple-element.43), channel_id=1, source_target_pairs={{0,12},{4,8},{8,4},{12,0},{16,28},{20,24},{24,20},{28,16},{1,13},{... | collective-permute-start | bytes 393224 | tf_op jit(solution)/shard_map/ppermute | solution.py:220
  28.5 0.8 %constant_dynamic-slice_fusion.1.refs_14_ = f32[8,2048]{1,0:T(8,128)S(1)} fusion(f32[64,2048]{1,0:T(8,128)} %param.8, s32[]{:T(128)S(6)} %select_n.43), kind=kLoop, calls=%fused_computation.15 | loop fusion | bytes 131076 | tf_op jit(solution)/shard_map/dynamic_slice | solution.py:271
  29.3 0.0 collective-permute-done.9.refs_5_
  29.3 1.1 %collective-permute-start.11 = (f32[8,2048]{1,0:T(8,128)S(1)}, f32[8,2048]{1,0:T(8,128)S(1)}, u32[]{:S(2)}, u32[]{:S(2)}) collective-permute-start(f32[8,2048]{1,0:T(8,128)S(1)} %get-tuple-element.54), channel_id=1, source_target_pairs={{0,28},{4,24},{8,20},{12,16},{16,12},{20,8},{24,4},{28,0},{1,29},{... | collective-permute-start | bytes 196616 | tf_op jit(solution)/shard_map/ppermute | solution.py:220
  30.4 0.0 collective-permute-done.10.refs_6_
  30.4 1.7 %collective-permute-start.12 = (f32[8,2048]{1,0:T(8,128)S(1)}, f32[8,2048]{1,0:T(8,128)S(1)}, u32[]{:S(2)}, u32[]{:S(2)}) collective-permute-start(f32[8,2048]{1,0:T(8,128)S(1)} %get-tuple-element.55), channel_id=1, source_target_pairs={{0,16},{4,20},{8,24},{12,28},{16,0},{20,4},{24,8},{28,12},{1,17},{... | collective-permute-start | bytes 196616 | tf_op jit(solution)/shard_map/ppermute | solution.py:220
  32.1 0.0 collective-permute-done.4.refs_1_
  32.1 1.3 %collective-permute-start.13 = (f32[8,2048]{1,0:T(8,128)S(1)}, f32[8,2048]{1,0:T(8,128)S(1)}, u32[]{:S(2)}, u32[]{:S(2)}) collective-permute-start(f32[8,2048]{1,0:T(8,128)S(1)} %get-tuple-element.56), channel_id=1, source_target_pairs={{0,20},{4,16},{8,28},{12,24},{16,4},{20,0},{24,12},{28,8},{1,21},{... | collective-permute-start | bytes 196616 | tf_op jit(solution)/shard_map/ppermute | solution.py:220
  33.4 0.0 collective-permute-done.5.refs_2_
  33.4 3.6 %collective-permute-start.14 = (f32[8,2048]{1,0:T(8,128)S(1)}, f32[8,2048]{1,0:T(8,128)S(1)}, u32[]{:S(2)}, u32[]{:S(2)}) collective-permute-start(f32[8,2048]{1,0:T(8,128)S(1)} %get-tuple-element.57), channel_id=1, source_target_pairs={{0,24},{4,28},{8,16},{12,20},{16,8},{20,12},{24,0},{28,4},{1,25},{... | collective-permute-start | bytes 196616 | tf_op jit(solution)/shard_map/ppermute | solution.py:220
  37.0 0.0 collective-permute-done.6.refs_3_
  37.0 1.1 %collective-permute-start.15 = (f32[8,2048]{1,0:T(8,128)S(1)}, f32[8,2048]{1,0:T(8,128)S(1)}, u32[]{:S(2)}, u32[]{:S(2)}) collective-permute-start(f32[8,2048]{1,0:T(8,128)S(1)} %get-tuple-element.58), channel_id=1, source_target_pairs={{0,28},{4,24},{8,20},{12,16},{16,12},{20,8},{24,4},{28,0},{1,29},{... | collective-permute-start | bytes 196616 | tf_op jit(solution)/shard_map/ppermute | solution.py:220
  38.1 3.1 %convolution_convert_fusion = bf16[512,2048]{1,0:T(8,128)(2,1)} fusion(f32[64,2048]{1,0:T(8,128)} %param.8, bf16[32,512]{1,0:T(8,128)(2,1)S(1)} %get-tuple-element.45, bf16[32,512]{1,0:T(8,128)(2,1)S(1)} %get-tuple-element.44, pred[]{:T(512)S(6)} %lt.24), kind=kOutput, calls=%fused_computation | convolution fusion | flops 135692288 | bytes 2686977 | tf_op jit(solution)/shard_map/dot_general | solution.py:264
  41.2 0.0 collective-permute-done.11.refs_7_
  41.2 0.2 gram_a.1.other_rows_ref
  41.4 0.1 collective-permute-done.12.refs_4_.refs_8_
  41.5 1.5 %collective-permute-done.13.refs_5_.refs_9_ = f32[8,2048]{1,0:T(8,128)S(1)} collective-permute-done((f32[8,2048]{1,0:T(8,128)S(1)}, f32[8,2048]{1,0:T(8,128)S(1)}, u32[]{:S(2)}, u32[]{:S(2)}) %collective-permute-start.13) | collective-permute-done | bytes 65568 | tf_op jit(solution)/shard_map/ppermute | solution.py:220
  43.1 0.0 collective-permute-done.14.refs_6_.refs_10_
  43.1 1.0 %collective-permute-done.15.refs_7_.refs_11_ = f32[8,2048]{1,0:T(8,128)S(1)} collective-permute-done((f32[8,2048]{1,0:T(8,128)S(1)}, f32[8,2048]{1,0:T(8,128)S(1)}, u32[]{:S(2)}, u32[]{:S(2)}) %collective-permute-start.15) | collective-permute-done | bytes 65568 | tf_op jit(solution)/shard_map/ppermute | solution.py:220
  44.0 0.7 %gram_b.1 = f32[32,1,128]{2,1,0:T(1,128)S(1)} custom-call(s32[1]{0:T(128)} %bitcast.me_ref, f32[64,128]{1,0:T(8,128)S(1)} %gram_a.1.other_rows_ref, f32[16,2048]{1,0:T(8,128)S(1)} %get-tuple-element.47.refs_0_, f32[16,2048]{1,0:T(8,128)S(1)} %collective-permute-done.4.refs_1_, f32[16,2048]{1,0:T(8,128)S(1)} %collective-permute-done.5.refs_2_, ...), custom_call_target="tpu_custom_call" | custom-call | tf_op jit(solution)/shard_map/gram_b/pallas_call | solution.py:287
  44.7 10.4 %all_to_all.5.gathered_ref = f32[32,1,128]{2,1,0:T(1,128)S(1)} all-to-all(f32[32,1,128]{2,1,0:T(1,128)S(1)} %gram_b.1), channel_id=1, replica_groups=mesh['dp'=8,'tensor'=4] {'dp','tensor'}, dimensions={0} | all-to-all | bytes 32768 | tf_op jit(solution)/shard_map/all_to_all | solution.py:295
  55.1 0.0 copy-done.4
  55.1 2.0 %finish.1 = (f32[8,2048]{1,0:T(8,128)}, f32[8,2048]{1,0:T(8,128)}, f32[2,8,2048]{2,1,0:T(8,128)}, f32[2,8,2048]{2,1,0:T(8,128)}) custom-call(s32[1]{0:T(128)} %bitcast.me_ref, f32[32,1,128]{2,1,0:T(1,128)S(1)} %all_to_all.5.gathered_ref, f32[16,2048]{1,0:T(8,128)S(1)} %get-tuple-element.47.refs_0_, f32[16,2048]{1,0:T(8,128)S(1)} %collective-permute-done.4.refs_1_, ...), custom_call_target="tpu_custom_call" | custom-call | tf_op jit(solution)/shard_map/finish/pallas_call | solution.py:299
  (13 shorter events, 0.1 us)
Async XLA Ops:
  0.6 3.2 %copy-start = (bf16[512,2048]{1,0:T(8,128)(2,1)S(1)}, bf16[512,2048]{1,0:T(8,128)(2,1)}, u32[]{:S(2)}) copy-start(bf16[512,2048]{1,0:T(8,128)(2,1)} %cotangent_ref.1) | copy-start | bytes 6291460
  0.6 3.2 %copy-start.5 = (f32[64,2048]{1,0:T(8,128)S(1)}, f32[64,2048]{1,0:T(8,128)}, u32[]{:S(2)}) copy-start(f32[64,2048]{1,0:T(8,128)} %param.9) | copy-start | bytes 1572868
  3.3 1.5 %collective-permute-start.1 = (f32[64,512]{1,0:T(8,128)S(1)}, f32[64,512]{1,0:T(8,128)S(1)}, u32[]{:S(2)}, u32[]{:S(2)}) collective-permute-start(f32[64,512]{1,0:T(8,128)S(1)} %fusion.3), channel_id=1, source_target_pairs={{0,1},{1,0},{2,3},{3,2},{4,5},{5,4},{6,7},{7,6},{8,9},{9,8},{10,11... | collective-permute-start | bytes 393224 | tf_op jit(solution)/shard_map/ppermute | solution.py:20
  4.6 3.2 %collective-permute-start = (f32[64,512]{1,0:T(8,128)S(1)}, f32[64,512]{1,0:T(8,128)S(1)}, u32[]{:S(2)}, u32[]{:S(2)}) collective-permute-start(f32[64,512]{1,0:T(8,128)S(1)} %fusion), channel_id=1, source_target_pairs={{0,1},{1,0},{2,3},{3,2},{4,5},{5,4},{6,7},{7,6},{8,9},{9,8},{10,11... | collective-permute-start | bytes 393224 | tf_op jit(solution)/shard_map/ppermute | solution.py:20
  4.9 12.0 %collective-permute-start.2 = (f32[32,512]{1,0:T(8,128)S(1)}, f32[32,512]{1,0:T(8,128)S(1)}, u32[]{:S(2)}, u32[]{:S(2)}) collective-permute-start(f32[32,512]{1,0:T(8,128)S(1)} %get-tuple-element.67.mine_ref), channel_id=1, source_target_pairs={{0,2},{1,3},{2,0},{3,1},{4,6},{5,7},{6,4},{7,5},{8,10},{9,11},{10,... | collective-permute-start | bytes 196616 | tf_op jit(solution)/shard_map/ppermute | solution.py:20
  7.8 4.3 %collective-permute-start.7 = (f32[32,512]{1,0:T(8,128)S(1)}, f32[32,512]{1,0:T(8,128)S(1)}, u32[]{:S(2)}, u32[]{:S(2)}) collective-permute-start(f32[32,512]{1,0:T(8,128)S(1)} %get-tuple-element.65.mine_ref), channel_id=1, source_target_pairs={{0,2},{1,3},{2,0},{3,1},{4,6},{5,7},{6,4},{7,5},{8,10},{9,11},{10,... | collective-permute-start | bytes 196616 | tf_op jit(solution)/shard_map/ppermute | solution.py:20
  12.2 1.6 %copy-start.1 = (bf16[512,2048]{1,0:T(8,128)(2,1)S(1)}, bf16[512,2048]{1,0:T(8,128)(2,1)}, u32[]{:S(2)}) copy-start(bf16[512,2048]{1,0:T(8,128)(2,1)} %rows_ref.3) | copy-start | bytes 6291460
  13.8 10.3 %copy-start.2 = (bf16[512,2048]{1,0:T(8,128)(2,1)S(1)}, bf16[512,2048]{1,0:T(8,128)(2,1)}, u32[]{:S(2)}) copy-start(bf16[512,2048]{1,0:T(8,128)(2,1)} %rows_ref.3) | copy-start | bytes 6291460
  14.2 12.6 %collective-permute-start.8 = (f32[8,2048]{1,0:T(8,128)S(1)}, f32[8,2048]{1,0:T(8,128)S(1)}, u32[]{:S(2)}, u32[]{:S(2)}) collective-permute-start(f32[8,2048]{1,0:T(8,128)S(1)} %get-tuple-element.51), channel_id=1, source_target_pairs={{0,16},{4,20},{8,24},{12,28},{16,0},{20,4},{24,8},{28,12},{1,17},{... | collective-permute-start | bytes 196616 | tf_op jit(solution)/shard_map/ppermute | solution.py:220
  17.9 6.2 %collective-permute-start.3 = (f32[64,512]{1,0:T(8,128)S(1)}, f32[64,512]{1,0:T(8,128)S(1)}, u32[]{:S(2)}, u32[]{:S(2)}) collective-permute-start(f32[64,512]{1,0:T(8,128)S(1)} %pad_maximum_fusion.mine_ref), channel_id=1, source_target_pairs={{0,2},{1,3},{2,0},{3,1},{4,6},{5,7},{6,4},{7,5},{8,10},{9,11},{10,... | collective-permute-start | bytes 393224 | tf_op jit(solution)/shard_map/ppermute | solution.py:20
  19.1 10.2 %collective-permute-start.9 = (f32[8,2048]{1,0:T(8,128)S(1)}, f32[8,2048]{1,0:T(8,128)S(1)}, u32[]{:S(2)}, u32[]{:S(2)}) collective-permute-start(f32[8,2048]{1,0:T(8,128)S(1)} %get-tuple-element.52), channel_id=1, source_target_pairs={{0,20},{4,16},{8,28},{12,24},{16,4},{20,0},{24,12},{28,8},{1,21},{... | collective-permute-start | bytes 196616 | tf_op jit(solution)/shard_map/ppermute | solution.py:220
  20.4 10.0 %collective-permute-start.10 = (f32[8,2048]{1,0:T(8,128)S(1)}, f32[8,2048]{1,0:T(8,128)S(1)}, u32[]{:S(2)}, u32[]{:S(2)}) collective-permute-start(f32[8,2048]{1,0:T(8,128)S(1)} %get-tuple-element.53), channel_id=1, source_target_pairs={{0,24},{4,28},{8,16},{12,20},{16,8},{20,12},{24,0},{28,4},{1,25},{... | collective-permute-start | bytes 196616 | tf_op jit(solution)/shard_map/ppermute | solution.py:220
  24.9 7.2 %collective-permute-start.4 = (f32[16,2048]{1,0:T(8,128)S(1)}, f32[16,2048]{1,0:T(8,128)S(1)}, u32[]{:S(2)}, u32[]{:S(2)}) collective-permute-start(f32[16,2048]{1,0:T(8,128)S(1)} %get-tuple-element.41), channel_id=1, source_target_pairs={{0,4},{4,0},{8,12},{12,8},{16,20},{20,16},{24,28},{28,24},{1,5},{5... | collective-permute-start | bytes 393224 | tf_op jit(solution)/shard_map/ppermute | solution.py:220
  25.5 7.9 %collective-permute-start.5 = (f32[16,2048]{1,0:T(8,128)S(1)}, f32[16,2048]{1,0:T(8,128)S(1)}, u32[]{:S(2)}, u32[]{:S(2)}) collective-permute-start(f32[16,2048]{1,0:T(8,128)S(1)} %get-tuple-element.42), channel_id=1, source_target_pairs={{0,8},{4,12},{8,0},{12,4},{16,24},{20,28},{24,16},{28,20},{1,9},{5... | collective-permute-start | bytes 393224 | tf_op jit(solution)/shard_map/ppermute | solution.py:220
  26.8 10.1 %collective-permute-start.6 = (f32[16,2048]{1,0:T(8,128)S(1)}, f32[16,2048]{1,0:T(8,128)S(1)}, u32[]{:S(2)}, u32[]{:S(2)}) collective-permute-start(f32[16,2048]{1,0:T(8,128)S(1)} %get-tuple-element.43), channel_id=1, source_target_pairs={{0,12},{4,8},{8,4},{12,0},{16,28},{20,24},{24,20},{28,16},{1,13},{... | collective-permute-start | bytes 393224 | tf_op jit(solution)/shard_map/ppermute | solution.py:220
  29.3 11.9 %collective-permute-start.11 = (f32[8,2048]{1,0:T(8,128)S(1)}, f32[8,2048]{1,0:T(8,128)S(1)}, u32[]{:S(2)}, u32[]{:S(2)}) collective-permute-start(f32[8,2048]{1,0:T(8,128)S(1)} %get-tuple-element.54), channel_id=1, source_target_pairs={{0,28},{4,24},{8,20},{12,16},{16,12},{20,8},{24,4},{28,0},{1,29},{... | collective-permute-start | bytes 196616 | tf_op jit(solution)/shard_map/ppermute | solution.py:220
  30.4 11.1 %collective-permute-start.12 = (f32[8,2048]{1,0:T(8,128)S(1)}, f32[8,2048]{1,0:T(8,128)S(1)}, u32[]{:S(2)}, u32[]{:S(2)}) collective-permute-start(f32[8,2048]{1,0:T(8,128)S(1)} %get-tuple-element.55), channel_id=1, source_target_pairs={{0,16},{4,20},{8,24},{12,28},{16,0},{20,4},{24,8},{28,12},{1,17},{... | collective-permute-start | bytes 196616 | tf_op jit(solution)/shard_map/ppermute | solution.py:220
  32.1 11.0 %collective-permute-start.13 = (f32[8,2048]{1,0:T(8,128)S(1)}, f32[8,2048]{1,0:T(8,128)S(1)}, u32[]{:S(2)}, u32[]{:S(2)}) collective-permute-start(f32[8,2048]{1,0:T(8,128)S(1)} %get-tuple-element.56), channel_id=1, source_target_pairs={{0,20},{4,16},{8,28},{12,24},{16,4},{20,0},{24,12},{28,8},{1,21},{... | collective-permute-start | bytes 196616 | tf_op jit(solution)/shard_map/ppermute | solution.py:220
  33.4 9.7 %collective-permute-start.14 = (f32[8,2048]{1,0:T(8,128)S(1)}, f32[8,2048]{1,0:T(8,128)S(1)}, u32[]{:S(2)}, u32[]{:S(2)}) collective-permute-start(f32[8,2048]{1,0:T(8,128)S(1)} %get-tuple-element.57), channel_id=1, source_target_pairs={{0,24},{4,28},{8,16},{12,20},{16,8},{20,12},{24,0},{28,4},{1,25},{... | collective-permute-start | bytes 196616 | tf_op jit(solution)/shard_map/ppermute | solution.py:220
  37.0 7.1 %collective-permute-start.15 = (f32[8,2048]{1,0:T(8,128)S(1)}, f32[8,2048]{1,0:T(8,128)S(1)}, u32[]{:S(2)}, u32[]{:S(2)}) collective-permute-start(f32[8,2048]{1,0:T(8,128)S(1)} %get-tuple-element.58), channel_id=1, source_target_pairs={{0,28},{4,24},{8,20},{12,16},{16,12},{20,8},{24,4},{28,0},{1,29},{... | collective-permute-start | bytes 196616 | tf_op jit(solution)/shard_map/ppermute | solution.py:220
  38.1 17.0 %copy-start.3 = (f32[2,8,2048]{2,1,0:T(8,128)S(1)}, f32[2,8,2048]{2,1,0:T(8,128)}, u32[]{:S(2)}) copy-start(f32[2,8,2048]{2,1,0:T(8,128)} %refs_12_.1) | copy-start | bytes 393220
  38.1 17.0 %copy-start.4 = (f32[2,8,2048]{2,1,0:T(8,128)S(1)}, f32[2,8,2048]{2,1,0:T(8,128)}, u32[]{:S(2)}) copy-start(f32[2,8,2048]{2,1,0:T(8,128)} %refs_13_.1) | copy-start | bytes 393220

commit v3 on v2

--- a/solution.py
+++ b/solution.py
@@ -37,42 +37,6 @@
         precision=lax.Precision.HIGHEST,
         preferred_element_type=jnp.float32,
     )
-
-
-def rank_sums(mine_ref, other_ref):
-    return (SCALE * (mine_ref[...] + other_ref[...])).astype(jnp.bfloat16)
-
-
-def gradient(sums, rows_ref):
-    return jnp.dot(sums, rows_ref[...], preferred_element_type=jnp.float32)
-
-
-def rank_block(ref, me, k, owned):
-    block = (me ^ k) % (ref.shape[0] // owned)
-    return ref[pl.ds(pl.multiple_of(block * owned, owned), owned), :]
-
-
-def far_kernel(me_ref, mine_ref, other_ref, rows_ref, sums_ref, *refs):
-    *piece_refs, grad_ref = refs
-    sums = rank_sums(mine_ref, other_ref)
-    sums_ref[...] = sums
-    grad_ref[...] = gradient(sums, rows_ref)
-    owned = piece_refs[0].shape[0]
-    for k, piece_ref in enumerate(piece_refs):
-        piece_ref[...] = rank_block(grad_ref, me_ref[0], k, owned)
-
-
-def near_kernel(me_ref, mine_ref, other_ref, tokens_ref, cotangent_ref, sums_ref, *refs):
-    *piece_refs, grad_a_ref, grad_b_ref = refs
-    sums = rank_sums(mine_ref, other_ref)
-    half = sums.shape[0] // 2
-    sums_ref[...] = sums[:half]
-    grad_a_ref[...] = gradient(sums[:half], tokens_ref)
-    grad_b_ref[...] = gradient(sums[half:], cotangent_ref)
-    owned = piece_refs[0].shape[0] // 2
-    for k, piece_ref in enumerate(piece_refs):
-        piece_ref[:owned] = rank_block(grad_a_ref, me_ref[0], k, owned)
-        piece_ref[owned:] = rank_block(grad_b_ref, me_ref[0], k, owned)
 
 
 def pieces_of(factor, refs, replicas, owned):
@@ -202,14 +166,13 @@
     def shape(*dims, dtype=jnp.float32):
         return jax.ShapeDtypeStruct(dims, dtype)
 
-    def chip_sum(block, factor):
-        partial = lax.dot_general(
+    def projected(block, factor):
+        return lax.dot_general(
             factor,
             block,
             (((1,), (1,)), ((), ())),
             preferred_element_type=jnp.float32,
         )
-        return partial + other_of(partial, "tensor", 1)
 
     def half_of(block, owner):
         start = owner // half * (half * owned_rows)
@@ -219,42 +182,43 @@
         route = [(here, here ^ apart) for here in range(replicas)]
         return lax.ppermute(block, "dp", route)
 
-    def far_exchange(sums, block, name):
-        sums, *pieces = pl.pallas_call(
-            far_kernel,
-            in_specs=[IN_SMEM] + [IN_VMEM] * 3,
-            out_shape=[shape(rank // 2, rows, dtype=jnp.bfloat16)]
-            + [shape(owned_rows, columns)] * half,
-            scratch_shapes=[pltpu.VMEM((rank // 2, columns), jnp.float32)],
-            compiler_params=params,
-            name=name,
-        )(position, *sums, block)
-        return sums, pieces
+    def rank_sums(addends):
+        return (SCALE * (addends[0] + addends[1])).astype(jnp.bfloat16)
+
+    def gradient(sums, block):
+        return jnp.dot(sums, block, preferred_element_type=jnp.float32)
+
+    def pieces_for(grad):
+        return [
+            lax.dynamic_slice_in_dim(
+                grad, (me ^ k) % half * owned_rows, owned_rows, 0
+            )
+            for k in range(half)
+        ]
 
     adapter_in = lowrank_down_factor.astype(jnp.bfloat16)
     adapter_out = lowrank_up_factor.astype(jnp.bfloat16)
-    upstream = chip_sum(cotangent, adapter_out)
-    hidden = chip_sum(tokens, adapter_in)
+    upstream = projected(cotangent, adapter_out)
+    hidden = projected(tokens, adapter_in)
+    upstream = upstream + other_of(upstream, "tensor", 1)
+    hidden = hidden + other_of(hidden, "tensor", 1)
     far_owner = (me + half) % replicas
-    upstream_far = butterfly_sum(half_of(upstream, far_owner), "tensor", 2)
-    hidden_far = butterfly_sum(half_of(hidden, far_owner), "tensor", 2)
-    near = jnp.concatenate([half_of(upstream, me), half_of(hidden, me)])
-    upstream_far, far_a = far_exchange(upstream_far, tokens, "far_a")
-    _, far_b = far_exchange(hidden_far, cotangent, "far_b")
-    near, far_b = lax.optimization_barrier((near, far_b))
-    near = butterfly_sum(near, "tensor", 2)
+    upstream_far = rank_sums(butterfly_sum(half_of(upstream, far_owner), "tensor", 2))
+    far_a = pieces_for(gradient(upstream_far, tokens))
+    rest = jnp.concatenate(
+        [half_of(hidden, far_owner), half_of(hidden, me), half_of(upstream, me)]
+    )
+    rest, upstream_far, far_a = lax.optimization_barrier((rest, upstream_far, far_a))
     far_a = [sent(piece, half + k) for k, piece in enumerate(far_a)]
+    rest = rank_sums(butterfly_sum(rest, "tensor", 2))
+    hidden, upstream_near = rest[:rank], rest[rank:]
+    grad_b = gradient(hidden, cotangent)
+    far_b = pieces_for(grad_b[: rank // 2])
+    near_b = pieces_for(grad_b[rank // 2 :])
+    near_a = pieces_for(gradient(upstream_near, tokens))
+    near = [jnp.concatenate(pair) for pair in zip(near_a, near_b)]
     far_b = [sent(piece, half + k) for k, piece in enumerate(far_b)]
-    upstream_near, own, *near = pl.pallas_call(
-        near_kernel,
-        in_specs=[IN_SMEM] + [IN_VMEM] * 4,
-        out_shape=[shape(rank // 2, rows, dtype=jnp.bfloat16)]
-        + [shape(2 * owned_rows, columns)] * half,
-        scratch_shapes=[pltpu.VMEM((rank // 2, columns), jnp.float32)] * 2,
-        compiler_params=params,
-        name="near",
-    )(position, *near, tokens, cotangent)
-    near = [own] + [sent(piece, k + 1) for k, piece in enumerate(near)]
+    near = near[:1] + [sent(piece, k) for k, piece in enumerate(near) if k]
 
     upstream = jnp.where(
         me < half,

time: 57.3 us -> 56.8 us (level)
  waiting for transfers between devices: 6.14 us -> 8.84 us
  Pallas kernels: 5.13 us -> 2.87 us
  local copies, waits for them, and re-layouts: 2.5 us -> 1.8 us
    ppermute x11, waiting for transfers between devices: 2.66 us -> 5.15 us  [sent(): return lax.ppermute(block, 'dp', route)]
    pallas_call x3 -> x0, Pallas kernels: 2.28 us -> none  [the longest x2 1.43 us: far_exchange(): pl.pallas_call(far_kernel, in_specs=[IN_SMEM] + [IN_VMEM] * 3, out_shape=...]
    dot_general x1, matrix products: 3.13 us -> 2.06 us  [body(): lax.dot_general(upstream, adapter_in, (((0,), (0,)), ((), ())), preferred...]
    ppermute x11, starting transfers between devices: 19.8 us -> 20.7 us  [sent(): return lax.ppermute(block, 'dp', route)]
    dynamic_slice x1, local copies, waits for them, and re-layouts: 0.84 us -> 0.01 us  [body(): lax.dynamic_slice_in_dim(lowrank_down_factor, me * owned_rows, owned_rows...]
    ppermute x5 -> x4, starting transfers between devices: 5.77 us -> 5.15 us  [other_of(): return lax.ppermute(block, axis, route)]
    dot_general x2 -> x5, matrix products: 3.42 us -> 4 us  [the longest x2 2.56 us: projected(): lax.dot_general(factor, block, (((1,), (1,)), ((), ())), preferred_elemen...]
    ppermute x5 -> x4, waiting for transfers between devices: 3.48 us -> 3.69 us  [other_of(): return lax.ppermute(block, axis, route)]
  transfers between devices with their start and end apart: 16 -> 15, of which waited for: 5 -> 5; matrix products, arithmetic and copies ran while one was open for 8% -> 7% of each run, Pallas kernels for 4% -> 0%
where the time goes in v3:
time: 56.8 us; the launch traced here: 56.7 us
  starting transfers between devices  25.9 us (46%)
  blocking collectives  10.1 us (18%)
  waiting for transfers between devices  8.84 us (16%)
  matrix products  6.06 us (11%)
  Pallas kernels  2.87 us (5%)
  local copies, waits for them, and re-layouts  1.8 us (3%)
  between operations  0.97 us (2%)
    ppermute x11, starting transfers between devices, sent(): return lax.ppermute(block, 'dp', route)  20.7 us
    all_to_all x1, blocking collectives, body(): gathered = lax.all_to_all(spread, ('dp', 'tensor'), 0, 0, tiled=True)  10.1 us
    ppermute x4, starting transfers between devices, other_of(): return lax.ppermute(block, axis, route)  5.15 us
    ppermute x11, waiting for transfers between devices, sent(): return lax.ppermute(block, 'dp', route)  5.15 us
    ppermute x4, waiting for transfers between devices, other_of(): return lax.ppermute(block, axis, route)  3.69 us
    dot_general x2, matrix products, projected(): lax.dot_general(factor, block, (((1,), (1,)), ((), ())), preferred_elemen...  2.56 us
    dot_general x1, matrix products, body(): lax.dot_general(upstream, adapter_in, (((0,), (0,)), ((), ())), preferred...  2.06 us
    pallas_call x1, Pallas kernels, body(): pl.pallas_call(functools.partial(finish_kernel, replicas=replicas), in_sp...  1.99 us
  transfers between devices with their start and end apart: 15, of which 5 were waited for; matrix products, arithmetic and copies ran while one was open for 7% of the time, Pallas kernels for 0%

profile of v3, /device:TPU:0, one launch (start us, length us, event | category | flops | bytes accessed | tf_op | source)
XLA Modules:
  0.0 56.7 jit_solution(2586437283938565878)
XLA Ops:
  0.6 0.0 copy-start
  0.7 0.0 copy-start.3
  0.7 1.6 %copy-done = bf16[512,2048]{1,0:T(8,128)(2,1)S(1)} copy-done((bf16[512,2048]{1,0:T(8,128)(2,1)S(1)}, bf16[512,2048]{1,0:T(8,128)(2,1)}, u32[]{:S(2)}) %copy-start) | copy-done | bytes 2097176
  2.2 1.8 %fusion.3 = f32[64,512]{1,0:T(8,128)S(1)} fusion(bf16[512,2048]{1,0:T(8,128)(2,1)S(1)} %copy-done, f32[64,2048]{1,0:T(8,128)} %param.8), kind=kOutput, calls=%fused_computation.10 | convolution fusion | flops 134348800 | bytes 2752512 | tf_op jit(solution)/shard_map/dot_general | solution.py:170
  4.0 0.5 collective-permute-start
  4.5 0.8 %fusion = f32[64,512]{1,0:T(8,128)S(1)} fusion(bf16[512,2048]{1,0:T(8,128)(2,1)S(1)} %copy-done.3, f32[64,2048]{1,0:T(8,128)S(1)} %copy-done.6), kind=kOutput, calls=%fused_computation.1 | convolution fusion | flops 134348800 | bytes 2752512 | tf_op jit(solution)/shard_map/dot_general | solution.py:170
  5.3 0.1 collective-permute-start.1
  5.5 0.0 collective-permute-done
  5.6 0.0 copy-start.5
  5.6 1.1 %collective-permute-done.1 = f32[64,512]{1,0:T(8,128)S(1)} collective-permute-done((f32[64,512]{1,0:T(8,128)S(1)}, f32[64,512]{1,0:T(8,128)S(1)}, u32[]{:S(2)}, u32[]{:S(2)}) %collective-permute-start.1) | collective-permute-done | bytes 131104 | tf_op jit(solution)/shard_map/ppermute | solution.py:20
  6.8 2.7 %collective-permute-start.2 = (f32[32,512]{1,0:T(8,128)S(1)}, f32[32,512]{1,0:T(8,128)S(1)}, u32[]{:S(2)}, u32[]{:S(2)}) collective-permute-start(f32[32,512]{1,0:T(8,128)S(1)} %get-tuple-element.57), channel_id=1, source_target_pairs={{0,2},{1,3},{2,0},{3,1},{4,6},{5,7},{6,4},{7,5},{8,10},{9,11},{10,... | collective-permute-start | bytes 196616 | tf_op jit(solution)/shard_map/ppermute | solution.py:20
  9.5 2.6 %collective-permute-done.2 = f32[32,512]{1,0:T(8,128)S(1)} collective-permute-done((f32[32,512]{1,0:T(8,128)S(1)}, f32[32,512]{1,0:T(8,128)S(1)}, u32[]{:S(2)}, u32[]{:S(2)}) %collective-permute-start.2) | collective-permute-done | bytes 65568 | tf_op jit(solution)/shard_map/ppermute | solution.py:20
  12.1 0.5 fusion.17
  12.6 1.8 %collective-permute-start.3 = (f32[96,512]{1,0:T(8,128)S(1)}, f32[96,512]{1,0:T(8,128)S(1)}, u32[]{:S(2)}, u32[]{:S(2)}) collective-permute-start(f32[96,512]{1,0:T(8,128)S(1)} %pad_maximum_fusion), channel_id=1, source_target_pairs={{0,2},{1,3},{2,0},{3,1},{4,6},{5,7},{6,4},{7,5},{8,10},{9,11},{10,... | collective-permute-start | bytes 589832 | tf_op jit(solution)/shard_map/ppermute | solution.py:20
  14.4 2.7 %collective-permute-start.7 = (f32[8,2048]{1,0:T(8,128)S(1)}, f32[8,2048]{1,0:T(8,128)S(1)}, u32[]{:S(2)}, u32[]{:S(2)}) collective-permute-start(f32[8,2048]{1,0:T(8,128)S(1)} %get-tuple-element.29), channel_id=1, source_target_pairs={{0,16},{4,20},{8,24},{12,28},{16,0},{20,4},{24,8},{28,12},{1,17},{... | collective-permute-start | bytes 196616 | tf_op jit(solution)/shard_map/ppermute | solution.py:183
  17.1 1.3 %collective-permute-start.8 = (f32[8,2048]{1,0:T(8,128)S(1)}, f32[8,2048]{1,0:T(8,128)S(1)}, u32[]{:S(2)}, u32[]{:S(2)}) collective-permute-start(f32[8,2048]{1,0:T(8,128)S(1)} %get-tuple-element.30), channel_id=1, source_target_pairs={{0,20},{4,16},{8,28},{12,24},{16,4},{20,0},{24,12},{28,8},{1,21},{... | collective-permute-start | bytes 196616 | tf_op jit(solution)/shard_map/ppermute | solution.py:183
  18.4 3.6 %collective-permute-start.9 = (f32[8,2048]{1,0:T(8,128)S(1)}, f32[8,2048]{1,0:T(8,128)S(1)}, u32[]{:S(2)}, u32[]{:S(2)}) collective-permute-start(f32[8,2048]{1,0:T(8,128)S(1)} %get-tuple-element.31), channel_id=1, source_target_pairs={{0,24},{4,28},{8,16},{12,20},{16,8},{20,12},{24,0},{28,4},{1,25},{... | collective-permute-start | bytes 196616 | tf_op jit(solution)/shard_map/ppermute | solution.py:183
  22.0 0.0 collective-permute-done.3
  22.0 0.0 copy-start.7
  22.0 0.5 fusion.14
  22.5 0.5 fusion.5
  23.1 0.0 slice-start
  23.2 0.1 collective-permute-start.6
  23.3 2.0 %collective-permute-start.5 = (f32[16,2048]{1,0:T(8,128)S(1)}, f32[16,2048]{1,0:T(8,128)S(1)}, u32[]{:S(2)}, u32[]{:S(2)}) collective-permute-start(f32[16,2048]{1,0:T(8,128)S(1)} %pad_maximum_fusion.3), channel_id=1, source_target_pairs={{0,8},{4,12},{8,0},{12,4},{16,24},{20,28},{24,16},{28,20},{1,9},{5... | collective-permute-start | bytes 393224 | tf_op jit(solution)/shard_map/ppermute | solution.py:183
  25.3 0.0 copy-start.1
  25.3 0.0 copy-start.2
  25.3 0.0 collective-permute-done.7.refs_4_
  25.3 1.6 %collective-permute-start.4 = (f32[16,2048]{1,0:T(8,128)S(1)}, f32[16,2048]{1,0:T(8,128)S(1)}, u32[]{:S(2)}, u32[]{:S(2)}) collective-permute-start(f32[16,2048]{1,0:T(8,128)S(1)} %pad_maximum_fusion.2), channel_id=1, source_target_pairs={{0,4},{4,0},{8,12},{12,8},{16,20},{20,16},{24,28},{28,24},{1,5},{5... | collective-permute-start | bytes 393224 | tf_op jit(solution)/shard_map/ppermute | solution.py:183
  26.9 2.1 %convolution_convert_fusion = bf16[512,2048]{1,0:T(8,128)(2,1)} fusion(f32[64,2048]{1,0:T(8,128)S(1)} %copy-done.5, bf16[32,512]{1,0:T(8,128)(2,1)S(1)} %multiply_convert_fusion.1, bf16[32,512]{1,0:T(8,128)(2,1)S(1)} %slice-done, pred[]{:T(512)S(6)} %lt.96), kind=kOutput, calls=%fused_computation | convolution fusion | flops 135692288 | bytes 2686977 | tf_op jit(solution)/shard_map/dot_general | solution.py:228
  29.0 0.0 collective-permute-done.8.refs_5_
  29.0 1.8 %collective-permute-start.10 = (f32[8,2048]{1,0:T(8,128)S(1)}, f32[8,2048]{1,0:T(8,128)S(1)}, u32[]{:S(2)}, u32[]{:S(2)}) collective-permute-start(f32[8,2048]{1,0:T(8,128)S(1)} %get-tuple-element.32), channel_id=1, source_target_pairs={{0,28},{4,24},{8,20},{12,16},{16,12},{20,8},{24,4},{28,0},{1,29},{... | collective-permute-start | bytes 196616 | tf_op jit(solution)/shard_map/ppermute | solution.py:183
  30.8 0.0 collective-permute-done.9.refs_6_
  30.8 2.9 %collective-permute-start.14 = (f32[8,2048]{1,0:T(8,128)S(1)}, f32[8,2048]{1,0:T(8,128)S(1)}, u32[]{:S(2)}, u32[]{:S(2)}) collective-permute-start(f32[8,2048]{1,0:T(8,128)S(1)} %get-tuple-element.41), channel_id=1, source_target_pairs={{0,28},{4,24},{8,20},{12,16},{16,12},{20,8},{24,4},{28,0},{1,29},{... | collective-permute-start | bytes 196616 | tf_op jit(solution)/shard_map/ppermute | solution.py:183
  33.7 0.0 collective-permute-done.6.refs_3_
  33.7 0.9 %collective-permute-start.13 = (f32[8,2048]{1,0:T(8,128)S(1)}, f32[8,2048]{1,0:T(8,128)S(1)}, u32[]{:S(2)}, u32[]{:S(2)}) collective-permute-start(f32[8,2048]{1,0:T(8,128)S(1)} %get-tuple-element.42), channel_id=1, source_target_pairs={{0,24},{4,28},{8,16},{12,20},{16,8},{20,12},{24,0},{28,4},{1,25},{... | collective-permute-start | bytes 196616 | tf_op jit(solution)/shard_map/ppermute | solution.py:183
  34.6 0.0 collective-permute-done.5.refs_2_
  34.6 0.0 collective-permute-start.12
  34.6 0.0 collective-permute-done.4.refs_1_
  34.6 3.9 %collective-permute-start.11 = (f32[8,2048]{1,0:T(8,128)S(1)}, f32[8,2048]{1,0:T(8,128)S(1)}, u32[]{:S(2)}, u32[]{:S(2)}) collective-permute-start(f32[8,2048]{1,0:T(8,128)S(1)} %get-tuple-element.44), channel_id=1, source_target_pairs={{0,16},{4,20},{8,24},{12,28},{16,0},{20,4},{24,8},{28,12},{1,17},{... | collective-permute-start | bytes 196616 | tf_op jit(solution)/shard_map/ppermute | solution.py:183
  38.5 0.0 collective-permute-done.10.refs_7_
  38.5 0.2 gram_a.1.other_rows_ref
  38.7 0.0 collective-permute-done.14.refs_7_.refs_11_
  38.7 1.0 %collective-permute-done.13.refs_6_.refs_10_ = f32[8,2048]{1,0:T(8,128)S(1)} collective-permute-done((f32[8,2048]{1,0:T(8,128)S(1)}, f32[8,2048]{1,0:T(8,128)S(1)}, u32[]{:S(2)}, u32[]{:S(2)}) %collective-permute-start.13) | collective-permute-done | bytes 65568 | tf_op jit(solution)/shard_map/ppermute | solution.py:183
  39.8 2.8 %collective-permute-done.12.refs_5_.refs_9_ = f32[8,2048]{1,0:T(8,128)S(1)} collective-permute-done((f32[8,2048]{1,0:T(8,128)S(1)}, f32[8,2048]{1,0:T(8,128)S(1)}, u32[]{:S(2)}, u32[]{:S(2)}) %collective-permute-start.12) | collective-permute-done | bytes 65568 | tf_op jit(solution)/shard_map/ppermute | solution.py:183
  42.6 1.3 %collective-permute-done.11.refs_4_.refs_8_ = f32[8,2048]{1,0:T(8,128)S(1)} collective-permute-done((f32[8,2048]{1,0:T(8,128)S(1)}, f32[8,2048]{1,0:T(8,128)S(1)}, u32[]{:S(2)}, u32[]{:S(2)}) %collective-permute-start.11) | collective-permute-done | bytes 65568 | tf_op jit(solution)/shard_map/ppermute | solution.py:183
  43.9 0.7 %gram_b.1 = f32[32,1,128]{2,1,0:T(1,128)S(1)} custom-call(s32[1]{0:T(128)} %bitcast.me_ref, f32[64,128]{1,0:T(8,128)S(1)} %gram_a.1.other_rows_ref, f32[16,2048]{1,0:T(8,128)S(1)} %pad_maximum_fusion.1.refs_0_, f32[16,2048]{1,0:T(8,128)S(1)} %collective-permute-done.4.refs_1_, f32[16,2048]{1,0:T(8,128)S(1)} %collective-permute-done.5.refs_2_, ...), custom_call_target="tpu_custom_call" | custom-call | tf_op jit(solution)/shard_map/gram_b/pallas_call | solution.py:251
  44.6 10.1 %all_to_all.5.gathered_ref = f32[32,1,128]{2,1,0:T(1,128)S(1)} all-to-all(f32[32,1,128]{2,1,0:T(1,128)S(1)} %gram_b.1), channel_id=1, replica_groups=mesh['dp'=8,'tensor'=4] {'dp','tensor'}, dimensions={0} | all-to-all | bytes 32768 | tf_op jit(solution)/shard_map/all_to_all | solution.py:259
  54.7 2.0 %finish.1 = (f32[8,2048]{1,0:T(8,128)}, f32[8,2048]{1,0:T(8,128)}, f32[2,8,2048]{2,1,0:T(8,128)}, f32[2,8,2048]{2,1,0:T(8,128)}) custom-call(s32[1]{0:T(128)} %bitcast.me_ref, f32[32,1,128]{2,1,0:T(1,128)S(1)} %all_to_all.5.gathered_ref, f32[16,2048]{1,0:T(8,128)S(1)} %pad_maximum_fusion.1.refs_0_, f32[16,2048]{1,0:T(8,128)S(1)} %collective-permute-done.4.refs_1_, ...), custom_call_target="tpu_custom_call" | custom-call | tf_op jit(solution)/shard_map/finish/pallas_call | solution.py:263
  (27 shorter events, 0.4 us)
Async XLA Ops:
  0.6 1.6 %copy-start = (bf16[512,2048]{1,0:T(8,128)(2,1)S(1)}, bf16[512,2048]{1,0:T(8,128)(2,1)}, u32[]{:S(2)}) copy-start(bf16[512,2048]{1,0:T(8,128)(2,1)} %param.6) | copy-start | bytes 6291460
  0.6 3.9 %copy-start.6 = (f32[64,2048]{1,0:T(8,128)S(1)}, f32[64,2048]{1,0:T(8,128)}, u32[]{:S(2)}) copy-start(f32[64,2048]{1,0:T(8,128)} %param.9) | copy-start | bytes 1572868
  0.7 3.9 %copy-start.3 = (bf16[512,2048]{1,0:T(8,128)(2,1)S(1)}, bf16[512,2048]{1,0:T(8,128)(2,1)}, u32[]{:S(2)}) copy-start(bf16[512,2048]{1,0:T(8,128)(2,1)} %param.7) | copy-start | bytes 6291460
  4.0 1.5 %collective-permute-start = (f32[64,512]{1,0:T(8,128)S(1)}, f32[64,512]{1,0:T(8,128)S(1)}, u32[]{:S(2)}, u32[]{:S(2)}) collective-permute-start(f32[64,512]{1,0:T(8,128)S(1)} %fusion.3), channel_id=1, source_target_pairs={{0,1},{1,0},{2,3},{3,2},{4,5},{5,4},{6,7},{7,6},{8,9},{9,8},{10,11... | collective-permute-start | bytes 393224 | tf_op jit(solution)/shard_map/ppermute | solution.py:20
  5.3 1.4 %collective-permute-start.1 = (f32[64,512]{1,0:T(8,128)S(1)}, f32[64,512]{1,0:T(8,128)S(1)}, u32[]{:S(2)}, u32[]{:S(2)}) collective-permute-start(f32[64,512]{1,0:T(8,128)S(1)} %fusion), channel_id=1, source_target_pairs={{0,1},{1,0},{2,3},{3,2},{4,5},{5,4},{6,7},{7,6},{8,9},{9,8},{10,11... | collective-permute-start | bytes 393224 | tf_op jit(solution)/shard_map/ppermute | solution.py:20
  5.6 8.8 %copy-start.5 = (f32[64,2048]{1,0:T(8,128)S(1)}, f32[64,2048]{1,0:T(8,128)}, u32[]{:S(2)}) copy-start(f32[64,2048]{1,0:T(8,128)} %param.8) | copy-start | bytes 1572868
  6.8 5.3 %collective-permute-start.2 = (f32[32,512]{1,0:T(8,128)S(1)}, f32[32,512]{1,0:T(8,128)S(1)}, u32[]{:S(2)}, u32[]{:S(2)}) collective-permute-start(f32[32,512]{1,0:T(8,128)S(1)} %get-tuple-element.57), channel_id=1, source_target_pairs={{0,2},{1,3},{2,0},{3,1},{4,6},{5,7},{6,4},{7,5},{8,10},{9,11},{10,... | collective-permute-start | bytes 196616 | tf_op jit(solution)/shard_map/ppermute | solution.py:20
  12.6 9.9 %copy-start.4 = (bf16[512,2048]{1,0:T(8,128)(2,1)S(1)}, bf16[512,2048]{1,0:T(8,128)(2,1)}, u32[]{:S(2)}) copy-start(bf16[512,2048]{1,0:T(8,128)(2,1)} %param.7) | copy-start | bytes 6291460
  12.6 9.4 %collective-permute-start.3 = (f32[96,512]{1,0:T(8,128)S(1)}, f32[96,512]{1,0:T(8,128)S(1)}, u32[]{:S(2)}, u32[]{:S(2)}) collective-permute-start(f32[96,512]{1,0:T(8,128)S(1)} %pad_maximum_fusion), channel_id=1, source_target_pairs={{0,2},{1,3},{2,0},{3,1},{4,6},{5,7},{6,4},{7,5},{8,10},{9,11},{10,... | collective-permute-start | bytes 589832 | tf_op jit(solution)/shard_map/ppermute | solution.py:20
  14.4 10.9 %collective-permute-start.7 = (f32[8,2048]{1,0:T(8,128)S(1)}, f32[8,2048]{1,0:T(8,128)S(1)}, u32[]{:S(2)}, u32[]{:S(2)}) collective-permute-start(f32[8,2048]{1,0:T(8,128)S(1)} %get-tuple-element.29), channel_id=1, source_target_pairs={{0,16},{4,20},{8,24},{12,28},{16,0},{20,4},{24,8},{28,12},{1,17},{... | collective-permute-start | bytes 196616 | tf_op jit(solution)/shard_map/ppermute | solution.py:183
  17.1 11.9 %collective-permute-start.8 = (f32[8,2048]{1,0:T(8,128)S(1)}, f32[8,2048]{1,0:T(8,128)S(1)}, u32[]{:S(2)}, u32[]{:S(2)}) collective-permute-start(f32[8,2048]{1,0:T(8,128)S(1)} %get-tuple-element.30), channel_id=1, source_target_pairs={{0,20},{4,16},{8,28},{12,24},{16,4},{20,0},{24,12},{28,8},{1,21},{... | collective-permute-start | bytes 196616 | tf_op jit(solution)/shard_map/ppermute | solution.py:183
  18.4 12.5 %collective-permute-start.9 = (f32[8,2048]{1,0:T(8,128)S(1)}, f32[8,2048]{1,0:T(8,128)S(1)}, u32[]{:S(2)}, u32[]{:S(2)}) collective-permute-start(f32[8,2048]{1,0:T(8,128)S(1)} %get-tuple-element.31), channel_id=1, source_target_pairs={{0,24},{4,28},{8,16},{12,20},{16,8},{20,12},{24,0},{28,4},{1,25},{... | collective-permute-start | bytes 196616 | tf_op jit(solution)/shard_map/ppermute | solution.py:183
  22.0 1.0 %copy-start.7 = (bf16[96,512]{1,0:T(8,128)(2,1)}, bf16[96,512]{1,0:T(8,128)(2,1)S(1)}, u32[]{:S(2)}) copy-start(bf16[96,512]{1,0:T(8,128)(2,1)S(1)} %multiply_convert_fusion) | copy-start | bytes 294916
  23.1 3.9 %slice-start = ((bf16[96,512]{1,0:T(8,128)(2,1)}), bf16[32,512]{1,0:T(8,128)(2,1)S(1)}, s32[]{:S(2)}) async-start(bf16[96,512]{1,0:T(8,128)(2,1)} %copy-done.7), calls=%async_computation.1 | async-start | bytes 65536 | tf_op jit(solution)/shard_map/slice | solution.py:214
  23.2 10.5 %collective-permute-start.6 = (f32[16,2048]{1,0:T(8,128)S(1)}, f32[16,2048]{1,0:T(8,128)S(1)}, u32[]{:S(2)}, u32[]{:S(2)}) collective-permute-start(f32[16,2048]{1,0:T(8,128)S(1)} %pad_maximum_fusion.4), channel_id=1, source_target_pairs={{0,12},{4,8},{8,4},{12,0},{16,28},{20,24},{24,20},{28,16},{1,13},{... | collective-permute-start | bytes 393224 | tf_op jit(solution)/shard_map/ppermute | solution.py:183
  23.3 11.3 %collective-permute-start.5 = (f32[16,2048]{1,0:T(8,128)S(1)}, f32[16,2048]{1,0:T(8,128)S(1)}, u32[]{:S(2)}, u32[]{:S(2)}) collective-permute-start(f32[16,2048]{1,0:T(8,128)S(1)} %pad_maximum_fusion.3), channel_id=1, source_target_pairs={{0,8},{4,12},{8,0},{12,4},{16,24},{20,28},{24,16},{28,20},{1,9},{5... | collective-permute-start | bytes 393224 | tf_op jit(solution)/shard_map/ppermute | solution.py:183
  25.3 29.4 %copy-start.1 = (f32[2,8,2048]{2,1,0:T(8,128)S(1)}, f32[2,8,2048]{2,1,0:T(8,128)}, u32[]{:S(2)}) copy-start(f32[2,8,2048]{2,1,0:T(8,128)} %refs_12_.1) | copy-start | bytes 393220
  25.3 29.4 %copy-start.2 = (f32[2,8,2048]{2,1,0:T(8,128)S(1)}, f32[2,8,2048]{2,1,0:T(8,128)}, u32[]{:S(2)}) copy-start(f32[2,8,2048]{2,1,0:T(8,128)} %refs_13_.1) | copy-start | bytes 393220
  25.3 9.3 %collective-permute-start.4 = (f32[16,2048]{1,0:T(8,128)S(1)}, f32[16,2048]{1,0:T(8,128)S(1)}, u32[]{:S(2)}, u32[]{:S(2)}) collective-permute-start(f32[16,2048]{1,0:T(8,128)S(1)} %pad_maximum_fusion.2), channel_id=1, source_target_pairs={{0,4},{4,0},{8,12},{12,8},{16,20},{20,16},{24,28},{28,24},{1,5},{5... | collective-permute-start | bytes 393224 | tf_op jit(solution)/shard_map/ppermute | solution.py:183
  29.0 9.5 %collective-permute-start.10 = (f32[8,2048]{1,0:T(8,128)S(1)}, f32[8,2048]{1,0:T(8,128)S(1)}, u32[]{:S(2)}, u32[]{:S(2)}) collective-permute-start(f32[8,2048]{1,0:T(8,128)S(1)} %get-tuple-element.32), channel_id=1, source_target_pairs={{0,28},{4,24},{8,20},{12,16},{16,12},{20,8},{24,4},{28,0},{1,29},{... | collective-permute-start | bytes 196616 | tf_op jit(solution)/shard_map/ppermute | solution.py:183
  30.8 7.9 %collective-permute-start.14 = (f32[8,2048]{1,0:T(8,128)S(1)}, f32[8,2048]{1,0:T(8,128)S(1)}, u32[]{:S(2)}, u32[]{:S(2)}) collective-permute-start(f32[8,2048]{1,0:T(8,128)S(1)} %get-tuple-element.41), channel_id=1, source_target_pairs={{0,28},{4,24},{8,20},{12,16},{16,12},{20,8},{24,4},{28,0},{1,29},{... | collective-permute-start | bytes 196616 | tf_op jit(solution)/shard_map/ppermute | solution.py:183
  33.7 6.1 %collective-permute-start.13 = (f32[8,2048]{1,0:T(8,128)S(1)}, f32[8,2048]{1,0:T(8,128)S(1)}, u32[]{:S(2)}, u32[]{:S(2)}) collective-permute-start(f32[8,2048]{1,0:T(8,128)S(1)} %get-tuple-element.42), channel_id=1, source_target_pairs={{0,24},{4,28},{8,16},{12,20},{16,8},{20,12},{24,0},{28,4},{1,25},{... | collective-permute-start | bytes 196616 | tf_op jit(solution)/shard_map/ppermute | solution.py:183
  34.6 8.0 %collective-permute-start.12 = (f32[8,2048]{1,0:T(8,128)S(1)}, f32[8,2048]{1,0:T(8,128)S(1)}, u32[]{:S(2)}, u32[]{:S(2)}) collective-permute-start(f32[8,2048]{1,0:T(8,128)S(1)} %get-tuple-element.43), channel_id=1, source_target_pairs={{0,20},{4,16},{8,28},{12,24},{16,4},{20,0},{24,12},{28,8},{1,21},{... | collective-permute-start | bytes 196616 | tf_op jit(solution)/shard_map/ppermute | solution.py:183
  34.6 9.2 %collective-permute-start.11 = (f32[8,2048]{1,0:T(8,128)S(1)}, f32[8,2048]{1,0:T(8,128)S(1)}, u32[]{:S(2)}, u32[]{:S(2)}) collective-permute-start(f32[8,2048]{1,0:T(8,128)S(1)} %get-tuple-element.44), channel_id=1, source_target_pairs={{0,16},{4,20},{8,24},{12,28},{16,0},{20,4},{24,8},{28,12},{1,17},{... | collective-permute-start | bytes 196616 | tf_op jit(solution)/shard_map/ppermute | solution.py:183

commit v4 on v3

--- a/solution.py
+++ b/solution.py
@@ -198,6 +198,7 @@
 
     adapter_in = lowrank_down_factor.astype(jnp.bfloat16)
     adapter_out = lowrank_up_factor.astype(jnp.bfloat16)
+    adapter_in = lax.optimization_barrier(adapter_in)
     upstream = projected(cotangent, adapter_out)
     hidden = projected(tokens, adapter_in)
     upstream = upstream + other_of(upstream, "tensor", 1)

time: 56.8 us -> 55 us (0.968)
  starting transfers between devices: 25.9 us -> 24.9 us
  matrix products: 6.06 us -> 6.92 us
  local copies, waits for them, and re-layouts: 1.8 us -> 1.07 us
  waiting for transfers between devices: 8.84 us -> 8.13 us
    unnamed x16 -> x12, local copies, waits for them, and re-layouts: 1.61 us -> 0.04 us
    ppermute x4, waiting for transfers between devices: 3.69 us -> 2.36 us  [other_of(): return lax.ppermute(block, axis, route)]
    ppermute x11, starting transfers between devices: 20.7 us -> 19.5 us  [sent(): return lax.ppermute(block, 'dp', route)]
    dot_general x2, matrix products: 2.56 us -> 3.42 us  [projected(): lax.dot_general(factor, block, (((1,), (1,)), ((), ())), preferred_elemen...]
    dynamic_slice x1, local copies, waits for them, and re-layouts: 0.01 us -> 0.84 us  [body(): lax.dynamic_slice_in_dim(lowrank_up_factor, me * owned_rows, owned_rows, 0)]
    ppermute x11, waiting for transfers between devices: 5.15 us -> 5.77 us  [sent(): return lax.ppermute(block, 'dp', route)]
  transfers between devices with their start and end apart: 15 -> 15, of which waited for: 5 -> 4; matrix products, arithmetic and copies ran while one was open for 7% -> 9% of each run, Pallas kernels for 0% -> 0%
where the time goes in v4:
time: 55 us; the launch traced here: 54.8 us
  starting transfers between devices  24.9 us (45%)
  blocking collectives  9.77 us (18%)
  waiting for transfers between devices  8.13 us (15%)
  matrix products  6.92 us (13%)
  Pallas kernels  2.87 us (5%)
  local copies, waits for them, and re-layouts  1.07 us (2%)
  between operations  0.97 us (2%)
    ppermute x11, starting transfers between devices, sent(): return lax.ppermute(block, 'dp', route)  19.5 us
    all_to_all x1, blocking collectives, body(): gathered = lax.all_to_all(spread, ('dp', 'tensor'), 0, 0, tiled=True)  9.77 us
    ppermute x11, waiting for transfers between devices, sent(): return lax.ppermute(block, 'dp', route)  5.77 us
    ppermute x4, starting transfers between devices, other_of(): return lax.ppermute(block, axis, route)  5.42 us
    dot_general x2, matrix products, projected(): lax.dot_general(factor, block, (((1,), (1,)), ((), ())), preferred_elemen...  3.42 us
    ppermute x4, waiting for transfers between devices, other_of(): return lax.ppermute(block, axis, route)  2.36 us
    dot_general x1, matrix products, body(): lax.dot_general(upstream, adapter_in, (((0,), (0,)), ((), ())), preferred...  2.06 us
    pallas_call x1, Pallas kernels, body(): pl.pallas_call(functools.partial(finish_kernel, replicas=replicas), in_sp...  1.99 us
  transfers between devices with their start and end apart: 15, of which 4 were waited for; matrix products, arithmetic and copies ran while one was open for 9% of the time, Pallas kernels for 0%

profile of v4, /device:TPU:0, one launch (start us, length us, event | category | flops | bytes accessed | tf_op | source)
XLA Modules:
  0.0 54.8 jit_solution(5600758050684394988)
XLA Ops:
  0.6 0.0 copy-start
  0.6 0.0 copy-start.4
  0.7 2.7 %fusion = f32[64,512]{1,0:T(8,128)S(1)} fusion(bf16[512,2048]{1,0:T(8,128)(2,1)} %param.7, f32[64,2048]{1,0:T(8,128)} %param.9), kind=kOutput, calls=%fused_computation.1 | convolution fusion | flops 134348800 | bytes 2752512 | tf_op jit(solution)/shard_map/dot_general | solution.py:170
  3.3 0.5 collective-permute-start.1
  3.9 0.8 %fusion.14 = f32[64,512]{1,0:T(8,128)S(1)} fusion(bf16[64,2048]{1,0:T(8,128)(2,1)S(1)} %convert_element_type.15, bf16[512,2048]{1,0:T(8,128)(2,1)S(1)} %copy-done), kind=kOutput, calls=%fused_computation.45 | convolution fusion | flops 134217728 | bytes 2490368 | tf_op jit(solution)/shard_map/dot_general | solution.py:170
  4.6 0.1 collective-permute-start
  4.9 0.0 collective-permute-done.1
  4.9 2.9 %collective-permute-start.2 = (f32[32,512]{1,0:T(8,128)S(1)}, f32[32,512]{1,0:T(8,128)S(1)}, u32[]{:S(2)}, u32[]{:S(2)}) collective-permute-start(f32[32,512]{1,0:T(8,128)S(1)} %get-tuple-element.57), channel_id=1, source_target_pairs={{0,2},{1,3},{2,0},{3,1},{4,6},{5,7},{6,4},{7,5},{8,10},{9,11},{10,... | collective-permute-start | bytes 196616 | tf_op jit(solution)/shard_map/ppermute | solution.py:20
  7.8 0.0 collective-permute-done
  7.9 2.4 %collective-permute-done.2 = f32[32,512]{1,0:T(8,128)S(1)} collective-permute-done((f32[32,512]{1,0:T(8,128)S(1)}, f32[32,512]{1,0:T(8,128)S(1)}, u32[]{:S(2)}, u32[]{:S(2)}) %collective-permute-start.2) | collective-permute-done | bytes 65568 | tf_op jit(solution)/shard_map/ppermute | solution.py:20
  10.3 0.5 fusion.15
  10.8 1.9 %collective-permute-start.3 = (f32[96,512]{1,0:T(8,128)S(1)}, f32[96,512]{1,0:T(8,128)S(1)}, u32[]{:S(2)}, u32[]{:S(2)}) collective-permute-start(f32[96,512]{1,0:T(8,128)S(1)} %pad_maximum_fusion), channel_id=1, source_target_pairs={{0,2},{1,3},{2,0},{3,1},{4,6},{5,7},{6,4},{7,5},{8,10},{9,11},{10,... | collective-permute-start | bytes 589832 | tf_op jit(solution)/shard_map/ppermute | solution.py:20
  12.7 0.8 %constant_dynamic-slice_fusion.4.refs_15_ = f32[8,2048]{1,0:T(8,128)S(1)} fusion(f32[64,2048]{1,0:T(8,128)} %param.9, s32[]{:T(128)S(6)} %select_n.115), kind=kLoop, calls=%fused_computation.23 | loop fusion | bytes 131076 | tf_op jit(solution)/shard_map/dynamic_slice | solution.py:239
  13.5 2.6 %collective-permute-start.7 = (f32[8,2048]{1,0:T(8,128)S(1)}, f32[8,2048]{1,0:T(8,128)S(1)}, u32[]{:S(2)}, u32[]{:S(2)}) collective-permute-start(f32[8,2048]{1,0:T(8,128)S(1)} %get-tuple-element.29), channel_id=1, source_target_pairs={{0,16},{4,20},{8,24},{12,28},{16,0},{20,4},{24,8},{28,12},{1,17},{... | collective-permute-start | bytes 196616 | tf_op jit(solution)/shard_map/ppermute | solution.py:183
  16.1 1.3 %collective-permute-start.8 = (f32[8,2048]{1,0:T(8,128)S(1)}, f32[8,2048]{1,0:T(8,128)S(1)}, u32[]{:S(2)}, u32[]{:S(2)}) collective-permute-start(f32[8,2048]{1,0:T(8,128)S(1)} %get-tuple-element.30), channel_id=1, source_target_pairs={{0,20},{4,16},{8,28},{12,24},{16,4},{20,0},{24,12},{28,8},{1,21},{... | collective-permute-start | bytes 196616 | tf_op jit(solution)/shard_map/ppermute | solution.py:183
  17.4 3.6 %collective-permute-start.9 = (f32[8,2048]{1,0:T(8,128)S(1)}, f32[8,2048]{1,0:T(8,128)S(1)}, u32[]{:S(2)}, u32[]{:S(2)}) collective-permute-start(f32[8,2048]{1,0:T(8,128)S(1)} %get-tuple-element.31), channel_id=1, source_target_pairs={{0,24},{4,28},{8,16},{12,20},{16,8},{20,12},{24,0},{28,4},{1,25},{... | collective-permute-start | bytes 196616 | tf_op jit(solution)/shard_map/ppermute | solution.py:183
  21.0 0.0 collective-permute-done.3
  21.1 0.0 copy-start.5
  21.1 0.5 fusion.11
  21.5 0.0 copy-done.3
  21.5 0.5 fusion.2
  22.1 0.0 slice-start
  22.2 0.1 collective-permute-start.6
  22.3 2.0 %collective-permute-start.5 = (f32[16,2048]{1,0:T(8,128)S(1)}, f32[16,2048]{1,0:T(8,128)S(1)}, u32[]{:S(2)}, u32[]{:S(2)}) collective-permute-start(f32[16,2048]{1,0:T(8,128)S(1)} %pad_maximum_fusion.3), channel_id=1, source_target_pairs={{0,8},{4,12},{8,0},{12,4},{16,24},{20,28},{24,16},{28,20},{1,9},{5... | collective-permute-start | bytes 393224 | tf_op jit(solution)/shard_map/ppermute | solution.py:183
  24.4 0.0 copy-start.1
  24.4 0.0 copy-start.2
  24.4 0.0 collective-permute-done.7.refs_4_
  24.4 1.6 %collective-permute-start.4 = (f32[16,2048]{1,0:T(8,128)S(1)}, f32[16,2048]{1,0:T(8,128)S(1)}, u32[]{:S(2)}, u32[]{:S(2)}) collective-permute-start(f32[16,2048]{1,0:T(8,128)S(1)} %pad_maximum_fusion.2), channel_id=1, source_target_pairs={{0,4},{4,0},{8,12},{12,8},{16,20},{20,16},{24,28},{28,24},{1,5},{5... | collective-permute-start | bytes 393224 | tf_op jit(solution)/shard_map/ppermute | solution.py:183
  26.0 2.1 %convolution_convert_fusion = bf16[512,2048]{1,0:T(8,128)(2,1)} fusion(bf16[64,2048]{1,0:T(8,128)(2,1)S(1)} %convert_element_type.15, bf16[32,512]{1,0:T(8,128)(2,1)S(1)} %multiply_convert_fusion.1, bf16[32,512]{1,0:T(8,128)(2,1)S(1)} %slice-done, pred[]{:T(512)S(6)} %lt.96), kind=kOutput, calls=%fused_computation | convolution fusion | flops 135561216 | bytes 2424833 | tf_op jit(solution)/shard_map/dot_general | solution.py:229
  28.0 0.0 collective-permute-done.8.refs_5_
  28.0 0.7 %collective-permute-start.10 = (f32[8,2048]{1,0:T(8,128)S(1)}, f32[8,2048]{1,0:T(8,128)S(1)}, u32[]{:S(2)}, u32[]{:S(2)}) collective-permute-start(f32[8,2048]{1,0:T(8,128)S(1)} %get-tuple-element.32), channel_id=1, source_target_pairs={{0,28},{4,24},{8,20},{12,16},{16,12},{20,8},{24,4},{28,0},{1,29},{... | collective-permute-start | bytes 196616 | tf_op jit(solution)/shard_map/ppermute | solution.py:183
  28.7 0.0 collective-permute-done.9.refs_6_
  28.7 4.0 %collective-permute-start.14 = (f32[8,2048]{1,0:T(8,128)S(1)}, f32[8,2048]{1,0:T(8,128)S(1)}, u32[]{:S(2)}, u32[]{:S(2)}) collective-permute-start(f32[8,2048]{1,0:T(8,128)S(1)} %get-tuple-element.41), channel_id=1, source_target_pairs={{0,28},{4,24},{8,20},{12,16},{16,12},{20,8},{24,4},{28,0},{1,29},{... | collective-permute-start | bytes 196616 | tf_op jit(solution)/shard_map/ppermute | solution.py:183
  32.8 0.0 collective-permute-done.6.refs_3_
  32.8 0.7 %collective-permute-start.13 = (f32[8,2048]{1,0:T(8,128)S(1)}, f32[8,2048]{1,0:T(8,128)S(1)}, u32[]{:S(2)}, u32[]{:S(2)}) collective-permute-start(f32[8,2048]{1,0:T(8,128)S(1)} %get-tuple-element.42), channel_id=1, source_target_pairs={{0,24},{4,28},{8,16},{12,20},{16,8},{20,12},{24,0},{28,4},{1,25},{... | collective-permute-start | bytes 196616 | tf_op jit(solution)/shard_map/ppermute | solution.py:183
  33.5 0.0 collective-permute-done.5.refs_2_
  33.5 0.0 collective-permute-start.12
  33.5 0.0 collective-permute-done.4.refs_1_
  33.5 2.9 %collective-permute-start.11 = (f32[8,2048]{1,0:T(8,128)S(1)}, f32[8,2048]{1,0:T(8,128)S(1)}, u32[]{:S(2)}, u32[]{:S(2)}) collective-permute-start(f32[8,2048]{1,0:T(8,128)S(1)} %get-tuple-element.44), channel_id=1, source_target_pairs={{0,16},{4,20},{8,24},{12,28},{16,0},{20,4},{24,8},{28,12},{1,17},{... | collective-permute-start | bytes 196616 | tf_op jit(solution)/shard_map/ppermute | solution.py:183
  36.4 0.0 collective-permute-done.10.refs_7_
  36.4 0.2 gram_a.1.other_rows_ref
  36.6 0.0 collective-permute-done.14.refs_7_.refs_11_
  36.6 2.3 %collective-permute-done.13.refs_6_.refs_10_ = f32[8,2048]{1,0:T(8,128)S(1)} collective-permute-done((f32[8,2048]{1,0:T(8,128)S(1)}, f32[8,2048]{1,0:T(8,128)S(1)}, u32[]{:S(2)}, u32[]{:S(2)}) %collective-permute-start.13) | collective-permute-done | bytes 65568 | tf_op jit(solution)/shard_map/ppermute | solution.py:183
  38.9 2.4 %collective-permute-done.12.refs_5_.refs_9_ = f32[8,2048]{1,0:T(8,128)S(1)} collective-permute-done((f32[8,2048]{1,0:T(8,128)S(1)}, f32[8,2048]{1,0:T(8,128)S(1)}, u32[]{:S(2)}, u32[]{:S(2)}) %collective-permute-start.12) | collective-permute-done | bytes 65568 | tf_op jit(solution)/shard_map/ppermute | solution.py:183
  41.3 1.1 %collective-permute-done.11.refs_4_.refs_8_ = f32[8,2048]{1,0:T(8,128)S(1)} collective-permute-done((f32[8,2048]{1,0:T(8,128)S(1)}, f32[8,2048]{1,0:T(8,128)S(1)}, u32[]{:S(2)}, u32[]{:S(2)}) %collective-permute-start.11) | collective-permute-done | bytes 65568 | tf_op jit(solution)/shard_map/ppermute | solution.py:183
  42.4 0.7 %gram_b.1 = f32[32,1,128]{2,1,0:T(1,128)S(1)} custom-call(s32[1]{0:T(128)} %bitcast.me_ref, f32[64,128]{1,0:T(8,128)S(1)} %gram_a.1.other_rows_ref, f32[16,2048]{1,0:T(8,128)S(1)} %pad_maximum_fusion.1.refs_0_, f32[16,2048]{1,0:T(8,128)S(1)} %collective-permute-done.4.refs_1_, f32[16,2048]{1,0:T(8,128)S(1)} %collective-permute-done.5.refs_2_, ...), custom_call_target="tpu_custom_call" | custom-call | tf_op jit(solution)/shard_map/gram_b/pallas_call | solution.py:252
  43.1 9.8 %all_to_all.5.gathered_ref = f32[32,1,128]{2,1,0:T(1,128)S(1)} all-to-all(f32[32,1,128]{2,1,0:T(1,128)S(1)} %gram_b.1), channel_id=1, replica_groups=mesh['dp'=8,'tensor'=4] {'dp','tensor'}, dimensions={0} | all-to-all | bytes 32768 | tf_op jit(solution)/shard_map/all_to_all | solution.py:260
  52.8 2.0 %finish.1 = (f32[8,2048]{1,0:T(8,128)}, f32[8,2048]{1,0:T(8,128)}, f32[2,8,2048]{2,1,0:T(8,128)}, f32[2,8,2048]{2,1,0:T(8,128)}) custom-call(s32[1]{0:T(128)} %bitcast.me_ref, f32[32,1,128]{2,1,0:T(1,128)S(1)} %all_to_all.5.gathered_ref, f32[16,2048]{1,0:T(8,128)S(1)} %pad_maximum_fusion.1.refs_0_, f32[16,2048]{1,0:T(8,128)S(1)} %collective-permute-done.4.refs_1_, ...), custom_call_target="tpu_custom_call" | custom-call | tf_op jit(solution)/shard_map/finish/pallas_call | solution.py:264
  (24 shorter events, 0.4 us)
Async XLA Ops:
  0.6 3.2 %copy-start = (bf16[512,2048]{1,0:T(8,128)(2,1)S(1)}, bf16[512,2048]{1,0:T(8,128)(2,1)}, u32[]{:S(2)}) copy-start(bf16[512,2048]{1,0:T(8,128)(2,1)} %param.6) | copy-start | bytes 6291460
  0.6 3.2 %copy-start.4 = (f32[64,2048]{1,0:T(8,128)S(1)}, f32[64,2048]{1,0:T(8,128)}, u32[]{:S(2)}) copy-start(f32[64,2048]{1,0:T(8,128)} %param.8) | copy-start | bytes 1572868
  3.3 1.6 %collective-permute-start.1 = (f32[64,512]{1,0:T(8,128)S(1)}, f32[64,512]{1,0:T(8,128)S(1)}, u32[]{:S(2)}, u32[]{:S(2)}) collective-permute-start(f32[64,512]{1,0:T(8,128)S(1)} %fusion), channel_id=1, source_target_pairs={{0,1},{1,0},{2,3},{3,2},{4,5},{5,4},{6,7},{7,6},{8,9},{9,8},{10,11... | collective-permute-start | bytes 393224 | tf_op jit(solution)/shard_map/ppermute | solution.py:20
  4.6 3.2 %collective-permute-start = (f32[64,512]{1,0:T(8,128)S(1)}, f32[64,512]{1,0:T(8,128)S(1)}, u32[]{:S(2)}, u32[]{:S(2)}) collective-permute-start(f32[64,512]{1,0:T(8,128)S(1)} %fusion.14), channel_id=1, source_target_pairs={{0,1},{1,0},{2,3},{3,2},{4,5},{5,4},{6,7},{7,6},{8,9},{9,8},{10,11... | collective-permute-start | bytes 393224 | tf_op jit(solution)/shard_map/ppermute | solution.py:20
  4.9 5.3 %collective-permute-start.2 = (f32[32,512]{1,0:T(8,128)S(1)}, f32[32,512]{1,0:T(8,128)S(1)}, u32[]{:S(2)}, u32[]{:S(2)}) collective-permute-start(f32[32,512]{1,0:T(8,128)S(1)} %get-tuple-element.57), channel_id=1, source_target_pairs={{0,2},{1,3},{2,0},{3,1},{4,6},{5,7},{6,4},{7,5},{8,10},{9,11},{10,... | collective-permute-start | bytes 196616 | tf_op jit(solution)/shard_map/ppermute | solution.py:20
  10.8 10.8 %copy-start.3 = (bf16[512,2048]{1,0:T(8,128)(2,1)S(1)}, bf16[512,2048]{1,0:T(8,128)(2,1)}, u32[]{:S(2)}) copy-start(bf16[512,2048]{1,0:T(8,128)(2,1)} %param.7) | copy-start | bytes 6291460
  10.8 10.2 %collective-permute-start.3 = (f32[96,512]{1,0:T(8,128)S(1)}, f32[96,512]{1,0:T(8,128)S(1)}, u32[]{:S(2)}, u32[]{:S(2)}) collective-permute-start(f32[96,512]{1,0:T(8,128)S(1)} %pad_maximum_fusion), channel_id=1, source_target_pairs={{0,2},{1,3},{2,0},{3,1},{4,6},{5,7},{6,4},{7,5},{8,10},{9,11},{10,... | collective-permute-start | bytes 589832 | tf_op jit(solution)/shard_map/ppermute | solution.py:20
  13.5 10.8 %collective-permute-start.7 = (f32[8,2048]{1,0:T(8,128)S(1)}, f32[8,2048]{1,0:T(8,128)S(1)}, u32[]{:S(2)}, u32[]{:S(2)}) collective-permute-start(f32[8,2048]{1,0:T(8,128)S(1)} %get-tuple-element.29), channel_id=1, source_target_pairs={{0,16},{4,20},{8,24},{12,28},{16,0},{20,4},{24,8},{28,12},{1,17},{... | collective-permute-start | bytes 196616 | tf_op jit(solution)/shard_map/ppermute | solution.py:183
  16.1 11.9 %collective-permute-start.8 = (f32[8,2048]{1,0:T(8,128)S(1)}, f32[8,2048]{1,0:T(8,128)S(1)}, u32[]{:S(2)}, u32[]{:S(2)}) collective-permute-start(f32[8,2048]{1,0:T(8,128)S(1)} %get-tuple-element.30), channel_id=1, source_target_pairs={{0,20},{4,16},{8,28},{12,24},{16,4},{20,0},{24,12},{28,8},{1,21},{... | collective-permute-start | bytes 196616 | tf_op jit(solution)/shard_map/ppermute | solution.py:183
  17.4 11.3 %collective-permute-start.9 = (f32[8,2048]{1,0:T(8,128)S(1)}, f32[8,2048]{1,0:T(8,128)S(1)}, u32[]{:S(2)}, u32[]{:S(2)}) collective-permute-start(f32[8,2048]{1,0:T(8,128)S(1)} %get-tuple-element.31), channel_id=1, source_target_pairs={{0,24},{4,28},{8,16},{12,20},{16,8},{20,12},{24,0},{28,4},{1,25},{... | collective-permute-start | bytes 196616 | tf_op jit(solution)/shard_map/ppermute | solution.py:183
  21.1 1.0 %copy-start.5 = (bf16[96,512]{1,0:T(8,128)(2,1)}, bf16[96,512]{1,0:T(8,128)(2,1)S(1)}, u32[]{:S(2)}) copy-start(bf16[96,512]{1,0:T(8,128)(2,1)S(1)} %multiply_convert_fusion) | copy-start | bytes 294916
  22.1 3.9 %slice-start = ((bf16[96,512]{1,0:T(8,128)(2,1)}), bf16[32,512]{1,0:T(8,128)(2,1)S(1)}, s32[]{:S(2)}) async-start(bf16[96,512]{1,0:T(8,128)(2,1)} %copy-done.5), calls=%async_computation.1 | async-start | bytes 65536 | tf_op jit(solution)/shard_map/slice | solution.py:215
  22.2 10.5 %collective-permute-start.6 = (f32[16,2048]{1,0:T(8,128)S(1)}, f32[16,2048]{1,0:T(8,128)S(1)}, u32[]{:S(2)}, u32[]{:S(2)}) collective-permute-start(f32[16,2048]{1,0:T(8,128)S(1)} %pad_maximum_fusion.4), channel_id=1, source_target_pairs={{0,12},{4,8},{8,4},{12,0},{16,28},{20,24},{24,20},{28,16},{1,13},{... | collective-permute-start | bytes 393224 | tf_op jit(solution)/shard_map/ppermute | solution.py:183
  22.3 11.2 %collective-permute-start.5 = (f32[16,2048]{1,0:T(8,128)S(1)}, f32[16,2048]{1,0:T(8,128)S(1)}, u32[]{:S(2)}, u32[]{:S(2)}) collective-permute-start(f32[16,2048]{1,0:T(8,128)S(1)} %pad_maximum_fusion.3), channel_id=1, source_target_pairs={{0,8},{4,12},{8,0},{12,4},{16,24},{20,28},{24,16},{28,20},{1,9},{5... | collective-permute-start | bytes 393224 | tf_op jit(solution)/shard_map/ppermute | solution.py:183
  24.4 28.5 %copy-start.1 = (f32[2,8,2048]{2,1,0:T(8,128)S(1)}, f32[2,8,2048]{2,1,0:T(8,128)}, u32[]{:S(2)}) copy-start(f32[2,8,2048]{2,1,0:T(8,128)} %refs_12_.1) | copy-start | bytes 393220
  24.4 28.5 %copy-start.2 = (f32[2,8,2048]{2,1,0:T(8,128)S(1)}, f32[2,8,2048]{2,1,0:T(8,128)}, u32[]{:S(2)}) copy-start(f32[2,8,2048]{2,1,0:T(8,128)} %refs_13_.1) | copy-start | bytes 393220
  24.4 9.1 %collective-permute-start.4 = (f32[16,2048]{1,0:T(8,128)S(1)}, f32[16,2048]{1,0:T(8,128)S(1)}, u32[]{:S(2)}, u32[]{:S(2)}) collective-permute-start(f32[16,2048]{1,0:T(8,128)S(1)} %pad_maximum_fusion.2), channel_id=1, source_target_pairs={{0,4},{4,0},{8,12},{12,8},{16,20},{20,16},{24,28},{28,24},{1,5},{5... | collective-permute-start | bytes 393224 | tf_op jit(solution)/shard_map/ppermute | solution.py:183
  28.0 8.4 %collective-permute-start.10 = (f32[8,2048]{1,0:T(8,128)S(1)}, f32[8,2048]{1,0:T(8,128)S(1)}, u32[]{:S(2)}, u32[]{:S(2)}) collective-permute-start(f32[8,2048]{1,0:T(8,128)S(1)} %get-tuple-element.32), channel_id=1, source_target_pairs={{0,28},{4,24},{8,20},{12,16},{16,12},{20,8},{24,4},{28,0},{1,29},{... | collective-permute-start | bytes 196616 | tf_op jit(solution)/shard_map/ppermute | solution.py:183
  28.7 7.9 %collective-permute-start.14 = (f32[8,2048]{1,0:T(8,128)S(1)}, f32[8,2048]{1,0:T(8,128)S(1)}, u32[]{:S(2)}, u32[]{:S(2)}) collective-permute-start(f32[8,2048]{1,0:T(8,128)S(1)} %get-tuple-element.41), channel_id=1, source_target_pairs={{0,28},{4,24},{8,20},{12,16},{16,12},{20,8},{24,4},{28,0},{1,29},{... | collective-permute-start | bytes 196616 | tf_op jit(solution)/shard_map/ppermute | solution.py:183
  32.8 6.2 %collective-permute-start.13 = (f32[8,2048]{1,0:T(8,128)S(1)}, f32[8,2048]{1,0:T(8,128)S(1)}, u32[]{:S(2)}, u32[]{:S(2)}) collective-permute-start(f32[8,2048]{1,0:T(8,128)S(1)} %get-tuple-element.42), channel_id=1, source_target_pairs={{0,24},{4,28},{8,16},{12,20},{16,8},{20,12},{24,0},{28,4},{1,25},{... | collective-permute-start | bytes 196616 | tf_op jit(solution)/shard_map/ppermute | solution.py:183
  33.5 7.8 %collective-permute-start.12 = (f32[8,2048]{1,0:T(8,128)S(1)}, f32[8,2048]{1,0:T(8,128)S(1)}, u32[]{:S(2)}, u32[]{:S(2)}) collective-permute-start(f32[8,2048]{1,0:T(8,128)S(1)} %get-tuple-element.43), channel_id=1, source_target_pairs={{0,20},{4,16},{8,28},{12,24},{16,4},{20,0},{24,12},{28,8},{1,21},{... | collective-permute-start | bytes 196616 | tf_op jit(solution)/shard_map/ppermute | solution.py:183
  33.5 8.9 %collective-permute-start.11 = (f32[8,2048]{1,0:T(8,128)S(1)}, f32[8,2048]{1,0:T(8,128)S(1)}, u32[]{:S(2)}, u32[]{:S(2)}) collective-permute-start(f32[8,2048]{1,0:T(8,128)S(1)} %get-tuple-element.44), channel_id=1, source_target_pairs={{0,16},{4,20},{8,24},{12,28},{16,0},{20,4},{24,8},{28,12},{1,17},{... | collective-permute-start | bytes 196616 | tf_op jit(solution)/shard_map/ppermute | solution.py:183

commit v5 on v4

--- a/solution.py
+++ b/solution.py
@@ -29,23 +29,13 @@
     return block, other
 
 
-def exact_dot(left, right, dims):
-    return lax.dot_general(
-        left,
-        right,
-        (dims, ((), ())),
-        precision=lax.Precision.HIGHEST,
-        preferred_element_type=jnp.float32,
-    )
-
-
 def pieces_of(factor, refs, replicas, owned):
     near = refs[: replicas // 2]
     far = refs[replicas // 2 : replicas]
     return [ref.at[factor * owned : (factor + 1) * owned] for ref in near] + list(far)
 
 
-def inner_products(pieces, rows_ref, first):
+def inner_products(pieces, rows_ref, first, me):
     replicas = len(pieces)
     columns = pieces[0].shape[1]
     pairs = [(i, j) for i in range(replicas) for j in range(i, replicas)]
@@ -57,78 +47,89 @@
             sums[i, j] = sums[i, j] + product if start else product
     for i, j in pairs:
         row = jnp.sum(sums[i, j], axis=0, keepdims=True)
-        at = first + i * replicas + j
-        rows_ref[at : at + 1, :] = row
+        one, two = i ^ me, j ^ me
+        rows_ref[pl.ds(first + one * replicas + two, 1), :] = row
         if i != j:
-            at = first + j * replicas + i
-            rows_ref[at : at + 1, :] = row
-
-
-def relabelled(gram, me, replicas):
-    lanes = gram.shape[1]
+            rows_ref[pl.ds(first + two * replicas + one, 1), :] = row
+
+
+def tree_maps(maps_ref, me, replicas):
+    size = replicas * replicas
+    lanes = maps_ref.shape[1]
     source = lax.broadcasted_iota(jnp.int32, (lanes, lanes), 0)
     target = lax.broadcasted_iota(jnp.int32, (lanes, lanes), 1)
-    chosen = jnp.where(target == source ^ (me * replicas + me), 1.0, 0.0)
-    return exact_dot(gram, chosen.astype(jnp.float32), ((1,), (0,)))
-
-
-def first_gram_kernel(*refs):
-    replicas = len(refs) - 1
-    owned = refs[replicas - 1].shape[0]
-    inner_products(pieces_of(0, refs, replicas, owned), refs[-1], 0)
-
-
-def second_gram_kernel(me_ref, other_rows_ref, *refs):
-    replicas = len(refs) - 2
-    owned = refs[replicas - 1].shape[0]
-    spread_ref, rows_ref = refs[-2:]
-    size = replicas * replicas
-    rows_ref[:size, :] = other_rows_ref[...]
-    inner_products(pieces_of(1, refs, replicas, owned), rows_ref, size)
-    ones = jnp.ones((8, LANES), jnp.float32)
-    gram = exact_dot(ones, rows_ref[...], ((1,), (1,)))
-    gram = relabelled(gram, me_ref[0], replicas)
-    spread_ref[...] = jnp.broadcast_to(gram[:1, :][None], spread_ref.shape)
-
-
-def tree_weights(gram, replicas):
-    size = replicas * replicas
-    lanes = gram.shape[1]
-    source = lax.broadcasted_iota(jnp.int32, (lanes, lanes), 0)
-    target = lax.broadcasted_iota(jnp.int32, (lanes, lanes), 1)
-    same_factor = source // size == target // size
-    source_i = source % size // replicas
-    source_j = source % replicas
-    target_i = target % size // replicas
-    target_j = target % replicas
-
-    def gather(values, wanted):
-        chosen = jnp.where(same_factor & wanted, 1.0, 0.0).astype(jnp.float32)
-        return exact_dot(values, chosen, ((1,), (0,)))
-
+    for level in range(maps_ref.shape[0]):
+        at = source ^ (me * replicas + me) if level == 0 else source
+        same_factor = at // size == target // size
+        left, right = at % size // replicas >> level, at % replicas >> level
+        maps = []
+        for group in (target % size // replicas >> level, target % replicas >> level):
+            maps.append(same_factor & (left == group) & (right == group))
+            maps.append(same_factor & (left == group) & (right == (group ^ 1)))
+        maps.append(at == target)
+        for place, chosen in enumerate(maps):
+            maps_ref[level, :, place * lanes : (place + 1) * lanes] = jnp.where(
+                chosen, 1.0, 0.0
+            ).astype(maps_ref.dtype)
+
+
+def mapped(values, map_ref, count):
+    high = values.astype(jnp.bfloat16).astype(jnp.float32)
+    middle = (values - high).astype(jnp.bfloat16).astype(jnp.float32)
+    row = lax.broadcasted_iota(jnp.int32, values.shape, 0)
+    parts = jnp.where(row == 0, high, jnp.where(row == 1, middle, values - high - middle))
+    parts = jnp.where(row < 3, parts, 0.0).astype(jnp.bfloat16)
+    lanes = values.shape[1]
+    found = jnp.dot(
+        parts, map_ref[:, : count * lanes], preferred_element_type=jnp.float32
+    )
+    found = jnp.broadcast_to(jnp.sum(found, axis=0, keepdims=True), found.shape)
+    return [found[:, k * lanes : (k + 1) * lanes] for k in range(count)]
+
+
+def tree_weights(gram, maps_ref):
     weights = jnp.ones_like(gram)
-    level = 0
-    while 1 << level < replicas:
-        left, right = source_i >> level, source_j >> level
+    for level in range(maps_ref.shape[0]):
+        if level == 0:
+            *terms, gram = mapped(gram, maps_ref.at[level], 5)
+        else:
+            terms = mapped(gram, maps_ref.at[level], 4)
         kept = []
-        for target_at in (target_i >> level, target_j >> level):
-            norm = gather(gram, (left == target_at) & (right == target_at))
-            cross = gather(gram, (left == target_at) & (right == (target_at ^ 1)))
+        for norm, cross in (terms[:2], terms[2:]):
+            norm = jnp.maximum(norm, 0.0)
             kept.append(1.0 - cross / (2.0 * (norm + NORM_EPS)))
         gram = gram * kept[0] * kept[1]
         weights = weights * kept[0]
-        level += 1
     return weights
 
 
-def finish_kernel(me_ref, gathered_ref, *refs, replicas):
+def first_gram_kernel(me_ref, *refs):
+    *piece_refs, rows_ref, maps_ref = refs
+    replicas = len(piece_refs)
+    owned = piece_refs[-1].shape[0]
+    inner_products(pieces_of(0, piece_refs, replicas, owned), rows_ref, 0, me_ref[0])
+    tree_maps(maps_ref, me_ref[0], replicas)
+
+
+def second_gram_kernel(me_ref, other_rows_ref, *refs):
+    *piece_refs, spread_ref, rows_ref = refs
+    replicas = len(piece_refs)
+    owned = piece_refs[-1].shape[0]
+    size = replicas * replicas
+    rows_ref[:size, :] = other_rows_ref[...]
+    inner_products(pieces_of(1, piece_refs, replicas, owned), rows_ref, size, me_ref[0])
+    gram = jnp.sum(rows_ref[...].T, axis=0, keepdims=True)
+    spread_ref[...] = jnp.broadcast_to(gram[None], spread_ref.shape)
+
+
+def finish_kernel(gathered_ref, maps_ref, *refs, replicas):
     half = replicas // 2
     near, far_a, far_b = refs[:half], refs[half : 2 * half], refs[2 * half : 3 * half]
     first_ref, second_ref, down_ref, up_ref = refs[3 * half : 3 * half + 4]
     new_down_ref, new_up_ref, new_first_ref, new_second_ref = refs[3 * half + 4 :]
     gram = jnp.sum(gathered_ref[...], axis=0)
-    gram = jnp.broadcast_to(gram, (8, gram.shape[1]))
-    weights = tree_weights(relabelled(gram, me_ref[0], replicas), replicas)
+    gram = jnp.broadcast_to(gram, (16, gram.shape[1]))
+    weights = tree_weights(gram, maps_ref)
     factors = ((far_a, down_ref, new_down_ref), (far_b, up_ref, new_up_ref))
     for factor, (far, old_ref, new_ref) in enumerate(factors):
         owned = old_ref.shape[0]
@@ -159,6 +160,7 @@
     rank = lowrank_down_factor.shape[0]
     owned_rows = first_moment_estimate.shape[1]
     size = replicas * replicas
+    levels = replicas.bit_length() - 1
     me = lax.axis_index("dp")
     position = me.astype(jnp.int32).reshape(1)
     params = pltpu.CompilerParams(vmem_limit_bytes=VMEM_LIMIT)
@@ -243,12 +245,16 @@
         (near, input_grad, owned_down, owned_up)
     )
 
-    rows_a = pl.pallas_call(
+    rows_a, maps = pl.pallas_call(
         first_gram_kernel,
-        out_shape=shape(size, LANES),
+        in_specs=[IN_SMEM] + [IN_VMEM] * replicas,
+        out_shape=[
+            shape(size, LANES),
+            shape(levels, 2 * size, 10 * size, dtype=jnp.bfloat16),
+        ],
         compiler_params=params,
         name="gram_a",
-    )(*near, *far_a)
+    )(position, *near, *far_a)
     spread = pl.pallas_call(
         second_gram_kernel,
         in_specs=[IN_SMEM] + [IN_VMEM] * (1 + replicas),
@@ -263,13 +269,12 @@
     moment_out = shape(*first_moment_estimate.shape)
     updated_down_factor, updated_up_factor, moment_one, moment_two = pl.pallas_call(
         functools.partial(finish_kernel, replicas=replicas),
-        in_specs=[IN_SMEM] + [IN_VMEM] * (3 * half + 5),
         out_shape=(row_out, row_out, moment_out, moment_out),
         compiler_params=params,
         name="finish",
     )(
-        position,
         gathered,
+        maps,
         *near,
         *far_a,
         *far_b,

time: 55 us -> 54 us (0.982)
  Pallas kernels: 2.87 us -> 2.19 us
  transfers between devices with their start and end apart: 15 -> 15, of which waited for: 4 -> 4; matrix products, arithmetic and copies ran while one was open for 9% -> 9% of each run, Pallas kernels for 0% -> 1%
where the time goes in v5:
time: 54 us; the launch traced here: 53.8 us
  starting transfers between devices  24.9 us (46%)
  blocking collectives  9.76 us (18%)
  waiting for transfers between devices  7.82 us (14%)
  matrix products  6.89 us (13%)
  Pallas kernels  2.19 us (4%)
  local copies, waits for them, and re-layouts  1.07 us (2%)
  between operations  0.98 us (2%)
    ppermute x11, starting transfers between devices, sent(): return lax.ppermute(block, 'dp', route)  19.5 us
    all_to_all x1, blocking collectives, body(): gathered = lax.all_to_all(spread, ('dp', 'tensor'), 0, 0, tiled=True)  9.76 us
    ppermute x11, waiting for transfers between devices, sent(): return lax.ppermute(block, 'dp', route)  5.46 us
    ppermute x4, starting transfers between devices, other_of(): return lax.ppermute(block, axis, route)  5.42 us
    dot_general x2, matrix products, projected(): lax.dot_general(factor, block, (((1,), (1,)), ((), ())), preferred_elemen...  3.42 us
    ppermute x4, waiting for transfers between devices, other_of(): return lax.ppermute(block, axis, route)  2.36 us
    dot_general x1, matrix products, body(): lax.dot_general(upstream, adapter_in, (((0,), (0,)), ((), ())), preferred...  2.06 us
    dot_general x3, matrix products, gradient(): return jnp.dot(sums, block, preferred_element_type=jnp.float32)  1.41 us
  transfers between devices with their start and end apart: 15, of which 4 were waited for; matrix products, arithmetic and copies ran while one was open for 9% of the time, Pallas kernels for 1%

profile of v5, /device:TPU:0, one launch (start us, length us, event | category | flops | bytes accessed | tf_op | source)
XLA Modules:
  0.0 53.8 jit_solution(8459465493523824940)
XLA Ops:
  0.6 0.0 copy-start
  0.6 0.0 copy-start.4
  0.7 2.7 %fusion = f32[64,512]{1,0:T(8,128)S(1)} fusion(bf16[512,2048]{1,0:T(8,128)(2,1)} %param.7, f32[64,2048]{1,0:T(8,128)} %param.9), kind=kOutput, calls=%fused_computation.1 | convolution fusion | flops 134348800 | bytes 2752512 | tf_op jit(solution)/shard_map/dot_general | solution.py:172
  3.3 0.5 collective-permute-start.1
  3.9 0.8 %fusion.14 = f32[64,512]{1,0:T(8,128)S(1)} fusion(bf16[64,2048]{1,0:T(8,128)(2,1)S(1)} %convert_element_type.15, bf16[512,2048]{1,0:T(8,128)(2,1)S(1)} %copy-done), kind=kOutput, calls=%fused_computation.45 | convolution fusion | flops 134217728 | bytes 2490368 | tf_op jit(solution)/shard_map/dot_general | solution.py:172
  4.6 0.1 collective-permute-start
  4.9 0.0 collective-permute-done.1
  4.9 2.9 %collective-permute-start.2 = (f32[32,512]{1,0:T(8,128)S(1)}, f32[32,512]{1,0:T(8,128)S(1)}, u32[]{:S(2)}, u32[]{:S(2)}) collective-permute-start(f32[32,512]{1,0:T(8,128)S(1)} %get-tuple-element.61), channel_id=1, source_target_pairs={{0,2},{1,3},{2,0},{3,1},{4,6},{5,7},{6,4},{7,5},{8,10},{9,11},{10,... | collective-permute-start | bytes 196616 | tf_op jit(solution)/shard_map/ppermute | solution.py:20
  7.8 0.0 collective-permute-done
  7.9 2.4 %collective-permute-done.2 = f32[32,512]{1,0:T(8,128)S(1)} collective-permute-done((f32[32,512]{1,0:T(8,128)S(1)}, f32[32,512]{1,0:T(8,128)S(1)}, u32[]{:S(2)}, u32[]{:S(2)}) %collective-permute-start.2) | collective-permute-done | bytes 65568 | tf_op jit(solution)/shard_map/ppermute | solution.py:20
  10.3 0.5 fusion.15
  10.8 1.9 %collective-permute-start.3 = (f32[96,512]{1,0:T(8,128)S(1)}, f32[96,512]{1,0:T(8,128)S(1)}, u32[]{:S(2)}, u32[]{:S(2)}) collective-permute-start(f32[96,512]{1,0:T(8,128)S(1)} %pad_maximum_fusion), channel_id=1, source_target_pairs={{0,2},{1,3},{2,0},{3,1},{4,6},{5,7},{6,4},{7,5},{8,10},{9,11},{10,... | collective-permute-start | bytes 589832 | tf_op jit(solution)/shard_map/ppermute | solution.py:20
  12.7 0.8 %constant_dynamic-slice_fusion.4.refs_15_ = f32[8,2048]{1,0:T(8,128)S(1)} fusion(f32[64,2048]{1,0:T(8,128)} %param.9, s32[]{:T(128)S(6)} %select_n.115), kind=kLoop, calls=%fused_computation.23 | loop fusion | bytes 131076 | tf_op jit(solution)/shard_map/dynamic_slice | solution.py:241
  13.5 2.6 %collective-permute-start.7 = (f32[8,2048]{1,0:T(8,128)S(1)}, f32[8,2048]{1,0:T(8,128)S(1)}, u32[]{:S(2)}, u32[]{:S(2)}) collective-permute-start(f32[8,2048]{1,0:T(8,128)S(1)} %get-tuple-element.31), channel_id=1, source_target_pairs={{0,16},{4,20},{8,24},{12,28},{16,0},{20,4},{24,8},{28,12},{1,17},{... | collective-permute-start | bytes 196616 | tf_op jit(solution)/shard_map/ppermute | solution.py:185
  16.1 1.3 %collective-permute-start.8 = (f32[8,2048]{1,0:T(8,128)S(1)}, f32[8,2048]{1,0:T(8,128)S(1)}, u32[]{:S(2)}, u32[]{:S(2)}) collective-permute-start(f32[8,2048]{1,0:T(8,128)S(1)} %get-tuple-element.32), channel_id=1, source_target_pairs={{0,20},{4,16},{8,28},{12,24},{16,4},{20,0},{24,12},{28,8},{1,21},{... | collective-permute-start | bytes 196616 | tf_op jit(solution)/shard_map/ppermute | solution.py:185
  17.4 3.6 %collective-permute-start.9 = (f32[8,2048]{1,0:T(8,128)S(1)}, f32[8,2048]{1,0:T(8,128)S(1)}, u32[]{:S(2)}, u32[]{:S(2)}) collective-permute-start(f32[8,2048]{1,0:T(8,128)S(1)} %get-tuple-element.33), channel_id=1, source_target_pairs={{0,24},{4,28},{8,16},{12,20},{16,8},{20,12},{24,0},{28,4},{1,25},{... | collective-permute-start | bytes 196616 | tf_op jit(solution)/shard_map/ppermute | solution.py:185
  21.0 0.0 collective-permute-done.3
  21.0 0.0 copy-start.5
  21.1 0.5 fusion.11
  21.5 0.5 fusion.2
  22.1 0.0 slice-start
  22.2 0.1 collective-permute-start.6
  22.3 2.0 %collective-permute-start.5 = (f32[16,2048]{1,0:T(8,128)S(1)}, f32[16,2048]{1,0:T(8,128)S(1)}, u32[]{:S(2)}, u32[]{:S(2)}) collective-permute-start(f32[16,2048]{1,0:T(8,128)S(1)} %pad_maximum_fusion.3), channel_id=1, source_target_pairs={{0,8},{4,12},{8,0},{12,4},{16,24},{20,28},{24,16},{28,20},{1,9},{5... | collective-permute-start | bytes 393224 | tf_op jit(solution)/shard_map/ppermute | solution.py:185
  24.3 0.0 copy-start.1
  24.3 0.0 copy-start.2
  24.3 0.0 collective-permute-done.7.refs_4_
  24.4 1.6 %collective-permute-start.4 = (f32[16,2048]{1,0:T(8,128)S(1)}, f32[16,2048]{1,0:T(8,128)S(1)}, u32[]{:S(2)}, u32[]{:S(2)}) collective-permute-start(f32[16,2048]{1,0:T(8,128)S(1)} %pad_maximum_fusion.2), channel_id=1, source_target_pairs={{0,4},{4,0},{8,12},{12,8},{16,20},{20,16},{24,28},{28,24},{1,5},{5... | collective-permute-start | bytes 393224 | tf_op jit(solution)/shard_map/ppermute | solution.py:185
  25.9 0.0 slice-done
  25.9 2.1 %convolution_convert_fusion = bf16[512,2048]{1,0:T(8,128)(2,1)} fusion(bf16[64,2048]{1,0:T(8,128)(2,1)S(1)} %convert_element_type.15, bf16[32,512]{1,0:T(8,128)(2,1)S(1)} %multiply_convert_fusion.1, bf16[32,512]{1,0:T(8,128)(2,1)S(1)} %slice-done, pred[]{:T(512)S(6)} %lt.96), kind=kOutput, calls=%fused_computation | convolution fusion | flops 135561216 | bytes 2424833 | tf_op jit(solution)/shard_map/dot_general | solution.py:231
  28.0 0.0 collective-permute-done.8.refs_5_
  28.0 0.7 %collective-permute-start.10 = (f32[8,2048]{1,0:T(8,128)S(1)}, f32[8,2048]{1,0:T(8,128)S(1)}, u32[]{:S(2)}, u32[]{:S(2)}) collective-permute-start(f32[8,2048]{1,0:T(8,128)S(1)} %get-tuple-element.34), channel_id=1, source_target_pairs={{0,28},{4,24},{8,20},{12,16},{16,12},{20,8},{24,4},{28,0},{1,29},{... | collective-permute-start | bytes 196616 | tf_op jit(solution)/shard_map/ppermute | solution.py:185
  28.7 0.0 collective-permute-done.9.refs_6_
  28.7 4.0 %collective-permute-start.14 = (f32[8,2048]{1,0:T(8,128)S(1)}, f32[8,2048]{1,0:T(8,128)S(1)}, u32[]{:S(2)}, u32[]{:S(2)}) collective-permute-start(f32[8,2048]{1,0:T(8,128)S(1)} %get-tuple-element.45), channel_id=1, source_target_pairs={{0,28},{4,24},{8,20},{12,16},{16,12},{20,8},{24,4},{28,0},{1,29},{... | collective-permute-start | bytes 196616 | tf_op jit(solution)/shard_map/ppermute | solution.py:185
  32.7 0.0 collective-permute-done.6.refs_3_
  32.7 0.8 %collective-permute-start.13 = (f32[8,2048]{1,0:T(8,128)S(1)}, f32[8,2048]{1,0:T(8,128)S(1)}, u32[]{:S(2)}, u32[]{:S(2)}) collective-permute-start(f32[8,2048]{1,0:T(8,128)S(1)} %get-tuple-element.46), channel_id=1, source_target_pairs={{0,24},{4,28},{8,16},{12,20},{16,8},{20,12},{24,0},{28,4},{1,25},{... | collective-permute-start | bytes 196616 | tf_op jit(solution)/shard_map/ppermute | solution.py:185
  33.5 0.0 collective-permute-done.5.refs_2_
  33.5 0.0 collective-permute-start.12
  33.5 0.0 collective-permute-done.4.refs_1_
  33.5 2.9 %collective-permute-start.11 = (f32[8,2048]{1,0:T(8,128)S(1)}, f32[8,2048]{1,0:T(8,128)S(1)}, u32[]{:S(2)}, u32[]{:S(2)}) collective-permute-start(f32[8,2048]{1,0:T(8,128)S(1)} %get-tuple-element.48), channel_id=1, source_target_pairs={{0,16},{4,20},{8,24},{12,28},{16,0},{20,4},{24,8},{28,12},{1,17},{... | collective-permute-start | bytes 196616 | tf_op jit(solution)/shard_map/ppermute | solution.py:185
  36.4 0.0 collective-permute-done.10.refs_7_
  36.4 0.5 gram_a.1
  36.9 0.0 collective-permute-done.14.refs_7_.refs_11_
  36.9 2.0 %collective-permute-done.13.refs_6_.refs_10_ = f32[8,2048]{1,0:T(8,128)S(1)} collective-permute-done((f32[8,2048]{1,0:T(8,128)S(1)}, f32[8,2048]{1,0:T(8,128)S(1)}, u32[]{:S(2)}, u32[]{:S(2)}) %collective-permute-start.13) | collective-permute-done | bytes 65568 | tf_op jit(solution)/shard_map/ppermute | solution.py:185
  38.9 2.4 %collective-permute-done.12.refs_5_.refs_9_ = f32[8,2048]{1,0:T(8,128)S(1)} collective-permute-done((f32[8,2048]{1,0:T(8,128)S(1)}, f32[8,2048]{1,0:T(8,128)S(1)}, u32[]{:S(2)}, u32[]{:S(2)}) %collective-permute-start.12) | collective-permute-done | bytes 65568 | tf_op jit(solution)/shard_map/ppermute | solution.py:185
  41.3 1.0 %collective-permute-done.11.refs_4_.refs_8_ = f32[8,2048]{1,0:T(8,128)S(1)} collective-permute-done((f32[8,2048]{1,0:T(8,128)S(1)}, f32[8,2048]{1,0:T(8,128)S(1)}, u32[]{:S(2)}, u32[]{:S(2)}) %collective-permute-start.11) | collective-permute-done | bytes 65568 | tf_op jit(solution)/shard_map/ppermute | solution.py:185
  42.3 0.3 gram_b.1
  42.6 9.8 %all_to_all.5.gathered_ref = f32[32,1,128]{2,1,0:T(1,128)S(1)} all-to-all(f32[32,1,128]{2,1,0:T(1,128)S(1)} %gram_b.1), channel_id=1, replica_groups=mesh['dp'=8,'tensor'=4] {'dp','tensor'}, dimensions={0} | all-to-all | bytes 32768 | tf_op jit(solution)/shard_map/all_to_all | solution.py:266
  52.4 1.4 %finish.1 = (f32[8,2048]{1,0:T(8,128)}, f32[8,2048]{1,0:T(8,128)}, f32[2,8,2048]{2,1,0:T(8,128)}, f32[2,8,2048]{2,1,0:T(8,128)}) custom-call(f32[32,1,128]{2,1,0:T(1,128)S(1)} %all_to_all.5.gathered_ref, bf16[3,128,640]{2,1,0:T(8,128)(2,1)S(1)} %get-tuple-element.36.maps_ref, f32[16,2048]{1,0:T(8,128)S(1)} %pad_maximum_fusion.1.refs_0_, ...), custom_call_target="tpu_custom_call" | custom-call | tf_op jit(solution)/shard_map/finish/pallas_call | solution.py:270
  (24 shorter events, 0.4 us)
Async XLA Ops:
  0.6 3.2 %copy-start = (bf16[512,2048]{1,0:T(8,128)(2,1)S(1)}, bf16[512,2048]{1,0:T(8,128)(2,1)}, u32[]{:S(2)}) copy-start(bf16[512,2048]{1,0:T(8,128)(2,1)} %param.6) | copy-start | bytes 6291460
  0.6 3.2 %copy-start.4 = (f32[64,2048]{1,0:T(8,128)S(1)}, f32[64,2048]{1,0:T(8,128)}, u32[]{:S(2)}) copy-start(f32[64,2048]{1,0:T(8,128)} %param.8) | copy-start | bytes 1572868
  3.3 1.6 %collective-permute-start.1 = (f32[64,512]{1,0:T(8,128)S(1)}, f32[64,512]{1,0:T(8,128)S(1)}, u32[]{:S(2)}, u32[]{:S(2)}) collective-permute-start(f32[64,512]{1,0:T(8,128)S(1)} %fusion), channel_id=1, source_target_pairs={{0,1},{1,0},{2,3},{3,2},{4,5},{5,4},{6,7},{7,6},{8,9},{9,8},{10,11... | collective-permute-start | bytes 393224 | tf_op jit(solution)/shard_map/ppermute | solution.py:20
  4.6 3.2 %collective-permute-start = (f32[64,512]{1,0:T(8,128)S(1)}, f32[64,512]{1,0:T(8,128)S(1)}, u32[]{:S(2)}, u32[]{:S(2)}) collective-permute-start(f32[64,512]{1,0:T(8,128)S(1)} %fusion.14), channel_id=1, source_target_pairs={{0,1},{1,0},{2,3},{3,2},{4,5},{5,4},{6,7},{7,6},{8,9},{9,8},{10,11... | collective-permute-start | bytes 393224 | tf_op jit(solution)/shard_map/ppermute | solution.py:20
  4.9 5.3 %collective-permute-start.2 = (f32[32,512]{1,0:T(8,128)S(1)}, f32[32,512]{1,0:T(8,128)S(1)}, u32[]{:S(2)}, u32[]{:S(2)}) collective-permute-start(f32[32,512]{1,0:T(8,128)S(1)} %get-tuple-element.61), channel_id=1, source_target_pairs={{0,2},{1,3},{2,0},{3,1},{4,6},{5,7},{6,4},{7,5},{8,10},{9,11},{10,... | collective-permute-start | bytes 196616 | tf_op jit(solution)/shard_map/ppermute | solution.py:20
  10.7 10.8 %copy-start.3 = (bf16[512,2048]{1,0:T(8,128)(2,1)S(1)}, bf16[512,2048]{1,0:T(8,128)(2,1)}, u32[]{:S(2)}) copy-start(bf16[512,2048]{1,0:T(8,128)(2,1)} %param.7) | copy-start | bytes 6291460
  10.8 10.2 %collective-permute-start.3 = (f32[96,512]{1,0:T(8,128)S(1)}, f32[96,512]{1,0:T(8,128)S(1)}, u32[]{:S(2)}, u32[]{:S(2)}) collective-permute-start(f32[96,512]{1,0:T(8,128)S(1)} %pad_maximum_fusion), channel_id=1, source_target_pairs={{0,2},{1,3},{2,0},{3,1},{4,6},{5,7},{6,4},{7,5},{8,10},{9,11},{10,... | collective-permute-start | bytes 589832 | tf_op jit(solution)/shard_map/ppermute | solution.py:20
  13.5 10.8 %collective-permute-start.7 = (f32[8,2048]{1,0:T(8,128)S(1)}, f32[8,2048]{1,0:T(8,128)S(1)}, u32[]{:S(2)}, u32[]{:S(2)}) collective-permute-start(f32[8,2048]{1,0:T(8,128)S(1)} %get-tuple-element.31), channel_id=1, source_target_pairs={{0,16},{4,20},{8,24},{12,28},{16,0},{20,4},{24,8},{28,12},{1,17},{... | collective-permute-start | bytes 196616 | tf_op jit(solution)/shard_map/ppermute | solution.py:185
  16.1 11.9 %collective-permute-start.8 = (f32[8,2048]{1,0:T(8,128)S(1)}, f32[8,2048]{1,0:T(8,128)S(1)}, u32[]{:S(2)}, u32[]{:S(2)}) collective-permute-start(f32[8,2048]{1,0:T(8,128)S(1)} %get-tuple-element.32), channel_id=1, source_target_pairs={{0,20},{4,16},{8,28},{12,24},{16,4},{20,0},{24,12},{28,8},{1,21},{... | collective-permute-start | bytes 196616 | tf_op jit(solution)/shard_map/ppermute | solution.py:185
  17.4 11.3 %collective-permute-start.9 = (f32[8,2048]{1,0:T(8,128)S(1)}, f32[8,2048]{1,0:T(8,128)S(1)}, u32[]{:S(2)}, u32[]{:S(2)}) collective-permute-start(f32[8,2048]{1,0:T(8,128)S(1)} %get-tuple-element.33), channel_id=1, source_target_pairs={{0,24},{4,28},{8,16},{12,20},{16,8},{20,12},{24,0},{28,4},{1,25},{... | collective-permute-start | bytes 196616 | tf_op jit(solution)/shard_map/ppermute | solution.py:185
  21.0 1.0 %copy-start.5 = (bf16[96,512]{1,0:T(8,128)(2,1)}, bf16[96,512]{1,0:T(8,128)(2,1)S(1)}, u32[]{:S(2)}) copy-start(bf16[96,512]{1,0:T(8,128)(2,1)S(1)} %multiply_convert_fusion) | copy-start | bytes 294916
  22.1 3.9 %slice-start = ((bf16[96,512]{1,0:T(8,128)(2,1)}), bf16[32,512]{1,0:T(8,128)(2,1)S(1)}, s32[]{:S(2)}) async-start(bf16[96,512]{1,0:T(8,128)(2,1)} %copy-done.5), calls=%async_computation.1 | async-start | bytes 65536 | tf_op jit(solution)/shard_map/slice | solution.py:217
  22.2 10.5 %collective-permute-start.6 = (f32[16,2048]{1,0:T(8,128)S(1)}, f32[16,2048]{1,0:T(8,128)S(1)}, u32[]{:S(2)}, u32[]{:S(2)}) collective-permute-start(f32[16,2048]{1,0:T(8,128)S(1)} %pad_maximum_fusion.4), channel_id=1, source_target_pairs={{0,12},{4,8},{8,4},{12,0},{16,28},{20,24},{24,20},{28,16},{1,13},{... | collective-permute-start | bytes 393224 | tf_op jit(solution)/shard_map/ppermute | solution.py:185
  22.3 11.2 %collective-permute-start.5 = (f32[16,2048]{1,0:T(8,128)S(1)}, f32[16,2048]{1,0:T(8,128)S(1)}, u32[]{:S(2)}, u32[]{:S(2)}) collective-permute-start(f32[16,2048]{1,0:T(8,128)S(1)} %pad_maximum_fusion.3), channel_id=1, source_target_pairs={{0,8},{4,12},{8,0},{12,4},{16,24},{20,28},{24,16},{28,20},{1,9},{5... | collective-permute-start | bytes 393224 | tf_op jit(solution)/shard_map/ppermute | solution.py:185
  24.3 28.1 %copy-start.1 = (f32[2,8,2048]{2,1,0:T(8,128)S(1)}, f32[2,8,2048]{2,1,0:T(8,128)}, u32[]{:S(2)}) copy-start(f32[2,8,2048]{2,1,0:T(8,128)} %refs_12_.1) | copy-start | bytes 393220
  24.3 28.1 %copy-start.2 = (f32[2,8,2048]{2,1,0:T(8,128)S(1)}, f32[2,8,2048]{2,1,0:T(8,128)}, u32[]{:S(2)}) copy-start(f32[2,8,2048]{2,1,0:T(8,128)} %refs_13_.1) | copy-start | bytes 393220
  24.4 9.2 %collective-permute-start.4 = (f32[16,2048]{1,0:T(8,128)S(1)}, f32[16,2048]{1,0:T(8,128)S(1)}, u32[]{:S(2)}, u32[]{:S(2)}) collective-permute-start(f32[16,2048]{1,0:T(8,128)S(1)} %pad_maximum_fusion.2), channel_id=1, source_target_pairs={{0,4},{4,0},{8,12},{12,8},{16,20},{20,16},{24,28},{28,24},{1,5},{5... | collective-permute-start | bytes 393224 | tf_op jit(solution)/shard_map/ppermute | solution.py:185
  28.0 8.4 %collective-permute-start.10 = (f32[8,2048]{1,0:T(8,128)S(1)}, f32[8,2048]{1,0:T(8,128)S(1)}, u32[]{:S(2)}, u32[]{:S(2)}) collective-permute-start(f32[8,2048]{1,0:T(8,128)S(1)} %get-tuple-element.34), channel_id=1, source_target_pairs={{0,28},{4,24},{8,20},{12,16},{16,12},{20,8},{24,4},{28,0},{1,29},{... | collective-permute-start | bytes 196616 | tf_op jit(solution)/shard_map/ppermute | solution.py:185
  28.7 8.2 %collective-permute-start.14 = (f32[8,2048]{1,0:T(8,128)S(1)}, f32[8,2048]{1,0:T(8,128)S(1)}, u32[]{:S(2)}, u32[]{:S(2)}) collective-permute-start(f32[8,2048]{1,0:T(8,128)S(1)} %get-tuple-element.45), channel_id=1, source_target_pairs={{0,28},{4,24},{8,20},{12,16},{16,12},{20,8},{24,4},{28,0},{1,29},{... | collective-permute-start | bytes 196616 | tf_op jit(solution)/shard_map/ppermute | solution.py:185
  32.7 6.2 %collective-permute-start.13 = (f32[8,2048]{1,0:T(8,128)S(1)}, f32[8,2048]{1,0:T(8,128)S(1)}, u32[]{:S(2)}, u32[]{:S(2)}) collective-permute-start(f32[8,2048]{1,0:T(8,128)S(1)} %get-tuple-element.46), channel_id=1, source_target_pairs={{0,24},{4,28},{8,16},{12,20},{16,8},{20,12},{24,0},{28,4},{1,25},{... | collective-permute-start | bytes 196616 | tf_op jit(solution)/shard_map/ppermute | solution.py:185
  33.5 7.8 %collective-permute-start.12 = (f32[8,2048]{1,0:T(8,128)S(1)}, f32[8,2048]{1,0:T(8,128)S(1)}, u32[]{:S(2)}, u32[]{:S(2)}) collective-permute-start(f32[8,2048]{1,0:T(8,128)S(1)} %get-tuple-element.47), channel_id=1, source_target_pairs={{0,20},{4,16},{8,28},{12,24},{16,4},{20,0},{24,12},{28,8},{1,21},{... | collective-permute-start | bytes 196616 | tf_op jit(solution)/shard_map/ppermute | solution.py:185
  33.5 8.8 %collective-permute-start.11 = (f32[8,2048]{1,0:T(8,128)S(1)}, f32[8,2048]{1,0:T(8,128)S(1)}, u32[]{:S(2)}, u32[]{:S(2)}) collective-permute-start(f32[8,2048]{1,0:T(8,128)S(1)} %get-tuple-element.48), channel_id=1, source_target_pairs={{0,16},{4,20},{8,24},{12,28},{16,0},{20,4},{24,8},{28,12},{1,17},{... | collective-permute-start | bytes 196616 | tf_op jit(solution)/shard_map/ppermute | solution.py:185

commit v6 on v5

--- a/solution.py
+++ b/solution.py
@@ -12,6 +12,7 @@
 LANES = 128
 VMEM_LIMIT = 32 * 1024 * 1024
 IN_VMEM = pl.BlockSpec(memory_space=pltpu.VMEM)
+IN_HBM = pl.BlockSpec(memory_space=pltpu.HBM)
 IN_SMEM = pl.BlockSpec(memory_space=pltpu.SMEM)
 
 
@@ -103,12 +104,21 @@
     return weights
 
 
-def first_gram_kernel(me_ref, *refs):
-    *piece_refs, rows_ref, maps_ref = refs
+def first_gram_kernel(me_ref, down_ref, up_ref, *refs):
+    *piece_refs, rows_ref, maps_ref, own_down_ref, own_up_ref, sems = refs
     replicas = len(piece_refs)
     owned = piece_refs[-1].shape[0]
+    place = pl.ds(pl.multiple_of(me_ref[0] * owned, owned), owned)
+    copies = [
+        pltpu.make_async_copy(down_ref.at[place], own_down_ref, sems.at[0]),
+        pltpu.make_async_copy(up_ref.at[place], own_up_ref, sems.at[1]),
+    ]
+    for copy in copies:
+        copy.start()
     inner_products(pieces_of(0, piece_refs, replicas, owned), rows_ref, 0, me_ref[0])
     tree_maps(maps_ref, me_ref[0], replicas)
+    for copy in copies:
+        copy.wait()
 
 
 def second_gram_kernel(me_ref, other_rows_ref, *refs):
@@ -211,8 +221,8 @@
     rest = jnp.concatenate(
         [half_of(hidden, far_owner), half_of(hidden, me), half_of(upstream, me)]
     )
-    rest, upstream_far, far_a = lax.optimization_barrier((rest, upstream_far, far_a))
-    far_a = [sent(piece, half + k) for k, piece in enumerate(far_a)]
+    for k in range(half):
+        far_a[k] = sent(far_a[k], half + k)
     rest = rank_sums(butterfly_sum(rest, "tensor", 2))
     hidden, upstream_near = rest[:rank], rest[rank:]
     grad_b = gradient(hidden, cotangent)
@@ -220,8 +230,14 @@
     near_b = pieces_for(grad_b[rank // 2 :])
     near_a = pieces_for(gradient(upstream_near, tokens))
     near = [jnp.concatenate(pair) for pair in zip(near_a, near_b)]
-    far_b = [sent(piece, half + k) for k, piece in enumerate(far_b)]
+    far_a[0], far_b[1] = lax.optimization_barrier((far_a[0], far_b[1]))
+    far_a[1], far_b[2] = lax.optimization_barrier((far_a[1], far_b[2]))
+    far_a[2], far_b[3] = lax.optimization_barrier((far_a[2], far_b[3]))
+    for k in range(half):
+        far_b[k] = sent(far_b[k], half + k)
     near = near[:1] + [sent(piece, k) for k, piece in enumerate(near) if k]
+
+    far_b[0], upstream_near = lax.optimization_barrier((far_b[0], upstream_near))
 
     upstream = jnp.where(
         me < half,
@@ -235,26 +251,22 @@
         preferred_element_type=jnp.float32,
     )
     input_grad = input_grad.astype(jnp.bfloat16)
-    owned_down = lax.dynamic_slice_in_dim(
-        lowrank_down_factor, me * owned_rows, owned_rows, 0
-    )
-    owned_up = lax.dynamic_slice_in_dim(
-        lowrank_up_factor, me * owned_rows, owned_rows, 0
-    )
-    near, input_grad, owned_down, owned_up = lax.optimization_barrier(
-        (near, input_grad, owned_down, owned_up)
-    )
-
-    rows_a, maps = pl.pallas_call(
+    near, input_grad = lax.optimization_barrier((near, input_grad))
+
+    row_out = shape(owned_rows, columns)
+    rows_a, maps, owned_down, owned_up = pl.pallas_call(
         first_gram_kernel,
-        in_specs=[IN_SMEM] + [IN_VMEM] * replicas,
+        in_specs=[IN_SMEM] + [IN_HBM] * 2 + [IN_VMEM] * replicas,
         out_shape=[
             shape(size, LANES),
             shape(levels, 2 * size, 10 * size, dtype=jnp.bfloat16),
+            row_out,
+            row_out,
         ],
+        scratch_shapes=[pltpu.SemaphoreType.DMA((2,))],
         compiler_params=params,
         name="gram_a",
-    )(position, *near, *far_a)
+    )(position, lowrank_down_factor, lowrank_up_factor, *near, *far_a)
     spread = pl.pallas_call(
         second_gram_kernel,
         in_specs=[IN_SMEM] + [IN_VMEM] * (1 + replicas),
@@ -265,7 +277,6 @@
     )(position, rows_a, *near, *far_b)
     gathered = lax.all_to_all(spread, ("dp", "tensor"), 0, 0, tiled=True)
 
-    row_out = shape(owned_rows, columns)
     moment_out = shape(*first_moment_estimate.shape)
     updated_down_factor, updated_up_factor, moment_one, moment_two = pl.pallas_call(
         functools.partial(finish_kernel, replicas=replicas),

time: 54 us -> 52.8 us (0.978)
  blocking collectives: 9.76 us -> 11.7 us
  starting transfers between devices: 24.9 us -> 23.2 us
  local copies, waits for them, and re-layouts: 1.07 us -> 0.22 us
  waiting for transfers between devices: 7.82 us -> 7.18 us
    all_to_all x1, blocking collectives: 9.76 us -> 11.7 us  [body(): gathered = lax.all_to_all(spread, ('dp', 'tensor'), 0, 0, tiled=True)]
    ppermute x4, waiting for transfers between devices: 2.36 us -> 1.41 us  [other_of(): return lax.ppermute(block, axis, route)]
    ppermute x4, starting transfers between devices: 5.42 us -> 4.48 us  [other_of(): return lax.ppermute(block, axis, route)]
    dynamic_slice x2 -> x0, local copies, waits for them, and re-layouts: 0.85 us -> none  [the longest x1 0.84 us: body(): lax.dynamic_slice_in_dim(lowrank_up_factor, me * owned_rows, owned_rows, 0)]
    ppermute x11, starting transfers between devices: 19.5 us -> 18.7 us  [sent(): return lax.ppermute(block, 'dp', route)]
  transfers between devices with their start and end apart: 15 -> 15, of which waited for: 4 -> 5; matrix products, arithmetic and copies ran while one was open for 9% -> 9% of each run, Pallas kernels for 1% -> 1%
where the time goes in v6:
time: 52.8 us; the launch traced here: 52.7 us
  starting transfers between devices  23.2 us (44%)
  blocking collectives  11.7 us (22%)
  waiting for transfers between devices  7.18 us (14%)
  matrix products  6.9 us (13%)
  Pallas kernels  2.36 us (4%)
  between operations  0.94 us (2%)
    ppermute x11, starting transfers between devices, sent(): return lax.ppermute(block, 'dp', route)  18.7 us
    all_to_all x1, blocking collectives, body(): gathered = lax.all_to_all(spread, ('dp', 'tensor'), 0, 0, tiled=True)  11.7 us
    ppermute x11, waiting for transfers between devices, sent(): return lax.ppermute(block, 'dp', route)  5.77 us
    ppermute x4, starting transfers between devices, other_of(): return lax.ppermute(block, axis, route)  4.48 us
    dot_general x2, matrix products, projected(): lax.dot_general(factor, block, (((1,), (1,)), ((), ())), preferred_elemen...  3.42 us
    dot_general x1, matrix products, body(): lax.dot_general(upstream, adapter_in, (((0,), (0,)), ((), ())), preferred...  2.05 us
    dot_general x3, matrix products, gradient(): return jnp.dot(sums, block, preferred_element_type=jnp.float32)  1.42 us
    ppermute x4, waiting for transfers between devices, other_of(): return lax.ppermute(block, axis, route)  1.41 us
  transfers between devices with their start and end apart: 15, of which 5 were waited for; matrix products, arithmetic and copies ran while one was open for 9% of the time, Pallas kernels for 1%

profile of v6, /device:TPU:0, one launch (start us, length us, event | category | flops | bytes accessed | tf_op | source)
XLA Modules:
  0.0 52.7 jit_solution(10264191870922133965)
XLA Ops:
  0.6 0.0 copy-start
  0.6 0.0 copy-start.1
  0.7 2.7 %fusion = f32[64,512]{1,0:T(8,128)S(1)} fusion(bf16[512,2048]{1,0:T(8,128)(2,1)} %param.7, f32[64,2048]{1,0:T(8,128)} %up_ref.1), kind=kOutput, calls=%fused_computation.1 | convolution fusion | flops 134348800 | bytes 2752512 | tf_op jit(solution)/shard_map/dot_general | solution.py:182
  3.3 0.5 collective-permute-start.1
  3.8 0.0 copy-done.1
  3.9 0.0 copy-done
  3.9 0.8 %fusion.14 = f32[64,512]{1,0:T(8,128)S(1)} fusion(bf16[64,2048]{1,0:T(8,128)(2,1)S(1)} %convert_element_type.15, bf16[512,2048]{1,0:T(8,128)(2,1)S(1)} %copy-done), kind=kOutput, calls=%fused_computation.43 | convolution fusion | flops 134217728 | bytes 2490368 | tf_op jit(solution)/shard_map/dot_general | solution.py:182
  4.6 0.1 collective-permute-start
  4.9 0.0 collective-permute-done.1
  4.9 2.9 %collective-permute-start.7 = (f32[32,512]{1,0:T(8,128)S(1)}, f32[32,512]{1,0:T(8,128)S(1)}, u32[]{:S(2)}, u32[]{:S(2)}) collective-permute-start(f32[32,512]{1,0:T(8,128)S(1)} %get-tuple-element.65), channel_id=1, source_target_pairs={{0,2},{1,3},{2,0},{3,1},{4,6},{5,7},{6,4},{7,5},{8,10},{9,11},{10,... | collective-permute-start | bytes 196616 | tf_op jit(solution)/shard_map/ppermute | solution.py:21
  7.8 0.0 collective-permute-done
  7.9 0.9 %collective-permute-start.2 = (f32[96,512]{1,0:T(8,128)S(1)}, f32[96,512]{1,0:T(8,128)S(1)}, u32[]{:S(2)}, u32[]{:S(2)}) collective-permute-start(f32[96,512]{1,0:T(8,128)S(1)} %pad_maximum_fusion), channel_id=1, source_target_pairs={{0,2},{1,3},{2,0},{3,1},{4,6},{5,7},{6,4},{7,5},{8,10},{9,11},{10,... | collective-permute-start | bytes 589832 | tf_op jit(solution)/shard_map/ppermute | solution.py:21
  8.8 1.4 %collective-permute-done.7 = f32[32,512]{1,0:T(8,128)S(1)} collective-permute-done((f32[32,512]{1,0:T(8,128)S(1)}, f32[32,512]{1,0:T(8,128)S(1)}, u32[]{:S(2)}, u32[]{:S(2)}) %collective-permute-start.7) | collective-permute-done | bytes 65568 | tf_op jit(solution)/shard_map/ppermute | solution.py:21
  10.3 0.5 fusion.15
  10.8 4.2 %collective-permute-start.10 = (f32[8,2048]{1,0:T(8,128)S(1)}, f32[8,2048]{1,0:T(8,128)S(1)}, u32[]{:S(2)}, u32[]{:S(2)}) collective-permute-start(f32[8,2048]{1,0:T(8,128)S(1)} %get-tuple-element.50), channel_id=1, source_target_pairs={{0,24},{4,28},{8,16},{12,20},{16,8},{20,12},{24,0},{28,4},{1,25},{... | collective-permute-start | bytes 196616 | tf_op jit(solution)/shard_map/ppermute | solution.py:195
  15.0 0.4 collective-permute-start.9
  15.4 3.5 %collective-permute-start.8 = (f32[8,2048]{1,0:T(8,128)S(1)}, f32[8,2048]{1,0:T(8,128)S(1)}, u32[]{:S(2)}, u32[]{:S(2)}) collective-permute-start(f32[8,2048]{1,0:T(8,128)S(1)} %get-tuple-element.52), channel_id=1, source_target_pairs={{0,16},{4,20},{8,24},{12,28},{16,0},{20,4},{24,8},{28,12},{1,17},{... | collective-permute-start | bytes 196616 | tf_op jit(solution)/shard_map/ppermute | solution.py:195
  18.9 0.0 collective-permute-done.2
  18.9 0.5 fusion.11
  19.4 0.0 copy-done.5
  19.4 0.5 fusion.2
  20.0 0.0 copy-start.2
  20.0 0.1 collective-permute-start.6
  20.1 1.1 %collective-permute-start.5 = (f32[16,2048]{1,0:T(8,128)S(1)}, f32[16,2048]{1,0:T(8,128)S(1)}, u32[]{:S(2)}, u32[]{:S(2)}) collective-permute-start(f32[16,2048]{1,0:T(8,128)S(1)} %pad_maximum_fusion.4), channel_id=1, source_target_pairs={{0,12},{4,8},{8,4},{12,0},{16,28},{20,24},{24,20},{28,16},{1,13},{... | collective-permute-start | bytes 393224 | tf_op jit(solution)/shard_map/ppermute | solution.py:195
  21.2 3.1 %collective-permute-done.9.refs_5_ = f32[8,2048]{1,0:T(8,128)S(1)} collective-permute-done((f32[8,2048]{1,0:T(8,128)S(1)}, f32[8,2048]{1,0:T(8,128)S(1)}, u32[]{:S(2)}, u32[]{:S(2)}) %collective-permute-start.9) | collective-permute-done | bytes 65568 | tf_op jit(solution)/shard_map/ppermute | solution.py:195
  24.4 0.0 collective-permute-start.4
  24.4 1.1 %collective-permute-done.8.refs_4_ = f32[8,2048]{1,0:T(8,128)S(1)} collective-permute-done((f32[8,2048]{1,0:T(8,128)S(1)}, f32[8,2048]{1,0:T(8,128)S(1)}, u32[]{:S(2)}, u32[]{:S(2)}) %collective-permute-start.8) | collective-permute-done | bytes 65568 | tf_op jit(solution)/shard_map/ppermute | solution.py:195
  25.4 3.5 %collective-permute-start.11 = (f32[8,2048]{1,0:T(8,128)S(1)}, f32[8,2048]{1,0:T(8,128)S(1)}, u32[]{:S(2)}, u32[]{:S(2)}) collective-permute-start(f32[8,2048]{1,0:T(8,128)S(1)} %get-tuple-element.49), channel_id=1, source_target_pairs={{0,28},{4,24},{8,20},{12,16},{16,12},{20,8},{24,4},{28,0},{1,29},{... | collective-permute-start | bytes 196616 | tf_op jit(solution)/shard_map/ppermute | solution.py:195
  29.0 0.0 collective-permute-done.10.refs_6_
  29.0 0.0 collective-permute-start.12
  29.0 0.0 copy-start.4
  29.0 0.0 collective-permute-done.6.refs_4_.refs_8_
  29.0 3.2 %collective-permute-start.13 = (f32[8,2048]{1,0:T(8,128)S(1)}, f32[8,2048]{1,0:T(8,128)S(1)}, u32[]{:S(2)}, u32[]{:S(2)}) collective-permute-start(f32[8,2048]{1,0:T(8,128)S(1)} %get-tuple-element.38), channel_id=1, source_target_pairs={{0,24},{4,28},{8,16},{12,20},{16,8},{20,12},{24,0},{28,4},{1,25},{... | collective-permute-start | bytes 196616 | tf_op jit(solution)/shard_map/ppermute | solution.py:195
  32.2 0.0 collective-permute-done.5.refs_3_
  32.2 1.1 %collective-permute-start.14 = (f32[8,2048]{1,0:T(8,128)S(1)}, f32[8,2048]{1,0:T(8,128)S(1)}, u32[]{:S(2)}, u32[]{:S(2)}) collective-permute-start(f32[8,2048]{1,0:T(8,128)S(1)} %get-tuple-element.39), channel_id=1, source_target_pairs={{0,28},{4,24},{8,20},{12,16},{16,12},{20,8},{24,4},{28,0},{1,29},{... | collective-permute-start | bytes 196616 | tf_op jit(solution)/shard_map/ppermute | solution.py:195
  33.3 0.0 collective-permute-done.4.refs_2_
  33.3 1.6 %collective-permute-start.3 = (f32[16,2048]{1,0:T(8,128)S(1)}, f32[16,2048]{1,0:T(8,128)S(1)}, u32[]{:S(2)}, u32[]{:S(2)}) collective-permute-start(f32[16,2048]{1,0:T(8,128)S(1)} %pad_maximum_fusion.2), channel_id=1, source_target_pairs={{0,4},{4,0},{8,12},{12,8},{16,20},{20,16},{24,28},{28,24},{1,5},{5... | collective-permute-start | bytes 393224 | tf_op jit(solution)/shard_map/ppermute | solution.py:195
  34.9 2.1 %convolution_convert_fusion = bf16[512,2048]{1,0:T(8,128)(2,1)} fusion(bf16[64,2048]{1,0:T(8,128)(2,1)S(1)} %convert_element_type.15, bf16[32,512]{1,0:T(8,128)(2,1)S(1)} %multiply_convert_fusion.1, bf16[32,512]{1,0:T(8,128)(2,1)S(1)} %slice.16, pred[]{:T(512)S(6)} %lt.92), kind=kOutput, calls=%fused_computation | convolution fusion | flops 135561216 | bytes 2424833 | tf_op jit(solution)/shard_map/dot_general | solution.py:247
  36.9 1.3 %collective-permute-done.3.refs_1_ = f32[16,2048]{1,0:T(8,128)S(1)} collective-permute-done((f32[16,2048]{1,0:T(8,128)S(1)}, f32[16,2048]{1,0:T(8,128)S(1)}, u32[]{:S(2)}, u32[]{:S(2)}) %collective-permute-start.3) | collective-permute-done | bytes 131104 | tf_op jit(solution)/shard_map/ppermute | solution.py:195
  38.3 0.0 collective-permute-done.11.refs_7_
  38.3 0.0 copy-done.2
  38.3 0.7 %gram_a.1 = (f32[64,128]{1,0:T(8,128)S(1)}, bf16[3,128,640]{2,1,0:T(8,128)(2,1)S(1)}, f32[8,2048]{1,0:T(8,128)S(1)}, f32[8,2048]{1,0:T(8,128)S(1)}) custom-call(s32[1]{0:T(128)} %bitcast.me_ref, f32[64,2048]{1,0:T(8,128)S(1)} %copy-done.1, f32[64,2048]{1,0:T(8,128)S(1)} %copy-done.2, f32[16,2048]{1,0:T(8,128)S(1)} %pad_maximum_fusion.1.refs_0_, ...), custom_call_target="tpu_custom_call" | custom-call | tf_op jit(solution)/shard_map/gram_a/pallas_call | solution.py:257
  38.9 0.0 collective-permute-done.12.refs_5_.refs_9_
  39.0 0.0 collective-permute-done.13.refs_6_.refs_10_
  39.0 0.3 collective-permute-done.14.refs_7_.refs_11_
  39.2 0.3 gram_b.1
  39.5 11.7 %all_to_all.5.gathered_ref = f32[32,1,128]{2,1,0:T(1,128)S(1)} all-to-all(f32[32,1,128]{2,1,0:T(1,128)S(1)} %gram_b.1), channel_id=1, replica_groups=mesh['dp'=8,'tensor'=4] {'dp','tensor'}, dimensions={0} | all-to-all | bytes 32768 | tf_op jit(solution)/shard_map/all_to_all | solution.py:278
  51.3 1.4 %finish.1 = (f32[8,2048]{1,0:T(8,128)}, f32[8,2048]{1,0:T(8,128)}, f32[2,8,2048]{2,1,0:T(8,128)}, f32[2,8,2048]{2,1,0:T(8,128)}) custom-call(f32[32,1,128]{2,1,0:T(1,128)S(1)} %all_to_all.5.gathered_ref, bf16[3,128,640]{2,1,0:T(8,128)(2,1)S(1)} %get-tuple-element.40.maps_ref, f32[16,2048]{1,0:T(8,128)S(1)} %pad_maximum_fusion.1.refs_0_, ...), custom_call_target="tpu_custom_call" | custom-call | tf_op jit(solution)/shard_map/finish/pallas_call | solution.py:281
  (21 shorter events, 0.4 us)
Async XLA Ops:
  0.6 3.2 %copy-start = (bf16[512,2048]{1,0:T(8,128)(2,1)S(1)}, bf16[512,2048]{1,0:T(8,128)(2,1)}, u32[]{:S(2)}) copy-start(bf16[512,2048]{1,0:T(8,128)(2,1)} %param.6) | copy-start | bytes 6291460
  0.6 3.2 %copy-start.1 = (f32[64,2048]{1,0:T(8,128)S(1)}, f32[64,2048]{1,0:T(8,128)}, u32[]{:S(2)}) copy-start(f32[64,2048]{1,0:T(8,128)} %down_ref.1) | copy-start | bytes 1572868
  3.3 1.5 %collective-permute-start.1 = (f32[64,512]{1,0:T(8,128)S(1)}, f32[64,512]{1,0:T(8,128)S(1)}, u32[]{:S(2)}, u32[]{:S(2)}) collective-permute-start(f32[64,512]{1,0:T(8,128)S(1)} %fusion), channel_id=1, source_target_pairs={{0,1},{1,0},{2,3},{3,2},{4,5},{5,4},{6,7},{7,6},{8,9},{9,8},{10,11... | collective-permute-start | bytes 393224 | tf_op jit(solution)/shard_map/ppermute | solution.py:21
  4.6 3.2 %collective-permute-start = (f32[64,512]{1,0:T(8,128)S(1)}, f32[64,512]{1,0:T(8,128)S(1)}, u32[]{:S(2)}, u32[]{:S(2)}) collective-permute-start(f32[64,512]{1,0:T(8,128)S(1)} %fusion.14), channel_id=1, source_target_pairs={{0,1},{1,0},{2,3},{3,2},{4,5},{5,4},{6,7},{7,6},{8,9},{9,8},{10,11... | collective-permute-start | bytes 393224 | tf_op jit(solution)/shard_map/ppermute | solution.py:21
  4.9 5.3 %collective-permute-start.7 = (f32[32,512]{1,0:T(8,128)S(1)}, f32[32,512]{1,0:T(8,128)S(1)}, u32[]{:S(2)}, u32[]{:S(2)}) collective-permute-start(f32[32,512]{1,0:T(8,128)S(1)} %get-tuple-element.65), channel_id=1, source_target_pairs={{0,2},{1,3},{2,0},{3,1},{4,6},{5,7},{6,4},{7,5},{8,10},{9,11},{10,... | collective-permute-start | bytes 196616 | tf_op jit(solution)/shard_map/ppermute | solution.py:21
  7.9 11.0 %collective-permute-start.2 = (f32[96,512]{1,0:T(8,128)S(1)}, f32[96,512]{1,0:T(8,128)S(1)}, u32[]{:S(2)}, u32[]{:S(2)}) collective-permute-start(f32[96,512]{1,0:T(8,128)S(1)} %pad_maximum_fusion), channel_id=1, source_target_pairs={{0,2},{1,3},{2,0},{3,1},{4,6},{5,7},{6,4},{7,5},{8,10},{9,11},{10,... | collective-permute-start | bytes 589832 | tf_op jit(solution)/shard_map/ppermute | solution.py:21
  10.7 8.7 %copy-start.5 = (bf16[512,2048]{1,0:T(8,128)(2,1)S(1)}, bf16[512,2048]{1,0:T(8,128)(2,1)}, u32[]{:S(2)}) copy-start(bf16[512,2048]{1,0:T(8,128)(2,1)} %param.7) | copy-start | bytes 6291460
  10.8 18.2 %collective-permute-start.10 = (f32[8,2048]{1,0:T(8,128)S(1)}, f32[8,2048]{1,0:T(8,128)S(1)}, u32[]{:S(2)}, u32[]{:S(2)}) collective-permute-start(f32[8,2048]{1,0:T(8,128)S(1)} %get-tuple-element.50), channel_id=1, source_target_pairs={{0,24},{4,28},{8,16},{12,20},{16,8},{20,12},{24,0},{28,4},{1,25},{... | collective-permute-start | bytes 196616 | tf_op jit(solution)/shard_map/ppermute | solution.py:195
  15.0 9.4 %collective-permute-start.9 = (f32[8,2048]{1,0:T(8,128)S(1)}, f32[8,2048]{1,0:T(8,128)S(1)}, u32[]{:S(2)}, u32[]{:S(2)}) collective-permute-start(f32[8,2048]{1,0:T(8,128)S(1)} %get-tuple-element.51), channel_id=1, source_target_pairs={{0,20},{4,16},{8,28},{12,24},{16,4},{20,0},{24,12},{28,8},{1,21},{... | collective-permute-start | bytes 196616 | tf_op jit(solution)/shard_map/ppermute | solution.py:195
  15.4 10.1 %collective-permute-start.8 = (f32[8,2048]{1,0:T(8,128)S(1)}, f32[8,2048]{1,0:T(8,128)S(1)}, u32[]{:S(2)}, u32[]{:S(2)}) collective-permute-start(f32[8,2048]{1,0:T(8,128)S(1)} %get-tuple-element.52), channel_id=1, source_target_pairs={{0,16},{4,20},{8,24},{12,28},{16,0},{20,4},{24,8},{28,12},{1,17},{... | collective-permute-start | bytes 196616 | tf_op jit(solution)/shard_map/ppermute | solution.py:195
  20.0 18.3 %copy-start.2 = (f32[64,2048]{1,0:T(8,128)S(1)}, f32[64,2048]{1,0:T(8,128)}, u32[]{:S(2)}) copy-start(f32[64,2048]{1,0:T(8,128)} %up_ref.1) | copy-start | bytes 1572868
  20.0 9.0 %collective-permute-start.6 = (f32[8,2048]{1,0:T(8,128)S(1)}, f32[8,2048]{1,0:T(8,128)S(1)}, u32[]{:S(2)}, u32[]{:S(2)}) collective-permute-start(f32[8,2048]{1,0:T(8,128)S(1)} %get-tuple-element.56), channel_id=1, source_target_pairs={{0,16},{4,20},{8,24},{12,28},{16,0},{20,4},{24,8},{28,12},{1,17},{... | collective-permute-start | bytes 196616 | tf_op jit(solution)/shard_map/ppermute | solution.py:195
  20.1 12.0 %collective-permute-start.5 = (f32[16,2048]{1,0:T(8,128)S(1)}, f32[16,2048]{1,0:T(8,128)S(1)}, u32[]{:S(2)}, u32[]{:S(2)}) collective-permute-start(f32[16,2048]{1,0:T(8,128)S(1)} %pad_maximum_fusion.4), channel_id=1, source_target_pairs={{0,12},{4,8},{8,4},{12,0},{16,28},{20,24},{24,20},{28,16},{1,13},{... | collective-permute-start | bytes 393224 | tf_op jit(solution)/shard_map/ppermute | solution.py:195
  24.4 8.9 %collective-permute-start.4 = (f32[16,2048]{1,0:T(8,128)S(1)}, f32[16,2048]{1,0:T(8,128)S(1)}, u32[]{:S(2)}, u32[]{:S(2)}) collective-permute-start(f32[16,2048]{1,0:T(8,128)S(1)} %pad_maximum_fusion.3), channel_id=1, source_target_pairs={{0,8},{4,12},{8,0},{12,4},{16,24},{20,28},{24,16},{28,20},{1,9},{5... | collective-permute-start | bytes 393224 | tf_op jit(solution)/shard_map/ppermute | solution.py:195
  25.4 12.8 %collective-permute-start.11 = (f32[8,2048]{1,0:T(8,128)S(1)}, f32[8,2048]{1,0:T(8,128)S(1)}, u32[]{:S(2)}, u32[]{:S(2)}) collective-permute-start(f32[8,2048]{1,0:T(8,128)S(1)} %get-tuple-element.49), channel_id=1, source_target_pairs={{0,28},{4,24},{8,20},{12,16},{16,12},{20,8},{24,4},{28,0},{1,29},{... | collective-permute-start | bytes 196616 | tf_op jit(solution)/shard_map/ppermute | solution.py:195
  29.0 10.0 %collective-permute-start.12 = (f32[8,2048]{1,0:T(8,128)S(1)}, f32[8,2048]{1,0:T(8,128)S(1)}, u32[]{:S(2)}, u32[]{:S(2)}) collective-permute-start(f32[8,2048]{1,0:T(8,128)S(1)} %get-tuple-element.37), channel_id=1, source_target_pairs={{0,20},{4,16},{8,28},{12,24},{16,4},{20,0},{24,12},{28,8},{1,21},{... | collective-permute-start | bytes 196616 | tf_op jit(solution)/shard_map/ppermute | solution.py:195
  29.0 22.3 %copy-start.3 = (f32[2,8,2048]{2,1,0:T(8,128)S(1)}, f32[2,8,2048]{2,1,0:T(8,128)}, u32[]{:S(2)}) copy-start(f32[2,8,2048]{2,1,0:T(8,128)} %refs_12_.1) | copy-start | bytes 393220
  29.0 22.3 %copy-start.4 = (f32[2,8,2048]{2,1,0:T(8,128)S(1)}, f32[2,8,2048]{2,1,0:T(8,128)}, u32[]{:S(2)}) copy-start(f32[2,8,2048]{2,1,0:T(8,128)} %refs_13_.1) | copy-start | bytes 393220
  29.0 10.0 %collective-permute-start.13 = (f32[8,2048]{1,0:T(8,128)S(1)}, f32[8,2048]{1,0:T(8,128)S(1)}, u32[]{:S(2)}, u32[]{:S(2)}) collective-permute-start(f32[8,2048]{1,0:T(8,128)S(1)} %get-tuple-element.38), channel_id=1, source_target_pairs={{0,24},{4,28},{8,16},{12,20},{16,8},{20,12},{24,0},{28,4},{1,25},{... | collective-permute-start | bytes 196616 | tf_op jit(solution)/shard_map/ppermute | solution.py:195
  32.2 7.1 %collective-permute-start.14 = (f32[8,2048]{1,0:T(8,128)S(1)}, f32[8,2048]{1,0:T(8,128)S(1)}, u32[]{:S(2)}, u32[]{:S(2)}) collective-permute-start(f32[8,2048]{1,0:T(8,128)S(1)} %get-tuple-element.39), channel_id=1, source_target_pairs={{0,28},{4,24},{8,20},{12,16},{16,12},{20,8},{24,4},{28,0},{1,29},{... | collective-permute-start | bytes 196616 | tf_op jit(solution)/shard_map/ppermute | solution.py:195
  33.3 5.0 %collective-permute-start.3 = (f32[16,2048]{1,0:T(8,128)S(1)}, f32[16,2048]{1,0:T(8,128)S(1)}, u32[]{:S(2)}, u32[]{:S(2)}) collective-permute-start(f32[16,2048]{1,0:T(8,128)S(1)} %pad_maximum_fusion.2), channel_id=1, source_target_pairs={{0,4},{4,0},{8,12},{12,8},{16,20},{20,16},{24,28},{28,24},{1,5},{5... | collective-permute-start | bytes 393224 | tf_op jit(solution)/shard_map/ppermute | solution.py:195

commit v7 on v6

--- a/solution.py
+++ b/solution.py
@@ -230,13 +230,14 @@
     near_b = pieces_for(grad_b[rank // 2 :])
     near_a = pieces_for(gradient(upstream_near, tokens))
     near = [jnp.concatenate(pair) for pair in zip(near_a, near_b)]
-    far_a[0], far_b[1] = lax.optimization_barrier((far_a[0], far_b[1]))
-    far_a[1], far_b[2] = lax.optimization_barrier((far_a[1], far_b[2]))
+    far_a[1], far_b[1] = lax.optimization_barrier((far_a[1], far_b[1]))
+    far_a[2], far_b[2] = lax.optimization_barrier((far_a[2], far_b[2]))
     far_a[2], far_b[3] = lax.optimization_barrier((far_a[2], far_b[3]))
+    far_a[0], near[1] = lax.optimization_barrier((far_a[0], near[1]))
+    for k in (1, 2, 3):
+        near[k] = sent(near[k], k)
     for k in range(half):
         far_b[k] = sent(far_b[k], half + k)
-    near = near[:1] + [sent(piece, k) for k, piece in enumerate(near) if k]
-
     far_b[0], upstream_near = lax.optimization_barrier((far_b[0], upstream_near))
 
     upstream = jnp.where(

time: 52.8 us -> 52 us (0.985)
  blocking collectives: 11.7 us -> 9.72 us
  starting transfers between devices: 23.2 us -> 25.1 us
  waiting for transfers between devices: 7.18 us -> 6.41 us
    all_to_all x1, blocking collectives: 11.7 us -> 9.72 us  [body(): gathered = lax.all_to_all(spread, ('dp', 'tensor'), 0, 0, tiled=True)]
    ppermute x11, starting transfers between devices: 18.7 us -> 20.6 us  [sent(): return lax.ppermute(block, 'dp', route)]
    ppermute x11, waiting for transfers between devices: 5.77 us -> 5.01 us  [sent(): return lax.ppermute(block, 'dp', route)]
where the time goes in v7:
time: 52 us; the launch traced here: 51.8 us
  starting transfers between devices  25.1 us (48%)
  blocking collectives  9.72 us (19%)
  matrix products  6.89 us (13%)
  waiting for transfers between devices  6.41 us (12%)
  Pallas kernels  2.37 us (5%)
  between operations  0.95 us (2%)
    ppermute x11, starting transfers between devices, sent(): return lax.ppermute(block, 'dp', route)  20.6 us
    all_to_all x1, blocking collectives, body(): gathered = lax.all_to_all(spread, ('dp', 'tensor'), 0, 0, tiled=True)  9.72 us
    ppermute x11, waiting for transfers between devices, sent(): return lax.ppermute(block, 'dp', route)  5.01 us
    ppermute x4, starting transfers between devices, other_of(): return lax.ppermute(block, axis, route)  4.48 us
    dot_general x2, matrix products, projected(): lax.dot_general(factor, block, (((1,), (1,)), ((), ())), preferred_elemen...  3.42 us
    dot_general x1, matrix products, body(): lax.dot_general(upstream, adapter_in, (((0,), (0,)), ((), ())), preferred...  2.05 us
    dot_general x3, matrix products, gradient(): return jnp.dot(sums, block, preferred_element_type=jnp.float32)  1.42 us
    ppermute x4, waiting for transfers between devices, other_of(): return lax.ppermute(block, axis, route)  1.41 us
  transfers between devices with their start and end apart: 15, of which 5 were waited for; matrix products, arithmetic and copies ran while one was open for 9% of the time, Pallas kernels for 1%

profile of v7, /device:TPU:0, one launch (start us, length us, event | category | flops | bytes accessed | tf_op | source)
XLA Modules:
  0.0 51.8 jit_solution(12926860220115512384)
XLA Ops:
  0.6 0.0 copy-start
  0.6 0.0 copy-start.1
  0.7 2.7 %fusion = f32[64,512]{1,0:T(8,128)S(1)} fusion(bf16[512,2048]{1,0:T(8,128)(2,1)} %param.7, f32[64,2048]{1,0:T(8,128)} %up_ref.1), kind=kOutput, calls=%fused_computation.1 | convolution fusion | flops 134348800 | bytes 2752512 | tf_op jit(solution)/shard_map/dot_general | solution.py:182
  3.3 0.5 collective-permute-start.1
  3.8 0.0 copy-done.1
  3.9 0.0 copy-done
  3.9 0.8 %fusion.14 = f32[64,512]{1,0:T(8,128)S(1)} fusion(bf16[64,2048]{1,0:T(8,128)(2,1)S(1)} %convert_element_type.15, bf16[512,2048]{1,0:T(8,128)(2,1)S(1)} %copy-done), kind=kOutput, calls=%fused_computation.43 | convolution fusion | flops 134217728 | bytes 2490368 | tf_op jit(solution)/shard_map/dot_general | solution.py:182
  4.6 0.1 collective-permute-start
  4.9 0.0 collective-permute-done.1
  4.9 2.9 %collective-permute-start.3 = (f32[32,512]{1,0:T(8,128)S(1)}, f32[32,512]{1,0:T(8,128)S(1)}, u32[]{:S(2)}, u32[]{:S(2)}) collective-permute-start(f32[32,512]{1,0:T(8,128)S(1)} %get-tuple-element.69), channel_id=1, source_target_pairs={{0,2},{1,3},{2,0},{3,1},{4,6},{5,7},{6,4},{7,5},{8,10},{9,11},{10,... | collective-permute-start | bytes 196616 | tf_op jit(solution)/shard_map/ppermute | solution.py:21
  7.8 0.0 collective-permute-done
  7.9 0.9 %collective-permute-start.2 = (f32[96,512]{1,0:T(8,128)S(1)}, f32[96,512]{1,0:T(8,128)S(1)}, u32[]{:S(2)}, u32[]{:S(2)}) collective-permute-start(f32[96,512]{1,0:T(8,128)S(1)} %pad_maximum_fusion), channel_id=1, source_target_pairs={{0,2},{1,3},{2,0},{3,1},{4,6},{5,7},{6,4},{7,5},{8,10},{9,11},{10,... | collective-permute-start | bytes 589832 | tf_op jit(solution)/shard_map/ppermute | solution.py:21
  8.8 1.4 %collective-permute-done.3 = f32[32,512]{1,0:T(8,128)S(1)} collective-permute-done((f32[32,512]{1,0:T(8,128)S(1)}, f32[32,512]{1,0:T(8,128)S(1)}, u32[]{:S(2)}, u32[]{:S(2)}) %collective-permute-start.3) | collective-permute-done | bytes 65568 | tf_op jit(solution)/shard_map/ppermute | solution.py:21
  10.3 0.5 fusion.15
  10.8 4.2 %collective-permute-start.10 = (f32[8,2048]{1,0:T(8,128)S(1)}, f32[8,2048]{1,0:T(8,128)S(1)}, u32[]{:S(2)}, u32[]{:S(2)}) collective-permute-start(f32[8,2048]{1,0:T(8,128)S(1)} %get-tuple-element.54), channel_id=1, source_target_pairs={{0,24},{4,28},{8,16},{12,20},{16,8},{20,12},{24,0},{28,4},{1,25},{... | collective-permute-start | bytes 196616 | tf_op jit(solution)/shard_map/ppermute | solution.py:195
  15.0 0.4 collective-permute-start.9
  15.4 3.5 %collective-permute-start.4 = (f32[8,2048]{1,0:T(8,128)S(1)}, f32[8,2048]{1,0:T(8,128)S(1)}, u32[]{:S(2)}, u32[]{:S(2)}) collective-permute-start(f32[8,2048]{1,0:T(8,128)S(1)} %get-tuple-element.56), channel_id=1, source_target_pairs={{0,16},{4,20},{8,24},{12,28},{16,0},{20,4},{24,8},{28,12},{1,17},{... | collective-permute-start | bytes 196616 | tf_op jit(solution)/shard_map/ppermute | solution.py:195
  18.9 0.0 collective-permute-done.2
  18.9 0.5 fusion.11
  19.4 0.0 copy-done.5
  19.4 0.5 fusion.2
  20.0 0.0 copy-start.2
  20.0 0.1 collective-permute-start.8
  20.1 1.1 %collective-permute-start.7 = (f32[16,2048]{1,0:T(8,128)S(1)}, f32[16,2048]{1,0:T(8,128)S(1)}, u32[]{:S(2)}, u32[]{:S(2)}) collective-permute-start(f32[16,2048]{1,0:T(8,128)S(1)} %pad_maximum_fusion.4), channel_id=1, source_target_pairs={{0,12},{4,8},{8,4},{12,0},{16,28},{20,24},{24,20},{28,16},{1,13},{... | collective-permute-start | bytes 393224 | tf_op jit(solution)/shard_map/ppermute | solution.py:195
  21.2 0.0 collective-permute-done.10.refs_6_
  21.3 1.1 %collective-permute-start.6 = (f32[16,2048]{1,0:T(8,128)S(1)}, f32[16,2048]{1,0:T(8,128)S(1)}, u32[]{:S(2)}, u32[]{:S(2)}) collective-permute-start(f32[16,2048]{1,0:T(8,128)S(1)} %pad_maximum_fusion.3), channel_id=1, source_target_pairs={{0,8},{4,12},{8,0},{12,4},{16,24},{20,28},{24,16},{28,20},{1,9},{5... | collective-permute-start | bytes 393224 | tf_op jit(solution)/shard_map/ppermute | solution.py:195
  22.3 2.0 %collective-permute-done.9.refs_5_ = f32[8,2048]{1,0:T(8,128)S(1)} collective-permute-done((f32[8,2048]{1,0:T(8,128)S(1)}, f32[8,2048]{1,0:T(8,128)S(1)}, u32[]{:S(2)}, u32[]{:S(2)}) %collective-permute-start.9) | collective-permute-done | bytes 65568 | tf_op jit(solution)/shard_map/ppermute | solution.py:195
  24.4 2.9 %collective-permute-start.11 = (f32[8,2048]{1,0:T(8,128)S(1)}, f32[8,2048]{1,0:T(8,128)S(1)}, u32[]{:S(2)}, u32[]{:S(2)}) collective-permute-start(f32[8,2048]{1,0:T(8,128)S(1)} %get-tuple-element.53), channel_id=1, source_target_pairs={{0,28},{4,24},{8,20},{12,16},{16,12},{20,8},{24,4},{28,0},{1,29},{... | collective-permute-start | bytes 196616 | tf_op jit(solution)/shard_map/ppermute | solution.py:195
  27.3 0.0 collective-permute-done.4.refs_4_
  27.3 0.0 collective-permute-start.12
  27.3 0.0 collective-permute-done.8.refs_4_.refs_8_
  27.3 2.8 %collective-permute-start.14 = (f32[8,2048]{1,0:T(8,128)S(1)}, f32[8,2048]{1,0:T(8,128)S(1)}, u32[]{:S(2)}, u32[]{:S(2)}) collective-permute-start(f32[8,2048]{1,0:T(8,128)S(1)} %get-tuple-element.43), channel_id=1, source_target_pairs={{0,28},{4,24},{8,20},{12,16},{16,12},{20,8},{24,4},{28,0},{1,29},{... | collective-permute-start | bytes 196616 | tf_op jit(solution)/shard_map/ppermute | solution.py:195
  30.1 1.1 %collective-permute-done.7.refs_3_ = f32[16,2048]{1,0:T(8,128)S(1)} collective-permute-done((f32[16,2048]{1,0:T(8,128)S(1)}, f32[16,2048]{1,0:T(8,128)S(1)}, u32[]{:S(2)}, u32[]{:S(2)}) %collective-permute-start.7) | collective-permute-done | bytes 131104 | tf_op jit(solution)/shard_map/ppermute | solution.py:195
  31.2 1.3 %collective-permute-start.13 = (f32[8,2048]{1,0:T(8,128)S(1)}, f32[8,2048]{1,0:T(8,128)S(1)}, u32[]{:S(2)}, u32[]{:S(2)}) collective-permute-start(f32[8,2048]{1,0:T(8,128)S(1)} %get-tuple-element.42), channel_id=1, source_target_pairs={{0,24},{4,28},{8,16},{12,20},{16,8},{20,12},{24,0},{28,4},{1,25},{... | collective-permute-start | bytes 196616 | tf_op jit(solution)/shard_map/ppermute | solution.py:195
  32.5 0.9 %collective-permute-done.6.refs_2_ = f32[16,2048]{1,0:T(8,128)S(1)} collective-permute-done((f32[16,2048]{1,0:T(8,128)S(1)}, f32[16,2048]{1,0:T(8,128)S(1)}, u32[]{:S(2)}, u32[]{:S(2)}) %collective-permute-start.6) | collective-permute-done | bytes 131104 | tf_op jit(solution)/shard_map/ppermute | solution.py:195
  33.4 3.3 %collective-permute-start.5 = (f32[16,2048]{1,0:T(8,128)S(1)}, f32[16,2048]{1,0:T(8,128)S(1)}, u32[]{:S(2)}, u32[]{:S(2)}) collective-permute-start(f32[16,2048]{1,0:T(8,128)S(1)} %pad_maximum_fusion.2), channel_id=1, source_target_pairs={{0,4},{4,0},{8,12},{12,8},{16,20},{20,16},{24,28},{28,24},{1,5},{5... | collective-permute-start | bytes 393224 | tf_op jit(solution)/shard_map/ppermute | solution.py:195
  36.8 2.0 %convolution_convert_fusion = bf16[512,2048]{1,0:T(8,128)(2,1)} fusion(bf16[64,2048]{1,0:T(8,128)(2,1)S(1)} %convert_element_type.15, bf16[32,512]{1,0:T(8,128)(2,1)S(1)} %multiply_convert_fusion.1, bf16[32,512]{1,0:T(8,128)(2,1)S(1)} %slice.16, pred[]{:T(512)S(6)} %lt.92), kind=kOutput, calls=%fused_computation | convolution fusion | flops 135561216 | bytes 2424833 | tf_op jit(solution)/shard_map/dot_general | solution.py:248
  38.8 0.9 %collective-permute-done.5.refs_1_ = f32[16,2048]{1,0:T(8,128)S(1)} collective-permute-done((f32[16,2048]{1,0:T(8,128)S(1)}, f32[16,2048]{1,0:T(8,128)S(1)}, u32[]{:S(2)}, u32[]{:S(2)}) %collective-permute-start.5) | collective-permute-done | bytes 131104 | tf_op jit(solution)/shard_map/ppermute | solution.py:195
  39.7 0.0 collective-permute-done.11.refs_7_
  39.7 0.0 copy-done.2
  39.7 0.7 %gram_a.1 = (f32[64,128]{1,0:T(8,128)S(1)}, bf16[3,128,640]{2,1,0:T(8,128)(2,1)S(1)}, f32[8,2048]{1,0:T(8,128)S(1)}, f32[8,2048]{1,0:T(8,128)S(1)}) custom-call(s32[1]{0:T(128)} %bitcast.me_ref, f32[64,2048]{1,0:T(8,128)S(1)} %copy-done.1, f32[64,2048]{1,0:T(8,128)S(1)} %copy-done.2, f32[16,2048]{1,0:T(8,128)S(1)} %pad_maximum_fusion.1.refs_0_, ...), custom_call_target="tpu_custom_call" | custom-call | tf_op jit(solution)/shard_map/gram_a/pallas_call | solution.py:258
  40.4 0.0 collective-permute-done.12.refs_5_.refs_9_
  40.4 0.0 collective-permute-done.14.refs_7_.refs_11_
  40.4 0.0 collective-permute-done.13.refs_6_.refs_10_
  40.4 0.3 gram_b.1
  40.7 9.7 %all_to_all.5.gathered_ref = f32[32,1,128]{2,1,0:T(1,128)S(1)} all-to-all(f32[32,1,128]{2,1,0:T(1,128)S(1)} %gram_b.1), channel_id=1, replica_groups=mesh['dp'=8,'tensor'=4] {'dp','tensor'}, dimensions={0} | all-to-all | bytes 32768 | tf_op jit(solution)/shard_map/all_to_all | solution.py:279
  50.4 0.0 copy-done.3
  50.4 1.4 %finish.1 = (f32[8,2048]{1,0:T(8,128)}, f32[8,2048]{1,0:T(8,128)}, f32[2,8,2048]{2,1,0:T(8,128)}, f32[2,8,2048]{2,1,0:T(8,128)}) custom-call(f32[32,1,128]{2,1,0:T(1,128)S(1)} %all_to_all.5.gathered_ref, bf16[3,128,640]{2,1,0:T(8,128)(2,1)S(1)} %get-tuple-element.44.maps_ref, f32[16,2048]{1,0:T(8,128)S(1)} %pad_maximum_fusion.1.refs_0_, ...), custom_call_target="tpu_custom_call" | custom-call | tf_op jit(solution)/shard_map/finish/pallas_call | solution.py:282
  (21 shorter events, 0.4 us)
Async XLA Ops:
  0.6 3.2 %copy-start = (bf16[512,2048]{1,0:T(8,128)(2,1)S(1)}, bf16[512,2048]{1,0:T(8,128)(2,1)}, u32[]{:S(2)}) copy-start(bf16[512,2048]{1,0:T(8,128)(2,1)} %param.6) | copy-start | bytes 6291460
  0.6 3.2 %copy-start.1 = (f32[64,2048]{1,0:T(8,128)S(1)}, f32[64,2048]{1,0:T(8,128)}, u32[]{:S(2)}) copy-start(f32[64,2048]{1,0:T(8,128)} %down_ref.1) | copy-start | bytes 1572868
  3.3 1.5 %collective-permute-start.1 = (f32[64,512]{1,0:T(8,128)S(1)}, f32[64,512]{1,0:T(8,128)S(1)}, u32[]{:S(2)}, u32[]{:S(2)}) collective-permute-start(f32[64,512]{1,0:T(8,128)S(1)} %fusion), channel_id=1, source_target_pairs={{0,1},{1,0},{2,3},{3,2},{4,5},{5,4},{6,7},{7,6},{8,9},{9,8},{10,11... | collective-permute-start | bytes 393224 | tf_op jit(solution)/shard_map/ppermute | solution.py:21
  4.6 3.2 %collective-permute-start = (f32[64,512]{1,0:T(8,128)S(1)}, f32[64,512]{1,0:T(8,128)S(1)}, u32[]{:S(2)}, u32[]{:S(2)}) collective-permute-start(f32[64,512]{1,0:T(8,128)S(1)} %fusion.14), channel_id=1, source_target_pairs={{0,1},{1,0},{2,3},{3,2},{4,5},{5,4},{6,7},{7,6},{8,9},{9,8},{10,11... | collective-permute-start | bytes 393224 | tf_op jit(solution)/shard_map/ppermute | solution.py:21
  4.9 5.3 %collective-permute-start.3 = (f32[32,512]{1,0:T(8,128)S(1)}, f32[32,512]{1,0:T(8,128)S(1)}, u32[]{:S(2)}, u32[]{:S(2)}) collective-permute-start(f32[32,512]{1,0:T(8,128)S(1)} %get-tuple-element.69), channel_id=1, source_target_pairs={{0,2},{1,3},{2,0},{3,1},{4,6},{5,7},{6,4},{7,5},{8,10},{9,11},{10,... | collective-permute-start | bytes 196616 | tf_op jit(solution)/shard_map/ppermute | solution.py:21
  7.9 11.0 %collective-permute-start.2 = (f32[96,512]{1,0:T(8,128)S(1)}, f32[96,512]{1,0:T(8,128)S(1)}, u32[]{:S(2)}, u32[]{:S(2)}) collective-permute-start(f32[96,512]{1,0:T(8,128)S(1)} %pad_maximum_fusion), channel_id=1, source_target_pairs={{0,2},{1,3},{2,0},{3,1},{4,6},{5,7},{6,4},{7,5},{8,10},{9,11},{10,... | collective-permute-start | bytes 589832 | tf_op jit(solution)/shard_map/ppermute | solution.py:21
  10.7 8.7 %copy-start.5 = (bf16[512,2048]{1,0:T(8,128)(2,1)S(1)}, bf16[512,2048]{1,0:T(8,128)(2,1)}, u32[]{:S(2)}) copy-start(bf16[512,2048]{1,0:T(8,128)(2,1)} %param.7) | copy-start | bytes 6291460
  10.8 10.5 %collective-permute-start.10 = (f32[8,2048]{1,0:T(8,128)S(1)}, f32[8,2048]{1,0:T(8,128)S(1)}, u32[]{:S(2)}, u32[]{:S(2)}) collective-permute-start(f32[8,2048]{1,0:T(8,128)S(1)} %get-tuple-element.54), channel_id=1, source_target_pairs={{0,24},{4,28},{8,16},{12,20},{16,8},{20,12},{24,0},{28,4},{1,25},{... | collective-permute-start | bytes 196616 | tf_op jit(solution)/shard_map/ppermute | solution.py:195
  15.0 9.4 %collective-permute-start.9 = (f32[8,2048]{1,0:T(8,128)S(1)}, f32[8,2048]{1,0:T(8,128)S(1)}, u32[]{:S(2)}, u32[]{:S(2)}) collective-permute-start(f32[8,2048]{1,0:T(8,128)S(1)} %get-tuple-element.55), channel_id=1, source_target_pairs={{0,20},{4,16},{8,28},{12,24},{16,4},{20,0},{24,12},{28,8},{1,21},{... | collective-permute-start | bytes 196616 | tf_op jit(solution)/shard_map/ppermute | solution.py:195
  15.4 11.9 %collective-permute-start.4 = (f32[8,2048]{1,0:T(8,128)S(1)}, f32[8,2048]{1,0:T(8,128)S(1)}, u32[]{:S(2)}, u32[]{:S(2)}) collective-permute-start(f32[8,2048]{1,0:T(8,128)S(1)} %get-tuple-element.56), channel_id=1, source_target_pairs={{0,16},{4,20},{8,24},{12,28},{16,0},{20,4},{24,8},{28,12},{1,17},{... | collective-permute-start | bytes 196616 | tf_op jit(solution)/shard_map/ppermute | solution.py:195
  20.0 19.7 %copy-start.2 = (f32[64,2048]{1,0:T(8,128)S(1)}, f32[64,2048]{1,0:T(8,128)}, u32[]{:S(2)}) copy-start(f32[64,2048]{1,0:T(8,128)} %up_ref.1) | copy-start | bytes 1572868
  20.0 7.3 %collective-permute-start.8 = (f32[8,2048]{1,0:T(8,128)S(1)}, f32[8,2048]{1,0:T(8,128)S(1)}, u32[]{:S(2)}, u32[]{:S(2)}) collective-permute-start(f32[8,2048]{1,0:T(8,128)S(1)} %get-tuple-element.60), channel_id=1, source_target_pairs={{0,16},{4,20},{8,24},{12,28},{16,0},{20,4},{24,8},{28,12},{1,17},{... | collective-permute-start | bytes 196616 | tf_op jit(solution)/shard_map/ppermute | solution.py:195
  20.1 11.1 %collective-permute-start.7 = (f32[16,2048]{1,0:T(8,128)S(1)}, f32[16,2048]{1,0:T(8,128)S(1)}, u32[]{:S(2)}, u32[]{:S(2)}) collective-permute-start(f32[16,2048]{1,0:T(8,128)S(1)} %pad_maximum_fusion.4), channel_id=1, source_target_pairs={{0,12},{4,8},{8,4},{12,0},{16,28},{20,24},{24,20},{28,16},{1,13},{... | collective-permute-start | bytes 393224 | tf_op jit(solution)/shard_map/ppermute | solution.py:195
  21.3 12.2 %collective-permute-start.6 = (f32[16,2048]{1,0:T(8,128)S(1)}, f32[16,2048]{1,0:T(8,128)S(1)}, u32[]{:S(2)}, u32[]{:S(2)}) collective-permute-start(f32[16,2048]{1,0:T(8,128)S(1)} %pad_maximum_fusion.3), channel_id=1, source_target_pairs={{0,8},{4,12},{8,0},{12,4},{16,24},{20,28},{24,16},{28,20},{1,9},{5... | collective-permute-start | bytes 393224 | tf_op jit(solution)/shard_map/ppermute | solution.py:195
  24.4 15.3 %collective-permute-start.11 = (f32[8,2048]{1,0:T(8,128)S(1)}, f32[8,2048]{1,0:T(8,128)S(1)}, u32[]{:S(2)}, u32[]{:S(2)}) collective-permute-start(f32[8,2048]{1,0:T(8,128)S(1)} %get-tuple-element.53), channel_id=1, source_target_pairs={{0,28},{4,24},{8,20},{12,16},{16,12},{20,8},{24,4},{28,0},{1,29},{... | collective-permute-start | bytes 196616 | tf_op jit(solution)/shard_map/ppermute | solution.py:195
  27.3 23.2 %copy-start.3 = (f32[2,8,2048]{2,1,0:T(8,128)S(1)}, f32[2,8,2048]{2,1,0:T(8,128)}, u32[]{:S(2)}) copy-start(f32[2,8,2048]{2,1,0:T(8,128)} %refs_12_.1) | copy-start | bytes 393220
  27.3 23.2 %copy-start.4 = (f32[2,8,2048]{2,1,0:T(8,128)S(1)}, f32[2,8,2048]{2,1,0:T(8,128)}, u32[]{:S(2)}) copy-start(f32[2,8,2048]{2,1,0:T(8,128)} %refs_13_.1) | copy-start | bytes 393220
  27.3 13.1 %collective-permute-start.12 = (f32[8,2048]{1,0:T(8,128)S(1)}, f32[8,2048]{1,0:T(8,128)S(1)}, u32[]{:S(2)}, u32[]{:S(2)}) collective-permute-start(f32[8,2048]{1,0:T(8,128)S(1)} %get-tuple-element.41), channel_id=1, source_target_pairs={{0,20},{4,16},{8,28},{12,24},{16,4},{20,0},{24,12},{28,8},{1,21},{... | collective-permute-start | bytes 196616 | tf_op jit(solution)/shard_map/ppermute | solution.py:195
  27.3 13.1 %collective-permute-start.14 = (f32[8,2048]{1,0:T(8,128)S(1)}, f32[8,2048]{1,0:T(8,128)S(1)}, u32[]{:S(2)}, u32[]{:S(2)}) collective-permute-start(f32[8,2048]{1,0:T(8,128)S(1)} %get-tuple-element.43), channel_id=1, source_target_pairs={{0,28},{4,24},{8,20},{12,16},{16,12},{20,8},{24,4},{28,0},{1,29},{... | collective-permute-start | bytes 196616 | tf_op jit(solution)/shard_map/ppermute | solution.py:195
  31.2 9.2 %collective-permute-start.13 = (f32[8,2048]{1,0:T(8,128)S(1)}, f32[8,2048]{1,0:T(8,128)S(1)}, u32[]{:S(2)}, u32[]{:S(2)}) collective-permute-start(f32[8,2048]{1,0:T(8,128)S(1)} %get-tuple-element.42), channel_id=1, source_target_pairs={{0,24},{4,28},{8,16},{12,20},{16,8},{20,12},{24,0},{28,4},{1,25},{... | collective-permute-start | bytes 196616 | tf_op jit(solution)/shard_map/ppermute | solution.py:195
  33.4 6.3 %collective-permute-start.5 = (f32[16,2048]{1,0:T(8,128)S(1)}, f32[16,2048]{1,0:T(8,128)S(1)}, u32[]{:S(2)}, u32[]{:S(2)}) collective-permute-start(f32[16,2048]{1,0:T(8,128)S(1)} %pad_maximum_fusion.2), channel_id=1, source_target_pairs={{0,4},{4,0},{8,12},{12,8},{16,20},{20,16},{24,28},{28,24},{1,5},{5... | collective-permute-start | bytes 393224 | tf_op jit(solution)/shard_map/ppermute | solution.py:195

commit v8 on v7

--- a/solution.py
+++ b/solution.py
@@ -10,7 +10,7 @@
 SCALE = 2.0
 NORM_EPS = 1e-06
 LANES = 128
-VMEM_LIMIT = 32 * 1024 * 1024
+VMEM_LIMIT = 12 * 1024 * 1024
 IN_VMEM = pl.BlockSpec(memory_space=pltpu.VMEM)
 IN_HBM = pl.BlockSpec(memory_space=pltpu.HBM)
 IN_SMEM = pl.BlockSpec(memory_space=pltpu.SMEM)
@@ -227,8 +227,8 @@
     hidden, upstream_near = rest[:rank], rest[rank:]
     grad_b = gradient(hidden, cotangent)
     far_b = pieces_for(grad_b[: rank // 2])
+    near_a = pieces_for(gradient(upstream_near, tokens))
     near_b = pieces_for(grad_b[rank // 2 :])
-    near_a = pieces_for(gradient(upstream_near, tokens))
     near = [jnp.concatenate(pair) for pair in zip(near_a, near_b)]
     far_a[1], far_b[1] = lax.optimization_barrier((far_a[1], far_b[1]))
     far_a[2], far_b[2] = lax.optimization_barrier((far_a[2], far_b[2]))

time: 52 us -> 52 us (level)
  no operation moved by 1% of the time
where the time goes in v8:
time: 52 us; the launch traced here: 51.8 us
  starting transfers between devices  25.1 us (48%)
  blocking collectives  9.71 us (19%)
  matrix products  6.89 us (13%)
  waiting for transfers between devices  6.37 us (12%)
  Pallas kernels  2.37 us (5%)
  between operations  0.95 us (2%)
    ppermute x11, starting transfers between devices, sent(): return lax.ppermute(block, 'dp', route)  20.7 us
    all_to_all x1, blocking collectives, body(): gathered = lax.all_to_all(spread, ('dp', 'tensor'), 0, 0, tiled=True)  9.71 us
    ppermute x11, waiting for transfers between devices, sent(): return lax.ppermute(block, 'dp', route)  4.96 us
    ppermute x4, starting transfers between devices, other_of(): return lax.ppermute(block, axis, route)  4.48 us
    dot_general x2, matrix products, projected(): lax.dot_general(factor, block, (((1,), (1,)), ((), ())), preferred_elemen...  3.42 us
    dot_general x1, matrix products, body(): lax.dot_general(upstream, adapter_in, (((0,), (0,)), ((), ())), preferred...  2.05 us
    dot_general x3, matrix products, gradient(): return jnp.dot(sums, block, preferred_element_type=jnp.float32)  1.42 us
    ppermute x4, waiting for transfers between devices, other_of(): return lax.ppermute(block, axis, route)  1.41 us
  transfers between devices with their start and end apart: 15, of which 5 were waited for; matrix products, arithmetic and copies ran while one was open for 9% of the time, Pallas kernels for 1%

profile of v8, /device:TPU:0, one launch (start us, length us, event | category | flops | bytes accessed | tf_op | source)
XLA Modules:
  0.0 51.8 jit_solution(11956187120029498849)
XLA Ops:
  0.6 0.0 copy-start
  0.6 0.0 copy-start.1
  0.7 2.7 %fusion = f32[64,512]{1,0:T(8,128)S(1)} fusion(bf16[512,2048]{1,0:T(8,128)(2,1)} %param.7, f32[64,2048]{1,0:T(8,128)} %up_ref.1), kind=kOutput, calls=%fused_computation.1 | convolution fusion | flops 134348800 | bytes 2752512 | tf_op jit(solution)/shard_map/dot_general | solution.py:182
  3.3 0.5 collective-permute-start.1
  3.8 0.0 copy-done.1
  3.9 0.0 copy-done
  3.9 0.8 %fusion.14 = f32[64,512]{1,0:T(8,128)S(1)} fusion(bf16[64,2048]{1,0:T(8,128)(2,1)S(1)} %convert_element_type.15, bf16[512,2048]{1,0:T(8,128)(2,1)S(1)} %copy-done), kind=kOutput, calls=%fused_computation.43 | convolution fusion | flops 134217728 | bytes 2490368 | tf_op jit(solution)/shard_map/dot_general | solution.py:182
  4.6 0.1 collective-permute-start
  4.9 0.0 collective-permute-done.1
  4.9 2.9 %collective-permute-start.3 = (f32[32,512]{1,0:T(8,128)S(1)}, f32[32,512]{1,0:T(8,128)S(1)}, u32[]{:S(2)}, u32[]{:S(2)}) collective-permute-start(f32[32,512]{1,0:T(8,128)S(1)} %get-tuple-element.69), channel_id=1, source_target_pairs={{0,2},{1,3},{2,0},{3,1},{4,6},{5,7},{6,4},{7,5},{8,10},{9,11},{10,... | collective-permute-start | bytes 196616 | tf_op jit(solution)/shard_map/ppermute | solution.py:21
  7.8 0.0 collective-permute-done
  7.9 0.9 %collective-permute-start.2 = (f32[96,512]{1,0:T(8,128)S(1)}, f32[96,512]{1,0:T(8,128)S(1)}, u32[]{:S(2)}, u32[]{:S(2)}) collective-permute-start(f32[96,512]{1,0:T(8,128)S(1)} %pad_maximum_fusion), channel_id=1, source_target_pairs={{0,2},{1,3},{2,0},{3,1},{4,6},{5,7},{6,4},{7,5},{8,10},{9,11},{10,... | collective-permute-start | bytes 589832 | tf_op jit(solution)/shard_map/ppermute | solution.py:21
  8.8 1.4 %collective-permute-done.3 = f32[32,512]{1,0:T(8,128)S(1)} collective-permute-done((f32[32,512]{1,0:T(8,128)S(1)}, f32[32,512]{1,0:T(8,128)S(1)}, u32[]{:S(2)}, u32[]{:S(2)}) %collective-permute-start.3) | collective-permute-done | bytes 65568 | tf_op jit(solution)/shard_map/ppermute | solution.py:21
  10.3 0.5 fusion.15
  10.8 4.2 %collective-permute-start.10 = (f32[8,2048]{1,0:T(8,128)S(1)}, f32[8,2048]{1,0:T(8,128)S(1)}, u32[]{:S(2)}, u32[]{:S(2)}) collective-permute-start(f32[8,2048]{1,0:T(8,128)S(1)} %get-tuple-element.54), channel_id=1, source_target_pairs={{0,24},{4,28},{8,16},{12,20},{16,8},{20,12},{24,0},{28,4},{1,25},{... | collective-permute-start | bytes 196616 | tf_op jit(solution)/shard_map/ppermute | solution.py:195
  15.0 0.4 collective-permute-start.9
  15.4 3.5 %collective-permute-start.4 = (f32[8,2048]{1,0:T(8,128)S(1)}, f32[8,2048]{1,0:T(8,128)S(1)}, u32[]{:S(2)}, u32[]{:S(2)}) collective-permute-start(f32[8,2048]{1,0:T(8,128)S(1)} %get-tuple-element.56), channel_id=1, source_target_pairs={{0,16},{4,20},{8,24},{12,28},{16,0},{20,4},{24,8},{28,12},{1,17},{... | collective-permute-start | bytes 196616 | tf_op jit(solution)/shard_map/ppermute | solution.py:195
  18.9 0.0 collective-permute-done.2
  18.9 0.5 fusion.11
  19.4 0.0 copy-done.5
  19.4 0.5 fusion.2
  20.0 0.0 copy-start.2
  20.0 0.1 collective-permute-start.8
  20.1 1.1 %collective-permute-start.7 = (f32[16,2048]{1,0:T(8,128)S(1)}, f32[16,2048]{1,0:T(8,128)S(1)}, u32[]{:S(2)}, u32[]{:S(2)}) collective-permute-start(f32[16,2048]{1,0:T(8,128)S(1)} %pad_maximum_fusion.4), channel_id=1, source_target_pairs={{0,12},{4,8},{8,4},{12,0},{16,28},{20,24},{24,20},{28,16},{1,13},{... | collective-permute-start | bytes 393224 | tf_op jit(solution)/shard_map/ppermute | solution.py:195
  21.3 0.0 collective-permute-done.10.refs_6_
  21.3 1.1 %collective-permute-start.6 = (f32[16,2048]{1,0:T(8,128)S(1)}, f32[16,2048]{1,0:T(8,128)S(1)}, u32[]{:S(2)}, u32[]{:S(2)}) collective-permute-start(f32[16,2048]{1,0:T(8,128)S(1)} %pad_maximum_fusion.3), channel_id=1, source_target_pairs={{0,8},{4,12},{8,0},{12,4},{16,24},{20,28},{24,16},{28,20},{1,9},{5... | collective-permute-start | bytes 393224 | tf_op jit(solution)/shard_map/ppermute | solution.py:195
  22.3 2.0 %collective-permute-done.9.refs_5_ = f32[8,2048]{1,0:T(8,128)S(1)} collective-permute-done((f32[8,2048]{1,0:T(8,128)S(1)}, f32[8,2048]{1,0:T(8,128)S(1)}, u32[]{:S(2)}, u32[]{:S(2)}) %collective-permute-start.9) | collective-permute-done | bytes 65568 | tf_op jit(solution)/shard_map/ppermute | solution.py:195
  24.4 2.9 %collective-permute-start.11 = (f32[8,2048]{1,0:T(8,128)S(1)}, f32[8,2048]{1,0:T(8,128)S(1)}, u32[]{:S(2)}, u32[]{:S(2)}) collective-permute-start(f32[8,2048]{1,0:T(8,128)S(1)} %get-tuple-element.53), channel_id=1, source_target_pairs={{0,28},{4,24},{8,20},{12,16},{16,12},{20,8},{24,4},{28,0},{1,29},{... | collective-permute-start | bytes 196616 | tf_op jit(solution)/shard_map/ppermute | solution.py:195
  27.3 0.0 collective-permute-done.4.refs_4_
  27.3 0.0 collective-permute-start.12
  27.3 0.0 collective-permute-done.8.refs_4_.refs_8_
  27.3 2.8 %collective-permute-start.14 = (f32[8,2048]{1,0:T(8,128)S(1)}, f32[8,2048]{1,0:T(8,128)S(1)}, u32[]{:S(2)}, u32[]{:S(2)}) collective-permute-start(f32[8,2048]{1,0:T(8,128)S(1)} %get-tuple-element.43), channel_id=1, source_target_pairs={{0,28},{4,24},{8,20},{12,16},{16,12},{20,8},{24,4},{28,0},{1,29},{... | collective-permute-start | bytes 196616 | tf_op jit(solution)/shard_map/ppermute | solution.py:195
  30.1 1.1 %collective-permute-done.7.refs_3_ = f32[16,2048]{1,0:T(8,128)S(1)} collective-permute-done((f32[16,2048]{1,0:T(8,128)S(1)}, f32[16,2048]{1,0:T(8,128)S(1)}, u32[]{:S(2)}, u32[]{:S(2)}) %collective-permute-start.7) | collective-permute-done | bytes 131104 | tf_op jit(solution)/shard_map/ppermute | solution.py:195
  31.2 1.3 %collective-permute-start.13 = (f32[8,2048]{1,0:T(8,128)S(1)}, f32[8,2048]{1,0:T(8,128)S(1)}, u32[]{:S(2)}, u32[]{:S(2)}) collective-permute-start(f32[8,2048]{1,0:T(8,128)S(1)} %get-tuple-element.42), channel_id=1, source_target_pairs={{0,24},{4,28},{8,16},{12,20},{16,8},{20,12},{24,0},{28,4},{1,25},{... | collective-permute-start | bytes 196616 | tf_op jit(solution)/shard_map/ppermute | solution.py:195
  32.5 0.9 %collective-permute-done.6.refs_2_ = f32[16,2048]{1,0:T(8,128)S(1)} collective-permute-done((f32[16,2048]{1,0:T(8,128)S(1)}, f32[16,2048]{1,0:T(8,128)S(1)}, u32[]{:S(2)}, u32[]{:S(2)}) %collective-permute-start.6) | collective-permute-done | bytes 131104 | tf_op jit(solution)/shard_map/ppermute | solution.py:195
  33.4 3.3 %collective-permute-start.5 = (f32[16,2048]{1,0:T(8,128)S(1)}, f32[16,2048]{1,0:T(8,128)S(1)}, u32[]{:S(2)}, u32[]{:S(2)}) collective-permute-start(f32[16,2048]{1,0:T(8,128)S(1)} %pad_maximum_fusion.2), channel_id=1, source_target_pairs={{0,4},{4,0},{8,12},{12,8},{16,20},{20,16},{24,28},{28,24},{1,5},{5... | collective-permute-start | bytes 393224 | tf_op jit(solution)/shard_map/ppermute | solution.py:195
  36.8 2.0 %convolution_convert_fusion = bf16[512,2048]{1,0:T(8,128)(2,1)} fusion(bf16[64,2048]{1,0:T(8,128)(2,1)S(1)} %convert_element_type.15, bf16[32,512]{1,0:T(8,128)(2,1)S(1)} %multiply_convert_fusion.1, bf16[32,512]{1,0:T(8,128)(2,1)S(1)} %slice.16, pred[]{:T(512)S(6)} %lt.92), kind=kOutput, calls=%fused_computation | convolution fusion | flops 135561216 | bytes 2424833 | tf_op jit(solution)/shard_map/dot_general | solution.py:248
  38.8 0.9 %collective-permute-done.5.refs_1_ = f32[16,2048]{1,0:T(8,128)S(1)} collective-permute-done((f32[16,2048]{1,0:T(8,128)S(1)}, f32[16,2048]{1,0:T(8,128)S(1)}, u32[]{:S(2)}, u32[]{:S(2)}) %collective-permute-start.5) | collective-permute-done | bytes 131104 | tf_op jit(solution)/shard_map/ppermute | solution.py:195
  39.7 0.0 collective-permute-done.11.refs_7_
  39.7 0.0 copy-done.2
  39.7 0.7 %gram_a.1 = (f32[64,128]{1,0:T(8,128)S(1)}, bf16[3,128,640]{2,1,0:T(8,128)(2,1)S(1)}, f32[8,2048]{1,0:T(8,128)S(1)}, f32[8,2048]{1,0:T(8,128)S(1)}) custom-call(s32[1]{0:T(128)} %bitcast.me_ref, f32[64,2048]{1,0:T(8,128)S(1)} %copy-done.1, f32[64,2048]{1,0:T(8,128)S(1)} %copy-done.2, f32[16,2048]{1,0:T(8,128)S(1)} %pad_maximum_fusion.1.refs_0_, ...), custom_call_target="tpu_custom_call" | custom-call | tf_op jit(solution)/shard_map/gram_a/pallas_call | solution.py:258
  40.4 0.0 collective-permute-done.12.refs_5_.refs_9_
  40.4 0.0 collective-permute-done.14.refs_7_.refs_11_
  40.4 0.0 collective-permute-done.13.refs_6_.refs_10_
  40.4 0.3 gram_b.1
  40.7 9.7 %all_to_all.5.gathered_ref = f32[32,1,128]{2,1,0:T(1,128)S(1)} all-to-all(f32[32,1,128]{2,1,0:T(1,128)S(1)} %gram_b.1), channel_id=1, replica_groups=mesh['dp'=8,'tensor'=4] {'dp','tensor'}, dimensions={0} | all-to-all | bytes 32768 | tf_op jit(solution)/shard_map/all_to_all | solution.py:279
  50.4 0.0 copy-done.4
  50.4 1.4 %finish.1 = (f32[8,2048]{1,0:T(8,128)}, f32[8,2048]{1,0:T(8,128)}, f32[2,8,2048]{2,1,0:T(8,128)}, f32[2,8,2048]{2,1,0:T(8,128)}) custom-call(f32[32,1,128]{2,1,0:T(1,128)S(1)} %all_to_all.5.gathered_ref, bf16[3,128,640]{2,1,0:T(8,128)(2,1)S(1)} %get-tuple-element.44.maps_ref, f32[16,2048]{1,0:T(8,128)S(1)} %pad_maximum_fusion.1.refs_0_, ...), custom_call_target="tpu_custom_call" | custom-call | tf_op jit(solution)/shard_map/finish/pallas_call | solution.py:282
  (21 shorter events, 0.4 us)
Async XLA Ops:
  0.6 3.2 %copy-start = (bf16[512,2048]{1,0:T(8,128)(2,1)S(1)}, bf16[512,2048]{1,0:T(8,128)(2,1)}, u32[]{:S(2)}) copy-start(bf16[512,2048]{1,0:T(8,128)(2,1)} %param.6) | copy-start | bytes 6291460
  0.6 3.2 %copy-start.1 = (f32[64,2048]{1,0:T(8,128)S(1)}, f32[64,2048]{1,0:T(8,128)}, u32[]{:S(2)}) copy-start(f32[64,2048]{1,0:T(8,128)} %down_ref.1) | copy-start | bytes 1572868
  3.3 1.5 %collective-permute-start.1 = (f32[64,512]{1,0:T(8,128)S(1)}, f32[64,512]{1,0:T(8,128)S(1)}, u32[]{:S(2)}, u32[]{:S(2)}) collective-permute-start(f32[64,512]{1,0:T(8,128)S(1)} %fusion), channel_id=1, source_target_pairs={{0,1},{1,0},{2,3},{3,2},{4,5},{5,4},{6,7},{7,6},{8,9},{9,8},{10,11... | collective-permute-start | bytes 393224 | tf_op jit(solution)/shard_map/ppermute | solution.py:21
  4.6 3.2 %collective-permute-start = (f32[64,512]{1,0:T(8,128)S(1)}, f32[64,512]{1,0:T(8,128)S(1)}, u32[]{:S(2)}, u32[]{:S(2)}) collective-permute-start(f32[64,512]{1,0:T(8,128)S(1)} %fusion.14), channel_id=1, source_target_pairs={{0,1},{1,0},{2,3},{3,2},{4,5},{5,4},{6,7},{7,6},{8,9},{9,8},{10,11... | collective-permute-start | bytes 393224 | tf_op jit(solution)/shard_map/ppermute | solution.py:21
  4.9 5.3 %collective-permute-start.3 = (f32[32,512]{1,0:T(8,128)S(1)}, f32[32,512]{1,0:T(8,128)S(1)}, u32[]{:S(2)}, u32[]{:S(2)}) collective-permute-start(f32[32,512]{1,0:T(8,128)S(1)} %get-tuple-element.69), channel_id=1, source_target_pairs={{0,2},{1,3},{2,0},{3,1},{4,6},{5,7},{6,4},{7,5},{8,10},{9,11},{10,... | collective-permute-start | bytes 196616 | tf_op jit(solution)/shard_map/ppermute | solution.py:21
  7.9 11.0 %collective-permute-start.2 = (f32[96,512]{1,0:T(8,128)S(1)}, f32[96,512]{1,0:T(8,128)S(1)}, u32[]{:S(2)}, u32[]{:S(2)}) collective-permute-start(f32[96,512]{1,0:T(8,128)S(1)} %pad_maximum_fusion), channel_id=1, source_target_pairs={{0,2},{1,3},{2,0},{3,1},{4,6},{5,7},{6,4},{7,5},{8,10},{9,11},{10,... | collective-permute-start | bytes 589832 | tf_op jit(solution)/shard_map/ppermute | solution.py:21
  10.7 8.7 %copy-start.5 = (bf16[512,2048]{1,0:T(8,128)(2,1)S(1)}, bf16[512,2048]{1,0:T(8,128)(2,1)}, u32[]{:S(2)}) copy-start(bf16[512,2048]{1,0:T(8,128)(2,1)} %param.7) | copy-start | bytes 6291460
  10.8 10.5 %collective-permute-start.10 = (f32[8,2048]{1,0:T(8,128)S(1)}, f32[8,2048]{1,0:T(8,128)S(1)}, u32[]{:S(2)}, u32[]{:S(2)}) collective-permute-start(f32[8,2048]{1,0:T(8,128)S(1)} %get-tuple-element.54), channel_id=1, source_target_pairs={{0,24},{4,28},{8,16},{12,20},{16,8},{20,12},{24,0},{28,4},{1,25},{... | collective-permute-start | bytes 196616 | tf_op jit(solution)/shard_map/ppermute | solution.py:195
  15.0 9.4 %collective-permute-start.9 = (f32[8,2048]{1,0:T(8,128)S(1)}, f32[8,2048]{1,0:T(8,128)S(1)}, u32[]{:S(2)}, u32[]{:S(2)}) collective-permute-start(f32[8,2048]{1,0:T(8,128)S(1)} %get-tuple-element.55), channel_id=1, source_target_pairs={{0,20},{4,16},{8,28},{12,24},{16,4},{20,0},{24,12},{28,8},{1,21},{... | collective-permute-start | bytes 196616 | tf_op jit(solution)/shard_map/ppermute | solution.py:195
  15.4 11.9 %collective-permute-start.4 = (f32[8,2048]{1,0:T(8,128)S(1)}, f32[8,2048]{1,0:T(8,128)S(1)}, u32[]{:S(2)}, u32[]{:S(2)}) collective-permute-start(f32[8,2048]{1,0:T(8,128)S(1)} %get-tuple-element.56), channel_id=1, source_target_pairs={{0,16},{4,20},{8,24},{12,28},{16,0},{20,4},{24,8},{28,12},{1,17},{... | collective-permute-start | bytes 196616 | tf_op jit(solution)/shard_map/ppermute | solution.py:195
  20.0 19.7 %copy-start.2 = (f32[64,2048]{1,0:T(8,128)S(1)}, f32[64,2048]{1,0:T(8,128)}, u32[]{:S(2)}) copy-start(f32[64,2048]{1,0:T(8,128)} %up_ref.1) | copy-start | bytes 1572868
  20.0 7.3 %collective-permute-start.8 = (f32[8,2048]{1,0:T(8,128)S(1)}, f32[8,2048]{1,0:T(8,128)S(1)}, u32[]{:S(2)}, u32[]{:S(2)}) collective-permute-start(f32[8,2048]{1,0:T(8,128)S(1)} %get-tuple-element.60), channel_id=1, source_target_pairs={{0,16},{4,20},{8,24},{12,28},{16,0},{20,4},{24,8},{28,12},{1,17},{... | collective-permute-start | bytes 196616 | tf_op jit(solution)/shard_map/ppermute | solution.py:195
  20.1 11.0 %collective-permute-start.7 = (f32[16,2048]{1,0:T(8,128)S(1)}, f32[16,2048]{1,0:T(8,128)S(1)}, u32[]{:S(2)}, u32[]{:S(2)}) collective-permute-start(f32[16,2048]{1,0:T(8,128)S(1)} %pad_maximum_fusion.4), channel_id=1, source_target_pairs={{0,12},{4,8},{8,4},{12,0},{16,28},{20,24},{24,20},{28,16},{1,13},{... | collective-permute-start | bytes 393224 | tf_op jit(solution)/shard_map/ppermute | solution.py:195
  21.3 12.1 %collective-permute-start.6 = (f32[16,2048]{1,0:T(8,128)S(1)}, f32[16,2048]{1,0:T(8,128)S(1)}, u32[]{:S(2)}, u32[]{:S(2)}) collective-permute-start(f32[16,2048]{1,0:T(8,128)S(1)} %pad_maximum_fusion.3), channel_id=1, source_target_pairs={{0,8},{4,12},{8,0},{12,4},{16,24},{20,28},{24,16},{28,20},{1,9},{5... | collective-permute-start | bytes 393224 | tf_op jit(solution)/shard_map/ppermute | solution.py:195
  24.4 15.3 %collective-permute-start.11 = (f32[8,2048]{1,0:T(8,128)S(1)}, f32[8,2048]{1,0:T(8,128)S(1)}, u32[]{:S(2)}, u32[]{:S(2)}) collective-permute-start(f32[8,2048]{1,0:T(8,128)S(1)} %get-tuple-element.53), channel_id=1, source_target_pairs={{0,28},{4,24},{8,20},{12,16},{16,12},{20,8},{24,4},{28,0},{1,29},{... | collective-permute-start | bytes 196616 | tf_op jit(solution)/shard_map/ppermute | solution.py:195
  27.3 23.2 %copy-start.3 = (f32[2,8,2048]{2,1,0:T(8,128)S(1)}, f32[2,8,2048]{2,1,0:T(8,128)}, u32[]{:S(2)}) copy-start(f32[2,8,2048]{2,1,0:T(8,128)} %refs_12_.1) | copy-start | bytes 393220
  27.3 23.2 %copy-start.4 = (f32[2,8,2048]{2,1,0:T(8,128)S(1)}, f32[2,8,2048]{2,1,0:T(8,128)}, u32[]{:S(2)}) copy-start(f32[2,8,2048]{2,1,0:T(8,128)} %refs_13_.1) | copy-start | bytes 393220
  27.3 13.1 %collective-permute-start.12 = (f32[8,2048]{1,0:T(8,128)S(1)}, f32[8,2048]{1,0:T(8,128)S(1)}, u32[]{:S(2)}, u32[]{:S(2)}) collective-permute-start(f32[8,2048]{1,0:T(8,128)S(1)} %get-tuple-element.41), channel_id=1, source_target_pairs={{0,20},{4,16},{8,28},{12,24},{16,4},{20,0},{24,12},{28,8},{1,21},{... | collective-permute-start | bytes 196616 | tf_op jit(solution)/shard_map/ppermute | solution.py:195
  27.3 13.1 %collective-permute-start.14 = (f32[8,2048]{1,0:T(8,128)S(1)}, f32[8,2048]{1,0:T(8,128)S(1)}, u32[]{:S(2)}, u32[]{:S(2)}) collective-permute-start(f32[8,2048]{1,0:T(8,128)S(1)} %get-tuple-element.43), channel_id=1, source_target_pairs={{0,28},{4,24},{8,20},{12,16},{16,12},{20,8},{24,4},{28,0},{1,29},{... | collective-permute-start | bytes 196616 | tf_op jit(solution)/shard_map/ppermute | solution.py:195
  31.2 9.2 %collective-permute-start.13 = (f32[8,2048]{1,0:T(8,128)S(1)}, f32[8,2048]{1,0:T(8,128)S(1)}, u32[]{:S(2)}, u32[]{:S(2)}) collective-permute-start(f32[8,2048]{1,0:T(8,128)S(1)} %get-tuple-element.42), channel_id=1, source_target_pairs={{0,24},{4,28},{8,16},{12,20},{16,8},{20,12},{24,0},{28,4},{1,25},{... | collective-permute-start | bytes 196616 | tf_op jit(solution)/shard_map/ppermute | solution.py:195
  33.4 6.3 %collective-permute-start.5 = (f32[16,2048]{1,0:T(8,128)S(1)}, f32[16,2048]{1,0:T(8,128)S(1)}, u32[]{:S(2)}, u32[]{:S(2)}) collective-permute-start(f32[16,2048]{1,0:T(8,128)S(1)} %pad_maximum_fusion.2), channel_id=1, source_target_pairs={{0,4},{4,0},{8,12},{12,8},{16,20},{20,16},{24,28},{28,24},{1,5},{5... | collective-permute-start | bytes 393224 | tf_op jit(solution)/shard_map/ppermute | solution.py:195
